TPU v7x, 32 devices: a whole 2x2x4 slice. The times are simulated.
32 devices in a mesh: leaf: 8 (over z, x), rhs: 4 (over y, core).
Axes of the slice: x: 2, y: 2, z: 4, core: 2. Of those that a mesh axis runs over, the one named last changes fastest.
Arguments:
- points: bfloat16 [16384, 784], P('leaf'), may hold values from -8 to 8
- vectors: bfloat16 [16384, 128], P('leaf', 'rhs'), may hold values from -6 to 6
- bases: float32 [64, 256, 64], P('leaf'), may hold values from -0.375 to 0.375
- leaf_coupling: float32 [64, 8, 64, 64], P('leaf'), may hold values from -0.75 to 0.75
- transfer: float32 [64, 64, 64], P('leaf'), may hold values from -0.75 to 0.75
- up_coupling: float32 [32, 8, 64, 64], P('leaf'), may hold values from -0.75 to 0.75
- far_leaf: int32 [64, 8], P('leaf'), may hold values from 0 to 63, as said below
- far_up: int32 [32, 8], P('leaf'), may hold values from 0 to 31, as said below
- near_lists: int32 [64, 8], P('leaf'), may hold values from -1 to 63, as said below
Outputs:
- product: float32 [16384, 128], P('leaf', 'rhs')
Inputs may be any that keep to these rules, and one draw needn't show every extreme that they name: `near_lists`: row i begins with i itself; the other entries are distinct leaves j with 0 < |i - j| <= 8, or -1 for an unused slot. `far_leaf`: each row holds 8 distinct leaves, each more than 8 away from the row's own leaf in index. `far_up`: each row holds 8 distinct parents, each at least 2 away from the row's own parent in index.
All inputs are finite; a program needn't handle non-finite values.
Results may differ from a plain program's by a relative error of at most 0.0025.
Values may be sent and summed in bfloat16 or wider, within the bound.
No kernel may reach another device: no remote copies, remote signals or barrier semaphores. Data moves between devices by JAX's collectives and lax.ppermute only.
A program may use at most 128 MiB of HBM per device.

v0:
```python
from functools import partial

import jax
import jax.numpy as jnp
from jax import lax
from jax.sharding import PartitionSpec as P

HIGHEST = lax.Precision.HIGHEST
RIDGE = 0.5


def with_halo(block, sides, width):
    for axis, dim in sides:
        count = lax.axis_size(axis)
        forward = [(i, i + 1) for i in range(count - 1)]
        backward = [(target, source) for source, target in forward]
        low = lax.ppermute(
            lax.slice_in_dim(block, block.shape[dim] - width, None, axis=dim), axis, forward
        )
        high = lax.ppermute(lax.slice_in_dim(block, 0, width, axis=dim), axis, backward)
        block = jnp.concatenate([low, block, high], axis=dim)
    return block


def fold_rows(targets, piece):
    piece_rows = piece.shape[0]
    global_rows = lax.iota(jnp.int32, piece_rows)
    select = (targets[:, None] == global_rows[None, :]).astype(jnp.float32)
    return jnp.dot(select, piece, precision=HIGHEST, preferred_element_type=jnp.float32)


def local(
    points, vectors, bases, leaf_coupling, transfer, up_coupling, far_leaf, far_up, near_lists
):
    leaf_count = bases.shape[0]
    leaf_pts = bases.shape[1]
    rank_size = bases.shape[2]
    columns = vectors.shape[1]
    shard_rows = points.shape[0]
    features = points.shape[1]
    far_count = far_leaf.shape[1]
    far_upper = far_up.shape[1]
    slot_count = near_lists.shape[1]
    half_count = leaf_count // 2
    device = lax.axis_index("leaf")
    rhs_count = lax.axis_size("rhs")
    vec_float = vectors.astype(jnp.float32).reshape(leaf_count, leaf_pts, columns)
    coeffs = jnp.einsum("lpr,lpc->lrc", bases, vec_float, precision=HIGHEST)
    lifted = jnp.einsum("lba,lbc->lac", transfer, coeffs, precision=HIGHEST)
    parents = lifted.reshape(half_count, 2, rank_size, columns).sum(axis=1)
    leaf_targets = far_leaf.reshape(-1)
    gathered = fold_rows(
        leaf_targets,
        lax.all_gather(coeffs.reshape(leaf_count, rank_size * columns), "leaf", axis=0, tiled=True),
    )
    leaf_field = jnp.einsum(
        "lkab,lkbc->lac",
        leaf_coupling,
        gathered.reshape(leaf_count, far_count, rank_size, columns),
        precision=HIGHEST,
    )
    up_targets = far_up.reshape(-1)
    up_gathered = fold_rows(
        up_targets,
        lax.all_gather(
            parents.reshape(half_count, rank_size * columns), "leaf", axis=0, tiled=True
        ),
    )
    upper_field = jnp.einsum(
        "qkab,qkbc->qac",
        up_coupling,
        up_gathered.reshape(half_count, far_upper, rank_size, columns),
        precision=HIGHEST,
    )
    pushed = jnp.einsum(
        "lab,lbc->lac", transfer, jnp.repeat(upper_field, 2, axis=0), precision=HIGHEST
    )
    far_part = jnp.einsum("lpr,lrc->lpc", bases, leaf_field + pushed, precision=HIGHEST).reshape(
        shard_rows, columns
    )
    window_points = with_halo(points, (("leaf", 0),), shard_rows)
    window_vectors = with_halo(vectors, (("leaf", 0),), shard_rows)
    dims_rowwise = (((1,), (1,)), ((0,), (0,)))
    window_sums = lax.dot_general(
        window_points, window_points, dims_rowwise, preferred_element_type=jnp.float32
    )
    own_sums = lax.dot_general(points, points, dims_rowwise, preferred_element_type=jnp.float32)
    first_leaf = device * leaf_count - leaf_count
    usable = near_lists >= 0
    window_leaf = jnp.where(usable, near_lists - first_leaf, 0)

    def near_tiles(vector_source, operands):
        own_points, own_norms, slot_ids, slot_usable = operands
        running = jnp.zeros((leaf_pts, vector_source.shape[1]), jnp.float32)
        for slot_index in range(slot_ids.shape[0]):
            begin_row = slot_ids[slot_index] * leaf_pts
            near_points = lax.dynamic_slice_in_dim(window_points, begin_row, leaf_pts, 0)
            near_norms = lax.dynamic_slice_in_dim(window_sums, begin_row, leaf_pts, 0)
            cross_terms = lax.dot_general(
                own_points,
                near_points,
                (((1,), (1,)), ((), ())),
                preferred_element_type=jnp.float32,
            )
            distance = own_norms[:, None] + near_norms[None, :] - 2.0 * cross_terms
            weight_mask = slot_usable[slot_index].astype(jnp.float32)
            kernel = (jnp.exp(-distance / features) * weight_mask).astype(jnp.bfloat16)
            near_vectors = lax.dynamic_slice_in_dim(vector_source, begin_row, leaf_pts, 0)
            running = running + jnp.dot(kernel, near_vectors, preferred_element_type=jnp.float32)
        return running

    point_blocks = points.reshape(leaf_count, leaf_pts, features)
    norm_blocks = own_sums.reshape(leaf_count, leaf_pts)
    picked = lax.axis_index("rhs") + rhs_count * lax.iota(jnp.int32, slot_count // rhs_count)
    part_leaf = jnp.take(window_leaf, picked, axis=1)
    part_usable = jnp.take(usable, picked, axis=1)
    all_vectors = lax.all_gather(window_vectors, "rhs", axis=1, tiled=True)
    partial_sums = lax.map(
        partial(near_tiles, all_vectors), (point_blocks, norm_blocks, part_leaf, part_usable)
    )
    near_part = lax.psum_scatter(
        partial_sums.reshape(shard_rows, all_vectors.shape[1]),
        "rhs",
        scatter_dimension=1,
        tiled=True,
    )
    return near_part + far_part + RIDGE * vectors.astype(jnp.float32)


def solution(mesh):
    return jax.shard_map(
        local,
        mesh=mesh,
        in_specs=(
            P("leaf", None),
            P("leaf", "rhs"),
            P("leaf", None, None),
            P("leaf", None, None, None),
            P("leaf", None, None),
            P("leaf", None, None, None),
            P("leaf", None),
            P("leaf", None),
            P("leaf", None),
        ),
        out_specs=P("leaf", "rhs"),
        check_vma=False,
    )
```

profile of v0, /device:TPU:10, one launch (start us, length us, event | category | flops | bytes accessed | tf_op | source)
XLA Modules:
  0.0 356.2 jit_solution(8973744379219532466)
XLA Ops:
  6.5 3.6 %collective-permute-start = (bf16[2048,784]{0,1:T(8,128)(2,1)}, bf16[2048,784]{0,1:T(8,128)(2,1)}, u32[]{:S(2)}, u32[]{:S(2)}) collective-permute-start(bf16[2048,784]{0,1:T(8,128)(2,1)} %param.11), channel_id=1, source_target_pairs={{0,4},{4,8},{8,12},{12,16},{16,20},{20,24},{24,28},{1,5},{5,9},{9,... | collective-permute-start | bytes 9633800 | tf_op jit(solution)/shard_map/ppermute | solution.py:17
  10.1 3.4 collective-permute-start.2
  13.5 2.4 collective-permute-start.3
  16.0 3.3 collective-permute-start.1
  19.3 135.2 %collective-permute-done.2 = bf16[2048,32]{0,1:T(8,128)(2,1)S(1)} collective-permute-done((bf16[2048,32]{0,1:T(8,128)(2,1)}, bf16[2048,32]{0,1:T(8,128)(2,1)S(1)}, u32[]{:S(2)}, u32[]{:S(2)}) %collective-permute-start.2) | collective-permute-done | bytes 131104 | tf_op jit(solution)/shard_map/ppermute | solution.py:17
  156.2 6.0 %copy.40 = bf16[2048,784]{1,0:T(8,128)(2,1)} copy(bf16[2048,784]{0,1:T(8,128)(2,1)} %param.11) | data formatting | bytes 6422528 | tf_op args[0]
  163.4 2.9 fusion.50
  166.4 9.7 %all-gather.3.cloned.1.call-done = bf16[6144,128]{0,1:T(8,128)(2,1)} async-done(((bf16[6144,32]{0,1:T(8,128)(2,1)}), bf16[6144,128]{0,1:T(8,128)(2,1)}) %all-gather.3.cloned.1.call-update) | async-done | bytes 1572880 | tf_op jit(solution)/shard_map/all_gather | solution.py:117
  176.1 2.6 copy.42
  178.7 4.3 %constant_dynamic-update-slice_fusion.2 = bf16[6144,784]{0,1:T(8,128)(2,1)} fusion(bf16[2048,784]{0,1:T(8,128)(2,1)} %collective-permute-done), kind=kLoop, calls=%fused_computation.71 | loop fusion | bytes 6422528
  185.0 4.2 %constant_dynamic-update-slice_fusion = bf16[6144,784]{0,1:T(8,128)(2,1)} fusion(bf16[6144,784]{0,1:T(8,128)(2,1)} %constant_dynamic-update-slice_fusion.1, bf16[2048,784]{0,1:T(8,128)(2,1)} %collective-permute-done.1), kind=kLoop, calls=%fused_computation.69 | loop fusion | bytes 6422528 | tf_op jit(solution)/shard_map/concatenate | solution.py:21
  189.2 13.5 %copy.41 = bf16[6144,784]{1,0:T(8,128)(2,1)} copy(bf16[6144,784]{0,1:T(8,128)(2,1)} %constant_dynamic-update-slice_fusion) | data formatting | bytes 19267584 | tf_op jit(solution)/shard_map/while | solution.py:118
  202.8 5.8 %fusion.49 = f32[6144]{0:T(1024)S(1)} fusion(bf16[6144,784]{0,1:T(8,128)(2,1)} %constant_dynamic-update-slice_fusion), kind=kLoop, calls=%fused_computation.50 | loop fusion | flops 14444544 | bytes 9658368 | tf_op jit(solution)/shard_map/dot_general | solution.py:84
  208.6 62.9 %while.10 = (s32[]{:T(128)}, f32[8,256,128]{2,1,0:T(8,128)}, f32[8,256]{1,0:T(8,128)S(1)}, s32[8,2]{0,1:T(2,128)S(1)}, f32[6144]{0:T(1024)S(1)}, /*index=5*/bf16...) while((s32[]{:T(128)}, f32[8,256,128]{2,1,0:T(8,128)}, ...), condition=%wide.region_1.2_spmd, body=%wide.region_0.0_spmd.sunk | while | flops 240025600 | bytes 2374431 | solution.py:118
  214.2 2.3 fusion.96
  222.1 2.3 fusion.96
  229.9 2.3 fusion.96
  245.6 2.3 fusion.96
  261.4 2.3 fusion.96
  271.6 2.5 copy.62
  274.9 28.7 %all_gather.10 = f32[64,2048]{1,0:T(8,128)S(1)} all-gather(f32[8,2048]{1,0:T(8,128)S(1)} %reshape.83), channel_id=1, replica_groups=mesh['leaf'=8,'rhs'=4] {'leaf'}, dimensions={0}, use_global_device_ids=true | all-gather | bytes 589824 | tf_op jit(solution)/shard_map/all_gather | solution.py:54
  306.6 30.9 %all-gather = f32[8,4,2048]{2,1,0:T(4,128)S(1)} all-gather(f32[1,4,2048]{2,1,0:T(4,128)S(1)} %reshape.108), channel_id=1, replica_groups=mesh['leaf'=8,'rhs'=4] {'leaf'}, dimensions={0}, use_global_device_ids=true | all-gather | bytes 294912 | tf_op jit(solution)/shard_map/all_gather | solution.py:65
  338.5 3.1 convolution_bitcast_fusion.2
  341.6 5.0 %convolution_bitcast_fusion.1 = f32[8,32,64]{2,1,0:T(8,128)S(1)} fusion(f32[8,8,64,32]{3,2,1,0:T(8,128)} %reshape.84, f32[8,8,64,64]{3,2,1,0:T(8,128)S(1)} %copy-done), kind=kOutput, calls=%fused_computation.55 | convolution fusion | flops 100663296 | bytes 1638400 | tf_op jit(solution)/shard_map/lkab,lkbc->lac/dot_general | solution.py:56
  (119 shorter events, 43.4 us)
Async XLA Ops:
  6.5 335.0 %copy-start = (f32[8,8,64,64]{3,2,1,0:T(8,128)S(1)}, f32[8,8,64,64]{3,2,1,0:T(8,128)}, u32[]{:S(2)}) copy-start(f32[8,8,64,64]{3,2,1,0:T(8,128)} %param.14) | copy-start | bytes 3145732
  6.5 169.6 %all-gather.3.cloned.1.call-start = ((), (), s32[]{:S(2)}) async-start(), calls=%async_computation.1 | async-start | bytes 1966080 | tf_op jit(solution)/shard_map/all_gather | solution.py:117
  6.5 172.2 %collective-permute-start = (bf16[2048,784]{0,1:T(8,128)(2,1)}, bf16[2048,784]{0,1:T(8,128)(2,1)}, u32[]{:S(2)}, u32[]{:S(2)}) collective-permute-start(bf16[2048,784]{0,1:T(8,128)(2,1)} %param.11), channel_id=1, source_target_pairs={{0,4},{4,8},{8,12},{12,16},{16,20},{20,24},{24,28},{1,5},{5,9},{9,... | collective-permute-start | bytes 9633800 | tf_op jit(solution)/shard_map/ppermute | solution.py:17
  10.1 144.3 %collective-permute-start.2 = (bf16[2048,32]{0,1:T(8,128)(2,1)}, bf16[2048,32]{0,1:T(8,128)(2,1)S(1)}, u32[]{:S(2)}, u32[]{:S(2)}) collective-permute-start(bf16[2048,32]{0,1:T(8,128)(2,1)} %param.12), channel_id=1, source_target_pairs={{0,4},{4,8},{8,12},{12,16},{16,20},{20,24},{24,28},{1,5},{5,9},{9,... | collective-permute-start | bytes 393224 | tf_op jit(solution)/shard_map/ppermute | solution.py:17
  13.5 140.9 %collective-permute-start.3 = (bf16[2048,32]{0,1:T(8,128)(2,1)}, bf16[2048,32]{0,1:T(8,128)(2,1)S(1)}, u32[]{:S(2)}, u32[]{:S(2)}) collective-permute-start(bf16[2048,32]{0,1:T(8,128)(2,1)} %param.12), channel_id=1, source_target_pairs={{4,0},{8,4},{12,8},{16,12},{20,16},{24,20},{28,24},{5,1},{9,5},{13... | collective-permute-start | bytes 393224 | tf_op jit(solution)/shard_map/ppermute | solution.py:20
  16.0 169.0 %collective-permute-start.1 = (bf16[2048,784]{0,1:T(8,128)(2,1)}, bf16[2048,784]{0,1:T(8,128)(2,1)}, u32[]{:S(2)}, u32[]{:S(2)}) collective-permute-start(bf16[2048,784]{0,1:T(8,128)(2,1)} %param.11), channel_id=1, source_target_pairs={{4,0},{8,4},{12,8},{16,12},{20,16},{24,20},{28,24},{5,1},{9,5},{13... | collective-permute-start | bytes 9633800 | tf_op jit(solution)/shard_map/ppermute | solution.py:20
  156.1 6.0 %copy-start.8 = (s32[8,8]{1,0:T(8,128)S(1)}, s32[8,8]{1,0:T(8,128)}, u32[]{:S(2)}) copy-start(s32[8,8]{1,0:T(8,128)} %param.19) | copy-start | bytes 772
  156.2 191.5 %reduce-scatter.2.cloned.1.call-start = ((), (), s32[]{:S(2)}) async-start(), calls=%async_computation.2 | async-start | bytes 1310720 | tf_op jit(solution)/shard_map/reduce_scatter | solution.py:121
  178.7 4.3 %copy-start.1 = (bf16[2048,784]{0,1:T(8,128)(2,1)S(1)}, bf16[2048,784]{0,1:T(8,128)(2,1)}, u32[]{:S(2)}) copy-start(bf16[2048,784]{0,1:T(8,128)(2,1)} %param.11) | copy-start | bytes 9633796
  208.6 65.5 %copy-start.2 = (f32[8,256,64]{1,2,0:T(8,128)S(1)}, f32[8,256,64]{1,2,0:T(8,128)}, u32[]{:S(2)}) copy-start(f32[8,256,64]{1,2,0:T(8,128)} %param.13) | copy-start | bytes 1572868
  208.6 65.5 %copy-start.4 = (bf16[2048,32]{0,1:T(8,128)(2,1)S(1)}, bf16[2048,32]{0,1:T(8,128)(2,1)}, u32[]{:S(2)}) copy-start(bf16[2048,32]{0,1:T(8,128)(2,1)} %param.12) | copy-start | bytes 393220
  271.6 3.3 copy-start.7
  274.1 32.0 %copy-start.5 = (f32[8,64,64]{2,1,0:T(8,128)S(1)}, f32[8,64,64]{2,1,0:T(8,128)}, u32[]{:S(2)}) copy-start(f32[8,64,64]{2,1,0:T(8,128)} %param.15) | copy-start | bytes 393220
  274.2 63.5 %copy-start.9 = (s32[4,8]{1,0:T(4,128)S(1)}, s32[4,8]{1,0:T(4,128)}, u32[]{:S(2)}) copy-start(s32[4,8]{1,0:T(4,128)} %param.18) | copy-start | bytes 388
  338.4 8.2 %copy-start.6 = (f32[8,64,64]{2,1,0:T(8,128)S(1)}, f32[8,64,64]{2,1,0:T(8,128)}, u32[]{:S(2)}) copy-start(f32[8,64,64]{2,1,0:T(8,128)} %param.15) | copy-start | bytes 393220
  338.5 8.7 %copy-start.3 = (f32[8,256,64]{1,2,0:T(8,128)S(1)}, f32[8,256,64]{1,2,0:T(8,128)}, u32[]{:S(2)}) copy-start(f32[8,256,64]{1,2,0:T(8,128)} %param.13) | copy-start | bytes 1572868
Sparse Core Ops, SparseCore 0:
  156.3 19.7 all-gather.2
  274.3 24.8 reduce-scatter.1
where the time goes:
time: 362 us; the launch traced here: 356 us
  waiting for transfers between devices  145 us (40%)
  blocking collectives  59.7 us (16%)
  local copies, waits for them, and re-layouts  50.3 us (14%)
  matrix products  42.6 us (12%)
  loops' own time  20.1 us (6%)
  between operations  13.7 us (4%)
  starting transfers between devices  12.8 us (4%)
  other arithmetic  12.3 us (3%)
    ppermute x2, waiting for transfers between devices, with_halo(): lax.ppermute(lax.slice_in_dim(block, block.shape[dim] - width, None, axis...  135 us
    dot_general x16, matrix products, near_tiles(): jnp.dot(kernel, near_vectors, preferred_element_type=jnp.float32)  32.1 us
    all_gather x1, blocking collectives, local(): lax.all_gather(parents.reshape(half_count, rank_size * columns), 'leaf',...  30.9 us
    all_gather x1, blocking collectives, local(): lax.all_gather(coeffs.reshape(leaf_count, rank_size * columns), 'leaf', a...  28.7 us
    another operation x1, loops' own time, local(): lax.map(partial(near_tiles, all_vectors), (point_blocks, norm_blocks, par...  20.1 us
    while x2, local copies, waits for them, and re-layouts, local(): lax.map(partial(near_tiles, all_vectors), (point_blocks, norm_blocks, par...  16.2 us
    unnamed x26, local copies, waits for them, and re-layouts  12.6 us
    all_gather x1, waiting for transfers between devices, local(): all_vectors = lax.all_gather(window_vectors, 'rhs', axis=1, tiled=True)  9.66 us
  transfers between devices with their start and end apart: 6, of which 2 were waited for; matrix products, arithmetic and copies ran while one was open for 10% of the time, Pallas kernels for 0%

commit v1 on v0

v1 whole, which is shorter than its diff:
```python
import functools
import math

import jax
import jax.numpy as jnp
from jax import lax
from jax.experimental import pallas as pl
from jax.experimental.pallas import tpu as pltpu
from jax.sharding import PartitionSpec as P

RIDGE = 0.5
LOG2E = math.log2(math.e)
F32 = jnp.float32
BF16 = jnp.bfloat16
NN = (((1,), (0,)), ((), ()))
NT = (((1,), (1,)), ((), ()))
VMEM = pl.BlockSpec(memory_space=pltpu.VMEM)
SMEM = pl.BlockSpec(memory_space=pltpu.SMEM)
MIB = 1 << 20


def dot(a, b, dims):
    return lax.dot_general(a, b, dims, preferred_element_type=F32)


def halves(x):
    high = x.astype(BF16)
    return high, (x - high.astype(F32)).astype(BF16)


def split_dot(a, b, dims):
    a_high, a_low = halves(a)
    b_high, b_low = halves(b)
    return dot(a_high, b_high, dims) + (dot(a_high, b_low, dims) + dot(a_low, b_high, dims))


def half_split_dot(a, b, dims):
    b_high, b_low = halves(b)
    return dot(a, b_high, dims) + dot(a, b_low, dims)


def pack_kernel(vec_ref, bases_ref, transfer_ref, vt_ref, msg_ref):
    leaves, pts, _ = bases_ref.shape
    coeffs = []
    lifted = []
    for leaf in range(leaves):
        vt = vec_ref[leaf * pts : (leaf + 1) * pts, :].astype(F32).T.astype(BF16)
        vt_ref[leaf] = vt
        coeffs.append(half_split_dot(vt, bases_ref[leaf], NN))
        lifted.append(split_dot(coeffs[-1], transfer_ref[leaf], NN))
    parents = [lifted[2 * q] + lifted[2 * q + 1] for q in range(leaves // 2)]
    entries = coeffs + parents
    for e in range(len(entries) // 2):
        msg_ref[e] = jnp.concatenate(entries[2 * e : 2 * e + 2], axis=1).astype(BF16)


def scaled_sums(x, features):
    sums = jnp.sum(jnp.square(x.astype(F32)), axis=1, keepdims=True) * (LOG2E / features)
    return jnp.broadcast_to(sums, (x.shape[0], 128))


def row_of(sums):
    return sums.T[0:1, :]


def near_tile(x_a, x_b, sums_a, row_b):
    pts, features = x_a.shape
    cross = dot(x_a, x_b, NT) * (2.0 * LOG2E / features)
    wide = jnp.concatenate([sums_a] * (pts // 128), axis=1)
    return jnp.exp2(cross - (wide + row_b)).astype(BF16)


def listed(lists_ref, row, leaf):
    found = lists_ref[row, 0] == leaf
    for k in range(1, lists_ref.shape[1]):
        found = found | (lists_ref[row, k] == leaf)
    return found


def block_order(count):
    bits = count.bit_length() - 1
    return [int(format(m, "b").zfill(bits)[::-1], 2) if bits else 0 for m in range(count)]


def fill_vectors(piece_refs, v_ref):
    cols = piece_refs[0].shape[1]
    count = v_ref.shape[1] // cols
    where = {}
    for piece in piece_refs:
        for part in range(piece.shape[1] // cols):
            where[len(where)] = (piece, part)
    for spot, m in enumerate(block_order(count)):
        piece, part = where[m]
        v_ref[:, spot * cols : (spot + 1) * cols, :] = piece[:, part * cols : (part + 1) * cols, :]


def own_kernel(pieces, sc_ref, lists_ref, x_ref, *refs):
    piece_refs, (acc_ref, sums_ref, v_ref) = refs[:pieces], refs[pieces:]
    leaves = acc_ref.shape[0]
    pts = x_ref.shape[0] // leaves
    features = x_ref.shape[1]
    base = sc_ref[2]
    fill_vectors(piece_refs, v_ref)
    for leaf in range(leaves):
        sums_ref[leaf] = scaled_sums(x_ref[leaf * pts : (leaf + 1) * pts, :], features)
    acc_ref[...] = jnp.zeros_like(acc_ref)
    low, high = sc_ref[0], sc_ref[1]
    for step in range(leaves + 1):
        first = step <= low
        b = jnp.where(first, low, high)
        a = jnp.where(first, step, step - low - 1)
        x_a = x_ref[pl.ds(pl.multiple_of(a * pts, pts), pts), :]
        x_b = x_ref[pl.ds(pl.multiple_of(b * pts, pts), pts), :]
        tile = near_tile(x_a, x_b, sums_ref[a], row_of(sums_ref[b]))
        from_b = listed(lists_ref, a, base + b).astype(F32)
        from_a = (listed(lists_ref, b, base + a) & (a != b)).astype(F32)
        acc_ref[a] += from_b * dot(v_ref[b], tile, NT)
        acc_ref[b] += from_a * dot(v_ref[a], tile, NN)


def cross_kernel(
    pieces, start, sc_ref, lists_ref, next_lists_ref, x_ref, halo_ref, sums_ref, halo_v_ref, *refs
):
    part = 0 if start == 0 else 1
    piece_refs, refs = refs[:pieces], refs[pieces:]
    leaves = sums_ref.shape[0]
    half = leaves // 2
    groups = [g for g in (0, 1) if g * half >= start]
    ins, outs = refs[: 2 * len(groups)], refs[2 * len(groups) : 4 * len(groups)]
    ret_ref, v_ref = refs[-2:]
    pts = x_ref.shape[0] // leaves
    features = x_ref.shape[1]
    rows = v_ref.shape[1]
    base = sc_ref[2]
    b = sc_ref[part]
    fill_vectors(piece_refs, v_ref)
    for source, target in zip(ins, outs):
        target[...] = source[...]
    ret_ref[...] = jnp.zeros_like(ret_ref)
    row_b = row_of(scaled_sums(halo_ref[...], features))
    for a in range(start, leaves):
        to_a = listed(lists_ref, a, base + leaves + b)
        to_b = listed(next_lists_ref, b, base + a)

        @pl.when((a >= b) & (to_a | to_b))
        def _():
            x_a = x_ref[a * pts : (a + 1) * pts, :]
            tile = near_tile(x_a, halo_ref[...], sums_ref[a], row_b)
            update = to_a.astype(F32) * dot(halo_v_ref[...], tile, NT)
            group = groups.index(a // half)
            outs[2 * group][a % half] += update[: rows // 2]
            outs[2 * group + 1][a % half] += update[rows // 2 :]
            ret_ref[...] += to_b.astype(F32) * dot(v_ref[a], tile, NN)


def far_kernel(
    sc_ref, far_leaf_ref, far_up_ref, all_ref, coupling_ref, up_ref, transfer_ref, bases_ref,
    vt_ref, out_ref
):
    leaves, _, rank = bases_ref.shape
    device = sc_ref[3]

    def entry(index, per_device, first):
        owner = lax.div(index, per_device)
        local = lax.rem(index, per_device)
        pair = all_ref[owner ^ device, first + lax.div(local, 2)].astype(F32)
        swapped = pltpu.roll(pair, rank, 1)
        return jnp.where(lax.rem(local, 2) == 1, swapped, pair)[:, :rank].astype(BF16)

    def field(list_ref, row, matrix_ref, per_device, first):
        total = None
        for k in range(list_ref.shape[1]):
            c = entry(list_ref[row, k], per_device, first)
            both = jnp.concatenate(halves(matrix_ref[row, k]), axis=0)
            term = dot(c, both, NT)
            total = term if total is None else total + term
        return total[:, :rank] + total[:, rank:]

    for parent in range(leaves // 2):
        upper = field(far_up_ref, parent, up_ref, leaves // 2, leaves // 2)
        for leaf in (2 * parent, 2 * parent + 1):
            total = field(far_leaf_ref, leaf, coupling_ref, leaves, 0)
            total = total + split_dot(upper, transfer_ref[leaf], NT)
            far = split_dot(total, bases_ref[leaf], NT)
            out_ref[leaf] = far + RIDGE * vt_ref[leaf].astype(F32)


def finish_kernel(low_ref, low_in_ref, high_ref, high_in_ref, far_ref, out_ref):
    half = low_ref.shape[0]
    pts = far_ref.shape[2]
    for leaf in range(2 * half):
        kept, came = (low_ref, low_in_ref) if leaf < half else (high_ref, high_in_ref)
        total = far_ref[leaf] + (kept[leaf % half] + came[leaf % half].astype(F32))
        out_ref[leaf * pts : (leaf + 1) * pts, :] = total.T


def call(body, out_shape, in_specs, args, flops=0, bytes_accessed=0, scratch=(), name=None):
    return pl.pallas_call(
        body,
        out_shape=out_shape,
        in_specs=in_specs,
        out_specs=jax.tree.map(lambda _: VMEM, out_shape),
        scratch_shapes=list(scratch),
        compiler_params=pltpu.CompilerParams(vmem_limit_bytes=40 * MIB),
        cost_estimate=pl.CostEstimate(
            flops=flops, bytes_accessed=bytes_accessed, transcendentals=0
        ),
        name=name,
    )(*args)


def xor_pairs(count, bit):
    return [(i, i ^ bit) for i in range(count)]


def local(
    points, vectors, bases, leaf_coupling, transfer, up_coupling, far_leaf, far_up, near_lists
):
    leaves, pts, rank = bases.shape
    cols = vectors.shape[1]
    half = leaves // 2
    shape = jax.ShapeDtypeStruct
    leaf_devices = lax.axis_size("leaf")
    rhs_devices = lax.axis_size("rhs")
    assert leaves == 2 * rhs_devices
    rows = cols * rhs_devices
    device = lax.axis_index("leaf")
    column = lax.axis_index("rhs")
    low, high = column, leaves - 1 - column
    down = [(i + 1, i) for i in range(leaf_devices - 1)]
    up = [(i, i + 1) for i in range(leaf_devices - 1)]
    scalars = jnp.stack([low, high, device * leaves, device]).astype(jnp.int32)

    def picked(array, leaf):
        return lax.dynamic_slice_in_dim(array, leaf * pts, pts, 0)

    halo_low = lax.ppermute(picked(points, low), "leaf", down)
    halo_high = lax.ppermute(picked(points, high), "leaf", down)
    next_lists = lax.ppermute(near_lists, "leaf", down)

    vt, message = call(
        pack_kernel,
        (
            shape((leaves, cols, pts), BF16),
            shape((half + half // 2, cols, 2 * rank), BF16),
        ),
        [VMEM] * 3,
        (vectors, bases, transfer),
        flops=10**8,
        bytes_accessed=3 * MIB,
        name="pack",
    )

    pieces = [vt]
    bit = 1
    while bit < rhs_devices:
        mine = pieces[0] if bit == 1 else jnp.concatenate(pieces, axis=1)
        pieces.append(lax.ppermute(mine, "rhs", xor_pairs(rhs_devices, bit)))
        bit *= 2

    everything = message[None]
    bit = 1
    while bit < leaf_devices:
        arrived = lax.ppermute(everything, "leaf", xor_pairs(leaf_devices, bit))
        everything = jnp.concatenate([everything, arrived], axis=0)
        bit *= 2

    def stacked(leaf):
        blocks = []
        for piece in pieces:
            chosen = lax.dynamic_index_in_dim(piece, leaf, 0, keepdims=False)
            blocks += [chosen[i : i + cols] for i in range(0, chosen.shape[0], cols)]
        return jnp.concatenate([blocks[m] for m in block_order(rhs_devices)], axis=0)

    halo_vectors = lax.ppermute(jnp.stack([stacked(low), stacked(high)]), "leaf", down)

    v_scratch = pltpu.VMEM((leaves, rows, pts), BF16)
    acc, sums = call(
        functools.partial(own_kernel, len(pieces)),
        (shape((leaves, rows, pts), F32), shape((leaves, pts, 128), F32)),
        [SMEM, SMEM] + [VMEM] * (1 + len(pieces)),
        (scalars, near_lists, points, *pieces),
        flops=3 * 10**9,
        bytes_accessed=6 * MIB,
        scratch=[v_scratch],
        name="own_tiles",
    )

    part = shape((half, rows // 2, pts), F32)
    back = shape((rows, pts), F32)

    def cross(start, halo, halo_v, totals):
        return call(
            functools.partial(cross_kernel, len(pieces), start),
            (part,) * len(totals) + (back,),
            [SMEM] * 3 + [VMEM] * (4 + len(pieces) + len(totals)),
            (scalars, near_lists, next_lists, points, halo, sums, halo_v, *pieces, *totals),
            flops=2 * 10**9,
            bytes_accessed=8 * MIB,
            scratch=[v_scratch],
            name="cross_tiles",
        )

    def reduced(keep, send, came, leaf):
        here = lax.iota(jnp.int32, half)[:, None, None] == leaf
        send = send + jnp.where(here, came[None, rows // 2 :], 0.0)
        keep = keep + jnp.where(here, came[None, : rows // 2], 0.0)
        bit = 1
        while True:
            arrived = lax.ppermute(send, "rhs", xor_pairs(rhs_devices, bit))
            bit *= 2
            if bit == rhs_devices:
                return keep, arrived
            total = keep + arrived.astype(F32)
            middle = total.shape[1] // 2
            keep, send = total[:, :middle], total[:, middle:].astype(BF16)

    totals = [
        acc[:half, : rows // 2], acc[:half, rows // 2 :],
        acc[half:, : rows // 2], acc[half:, rows // 2 :],
    ]
    keep_low, send_low, keep_high, send_high, back_low = cross(
        0, halo_low, halo_vectors[0], totals
    )
    came_low = lax.ppermute(back_low.astype(BF16), "leaf", up).astype(F32)
    low_parts = reduced(keep_low, send_low, came_low, low)
    keep_high, send_high, back_high = cross(
        half, halo_high, halo_vectors[1], [keep_high, send_high]
    )
    came_high = lax.ppermute(back_high.astype(BF16), "leaf", up).astype(F32)
    high_parts = reduced(keep_high, send_high, came_high, high - half)

    far = call(
        far_kernel,
        shape((leaves, cols, pts), F32),
        [SMEM] * 3 + [VMEM] * 6,
        (
            scalars, far_leaf, far_up, everything, leaf_coupling, up_coupling, transfer, bases,
            vt,
        ),
        flops=10**9,
        bytes_accessed=6 * MIB,
        name="far_field",
    )
    return call(
        finish_kernel,
        shape((leaves * pts, cols), F32),
        [VMEM] * 5,
        (*low_parts, *high_parts, far),
        bytes_accessed=2 * MIB,
        name="finish",
    )


def solution(mesh):
    return jax.shard_map(
        local,
        mesh=mesh,
        in_specs=(
            P("leaf", None),
            P("leaf", "rhs"),
            P("leaf", None, None),
            P("leaf", None, None, None),
            P("leaf", None, None),
            P("leaf", None, None, None),
            P("leaf", None),
            P("leaf", None),
            P("leaf", None),
        ),
        out_specs=P("leaf", "rhs"),
        check_vma=False,
    )
```

time: 362 us -> 83.5 us (0.23)
  the two profiles are of different devices: /device:TPU:10 before, /device:TPU:9 now
where the time goes in v1:
time: 83.5 us; the launch traced here: 83.3 us
  starting transfers between devices  29.5 us (35%)
  waiting for transfers between devices  21 us (25%)
  Pallas kernels  17.8 us (21%)
  local copies, waits for them, and re-layouts  14 us (17%)
    pallas_call x6, Pallas kernels, call(): pl.pallas_call(body, out_shape=out_shape, in_specs=in_specs, out_specs=ja...  17.8 us
    ppermute x3, waiting for transfers between devices, local(): arrived = lax.ppermute(everything, 'leaf', xor_pairs(leaf_devices, bit))  17.2 us
    unnamed x19, local copies, waits for them, and re-layouts  11.5 us
    ppermute x1, starting transfers between devices, local(): came_low = lax.ppermute(back_low.astype(BF16), 'leaf', up).astype(F32)  7.24 us
    ppermute x1, waiting for transfers between devices, local(): came_high = lax.ppermute(back_high.astype(BF16), 'leaf', up).astype(F32)  3.75 us
    ppermute x4, starting transfers between devices, reduced(): arrived = lax.ppermute(send, 'rhs', xor_pairs(rhs_devices, bit))  3.66 us
    ppermute x3, starting transfers between devices, local(): arrived = lax.ppermute(everything, 'leaf', xor_pairs(leaf_devices, bit))  3.6 us
    ppermute x2, starting transfers between devices, local(): pieces.append(lax.ppermute(mine, 'rhs', xor_pairs(rhs_devices, bit)))  3.06 us
  transfers between devices with their start and end apart: 15, of which 2 were waited for; matrix products, arithmetic and copies ran while one was open for 13% of the time, Pallas kernels for 21%

profile of v1, /device:TPU:9, one launch (start us, length us, event | category | flops | bytes accessed | tf_op | source)
XLA Modules:
  0.0 83.3 jit_solution(2301610874368406815)
XLA Ops:
  0.0 3.0 %collective-permute-start = (s32[8,8]{1,0:T(8,128)}, s32[8,8]{1,0:T(8,128)S(1)}, u32[]{:S(2)}, u32[]{:S(2)}) collective-permute-start(s32[8,8]{1,0:T(8,128)} %lists_ref.5), channel_id=1, source_target_pairs={{4,0},{8,4},{12,8},{16,12},{20,16},{24,20},{28,24},{5,1},{9,5},{13... | collective-permute-start | bytes 776 | tf_op jit(solution)/shard_map/ppermute | solution.py:239
  3.0 1.2 %copy.11.vec_ref = bf16[2048,32]{1,0:T(8,128)(2,1)S(1)} copy(bf16[2048,32]{0,1:T(8,128)(2,1)} %param.10) | data formatting | bytes 262144 | tf_op args[1]
  4.2 1.4 %copy.12.bases_ref = f32[8,256,64]{2,1,0:T(8,128)S(1)} copy(f32[8,256,64]{1,2,0:T(8,128)} %param.11) | data formatting | bytes 1048576 | tf_op args[2]
  6.5 1.3 %pack.1 = (bf16[8,32,256]{2,1,0:T(8,128)(2,1)S(1)}, bf16[6,32,128]{2,1,0:T(8,128)(2,1)S(1)}) custom-call(bf16[2048,32]{1,0:T(8,128)(2,1)S(1)} %copy.11.vec_ref, f32[8,256,64]{2,1,0:T(8,128)S(1)} %copy.12.bases_ref, f32[8,64,64]{2,1,0:T(8,128)S(1)} %copy-done.2), custom_call_target="tpu_custom_call" | custom-call | flops 100000000 | bytes 3145728 | tf_op jit(solution)/shard_map/pack/pallas_call | solution.py:198
  8.2 1.2 %collective-permute-start.2 = (bf16[8,32,256]{2,1,0:T(8,128)(2,1)S(1)}, bf16[8,32,256]{2,1,0:T(8,128)(2,1)S(1)}, u32[]{:S(2)}, u32[]{:S(2)}) collective-permute-start(bf16[8,32,256]{2,1,0:T(8,128)(2,1)S(1)} %get-tuple-element.17.refs_0_.vt_ref), channel_id=1, source_target_pairs={{0,1},{1,0},{2,3},{3,2},{4,5},{5,4},{6,7},{7,6},{8,9},{9,8},{10,11... | collective-permute-start | bytes 393224 | tf_op jit(solution)/shard_map/ppermute | solution.py:258
  9.4 5.9 %copy.14.x_ref = bf16[2048,784]{1,0:T(8,128)(2,1)} copy(bf16[2048,784]{0,1:T(8,128)(2,1)} %param.9) | data formatting | bytes 6422528 | tf_op args[0]
  15.3 1.2 %constant_dynamic-slice_fusion = (bf16[256,784]{1,0:T(8,128)(2,1)S(1)}, bf16[256,784]{1,0:T(8,128)(2,1)S(1)}) fusion(bf16[2048,784]{1,0:T(8,128)(2,1)} %copy.14.x_ref, s32[]{:T(128)S(6)} %select_n.36, s32[]{:T(128)S(6)} %select_n.31), kind=kLoop, calls=%fused_computation.23 | loop fusion | bytes 1605640 | tf_op jit(solution)/shard_map/dynamic_slice | solution.py:235
  16.6 1.9 %collective-permute-start.8 = (bf16[256,784]{1,0:T(8,128)(2,1)S(1)}, bf16[256,784]{1,0:T(8,128)(2,1)S(1)}, u32[]{:S(2)}, u32[]{:S(2)}) collective-permute-start(bf16[256,784]{1,0:T(8,128)(2,1)S(1)} %get-tuple-element.29), channel_id=1, source_target_pairs={{4,0},{8,4},{12,8},{16,12},{20,16},{24,20},{28,24},{5,1},{9,5},{13... | collective-permute-start | bytes 1204232 | tf_op jit(solution)/shard_map/ppermute | solution.py:238
  18.5 2.7 %collective-permute-start.1 = (bf16[256,784]{1,0:T(8,128)(2,1)S(1)}, bf16[256,784]{1,0:T(8,128)(2,1)S(1)}, u32[]{:S(2)}, u32[]{:S(2)}) collective-permute-start(bf16[256,784]{1,0:T(8,128)(2,1)S(1)} %get-tuple-element.30), channel_id=1, source_target_pairs={{4,0},{8,4},{12,8},{16,12},{20,16},{24,20},{28,24},{5,1},{9,5},{13... | collective-permute-start | bytes 1204232 | tf_op jit(solution)/shard_map/ppermute | solution.py:237
  21.4 1.8 %collective-permute-start.3 = (bf16[8,64,256]{2,1,0:T(8,128)(2,1)S(1)}, bf16[8,64,256]{2,1,0:T(8,128)(2,1)S(1)}, u32[]{:S(2)}, u32[]{:S(2)}) collective-permute-start(bf16[8,64,256]{2,1,0:T(8,128)(2,1)S(1)} %pad_maximum_fusion.1), channel_id=1, source_target_pairs={{0,2},{1,3},{2,0},{3,1},{4,6},{5,7},{6,4},{7,5},{8,10},{9,11},{10,... | collective-permute-start | bytes 786440 | tf_op jit(solution)/shard_map/ppermute | solution.py:258
  23.3 17.2 %collective-permute-done.13 = bf16[2,6,32,128]{3,2,1,0:T(8,128)(2,1)S(1)} collective-permute-done((bf16[2,6,32,128]{3,2,1,0:T(8,128)(2,1)S(1)}, bf16[2,6,32,128]{3,2,1,0:T(8,128)(2,1)S(1)}, u32[]{:S(2)}, u32[]{:S(2)}) %collective-permute-start.13) | collective-permute-done | bytes 98336 | tf_op jit(solution)/shard_map/ppermute | solution.py:264
  40.6 3.1 %collective-permute-start.14 = (bf16[4,6,32,128]{3,2,1,0:T(8,128)(2,1)S(1)}, bf16[4,6,32,128]{3,2,1,0:T(8,128)(2,1)S(1)}, u32[]{:S(2)}, u32[]{:S(2)}) collective-permute-start(bf16[4,6,32,128]{3,2,1,0:T(8,128)(2,1)S(1)} %pad_maximum_fusion.2), channel_id=1, source_target_pairs={{0,16},{4,20},{8,24},{12,28},{16,0},{20,4},{24,8},{28,12},{1,17},{... | collective-permute-start | bytes 589832 | tf_op jit(solution)/shard_map/ppermute | solution.py:264
  43.8 1.9 %collective-permute-start.4 = (bf16[2,128,256]{2,1,0:T(8,128)(2,1)S(1)}, bf16[2,128,256]{2,1,0:T(8,128)(2,1)S(1)}, u32[]{:S(2)}, u32[]{:S(2)}) collective-permute-start(bf16[2,128,256]{2,1,0:T(8,128)(2,1)S(1)} %pad_maximum_fusion.3), channel_id=1, source_target_pairs={{4,0},{8,4},{12,8},{16,12},{20,16},{24,20},{28,24},{5,1},{9,5},{13... | collective-permute-start | bytes 393224 | tf_op jit(solution)/shard_map/ppermute | solution.py:275
  45.7 2.0 %copy-done = bf16[2048,784]{1,0:T(8,128)(2,1)S(1)} copy-done((bf16[2048,784]{1,0:T(8,128)(2,1)S(1)}, bf16[2048,784]{1,0:T(8,128)(2,1)}, u32[]{:S(2)}) %copy-start) | copy-done | bytes 3211288
  47.8 5.9 %own_tiles.1 = (f32[8,128,256]{2,1,0:T(8,128)S(1)}, f32[8,256,128]{2,1,0:T(8,128)S(1)}) custom-call(s32[4]{0:T(128)S(1)} %pad_add_fusion.sc_ref, s32[8,8]{1,0:T(8,128)S(1)} %copy-done.7, bf16[2048,784]{1,0:T(8,128)(2,1)S(1)} %copy-done, bf16[8,32,256]{2,1,0:T(8,128)(2,1)S(1)} %get-tuple-element.17.refs_0_.vt_ref, ...), custom_call_target="tpu_custom_call" | custom-call | flops 3000000000 | bytes 6291456 | tf_op jit(solution)/shard_map/own_tiles/pallas_call | solution.py:198
  53.8 3.4 %cross_tiles.2 = (f32[4,64,256]{2,1,0:T(8,128)S(1)}, f32[4,64,256]{2,1,0:T(8,128)S(1)}, f32[4,64,256]{2,1,0:T(8,128)S(1)}, f32[4,64,256]{2,1,0:T(8,128)S(1)}, f32[128,256]{1,0:T(8,128)S(1)}) custom-call(s32[4]{0:T(128)S(1)} %pad_add_fusion.sc_ref, s32[8,8]{1,0:T(8,128)S(1)} %copy-done.7, s32[8,8]{1,0:T(8,128)S(1)} %collective-permute-done.next_lists_ref, ...), custom_call_target="tpu_custom_call" | custom-call | flops 2000000000 | bytes 8388608 | tf_op jit(solution)/shard_map/cross_tiles/pallas_call | solution.py:198
  57.3 7.2 %collective-permute-start.5 = (bf16[128,256]{1,0:T(8,128)(2,1)S(1)}, bf16[128,256]{1,0:T(8,128)(2,1)S(1)}, u32[]{:S(2)}, u32[]{:S(2)}) collective-permute-start(bf16[128,256]{1,0:T(8,128)(2,1)S(1)} %convert_element_type.14), channel_id=1, source_target_pairs={{0,4},{4,8},{8,12},{12,16},{16,20},{20,24},{24,28},{1,5},{5,9},{9,... | collective-permute-start | bytes 196616 | tf_op jit(solution)/shard_map/ppermute | solution.py:325
  64.5 2.1 %cross_tiles.3 = (f32[4,64,256]{2,1,0:T(8,128)S(1)}, f32[4,64,256]{2,1,0:T(8,128)S(1)}, f32[128,256]{1,0:T(8,128)S(1)}) custom-call(s32[4]{0:T(128)S(1)} %pad_add_fusion.sc_ref, s32[8,8]{1,0:T(8,128)S(1)} %copy-done.7, s32[8,8]{1,0:T(8,128)S(1)} %collective-permute-done.next_lists_ref, bf16[2048,784]{1,0:T(8,128)(2,1)S(1)} %copy-done, ...), custom_call_target="tpu_custom_call" | custom-call | flops 2000000000 | bytes 8388608 | tf_op jit(solution)/shard_map/cross_tiles/pallas_call | solution.py:198
  66.7 2.4 %collective-permute-start.9 = (bf16[128,256]{1,0:T(8,128)(2,1)S(1)}, bf16[128,256]{1,0:T(8,128)(2,1)S(1)}, u32[]{:S(2)}, u32[]{:S(2)}) collective-permute-start(bf16[128,256]{1,0:T(8,128)(2,1)S(1)} %convert_element_type.16), channel_id=1, source_target_pairs={{0,4},{4,8},{8,12},{12,16},{16,20},{20,24},{24,28},{1,5},{5,9},{9,... | collective-permute-start | bytes 196616 | tf_op jit(solution)/shard_map/ppermute | solution.py:330
  69.3 3.7 %collective-permute-done.9 = bf16[128,256]{1,0:T(8,128)(2,1)S(1)} collective-permute-done((bf16[128,256]{1,0:T(8,128)(2,1)S(1)}, bf16[128,256]{1,0:T(8,128)(2,1)S(1)}, u32[]{:S(2)}, u32[]{:S(2)}) %collective-permute-start.9) | collective-permute-done | bytes 65568 | tf_op jit(solution)/shard_map/ppermute | solution.py:330
  73.6 2.3 %collective-permute-start.7 = (bf16[4,32,256]{2,1,0:T(8,128)(2,1)S(1)}, bf16[4,32,256]{2,1,0:T(8,128)(2,1)S(1)}, u32[]{:S(2)}, u32[]{:S(2)}) collective-permute-start(bf16[4,32,256]{2,1,0:T(8,128)(2,1)S(1)} %slice.105), channel_id=1, source_target_pairs={{0,2},{1,3},{2,0},{3,1},{4,6},{5,7},{6,4},{7,5},{8,10},{9,11},{10,... | collective-permute-start | bytes 196616 | tf_op jit(solution)/shard_map/ppermute | solution.py:310
  76.1 1.0 %collective-permute-start.11 = (bf16[4,32,256]{2,1,0:T(8,128)(2,1)S(1)}, bf16[4,32,256]{2,1,0:T(8,128)(2,1)S(1)}, u32[]{:S(2)}, u32[]{:S(2)}) collective-permute-start(bf16[4,32,256]{2,1,0:T(8,128)(2,1)S(1)} %slice.104), channel_id=1, source_target_pairs={{0,2},{1,3},{2,0},{3,1},{4,6},{5,7},{6,4},{7,5},{8,10},{9,11},{10,... | collective-permute-start | bytes 196616 | tf_op jit(solution)/shard_map/ppermute | solution.py:310
  77.1 4.8 %far_field.1.far_ref = f32[8,32,256]{2,1,0:T(8,128)S(1)} custom-call(s32[4]{0:T(128)S(1)} %pad_add_fusion.sc_ref, s32[8,8]{1,0:T(8,128)S(1)} %copy-done.5, s32[4,8]{1,0:T(4,128)S(1)} %copy-done.6, bf16[8,6,32,128]{3,2,1,0:T(8,128)(2,1)S(1)} %pad_maximum_fusion.all_ref, f32[8,8,64,64]{3,2,1,0:T(8,128)S(1)} %copy-done.1, f32[4,8,64,64]{3,2,1,0:T(8,128)S(1)} %copy-done.4, ...), custom_call_target="tpu_custom_call" | custom-call | flops 1000000000 | bytes 6291456 | tf_op jit(solution)/shard_map/far_field/pallas_call | solution.py:198
  82.3 1.0 %copy.18 = f32[2048,32]{0,1:T(8,128)} copy(f32[2048,32]{1,0:T(8,128)S(1)} %finish.1) | data formatting | bytes 524288 | tf_op jit(solution)/shard_map/finish/pallas_call | solution.py:198
  (59 shorter events, 3.0 us)
Async XLA Ops:
  0.0 53.8 %collective-permute-start = (s32[8,8]{1,0:T(8,128)}, s32[8,8]{1,0:T(8,128)S(1)}, u32[]{:S(2)}, u32[]{:S(2)}) collective-permute-start(s32[8,8]{1,0:T(8,128)} %lists_ref.5), channel_id=1, source_target_pairs={{4,0},{8,4},{12,8},{16,12},{20,16},{24,20},{28,24},{5,1},{9,5},{13... | collective-permute-start | bytes 776 | tf_op jit(solution)/shard_map/ppermute | solution.py:239
  5.6 1.0 %copy-start.2 = (f32[8,64,64]{2,1,0:T(8,128)S(1)}, f32[8,64,64]{2,1,0:T(8,128)}, u32[]{:S(2)}) copy-start(f32[8,64,64]{2,1,0:T(8,128)} %transfer_ref.3) | copy-start | bytes 393220
  7.8 15.4 %collective-permute-start.12 = (bf16[1,6,32,128]{3,2,1,0:T(8,128)(2,1)S(1)}, bf16[1,6,32,128]{3,2,1,0:T(8,128)(2,1)S(1)}, u32[]{:S(2)}, u32[]{:S(2)}) collective-permute-start(bf16[1,6,32,128]{3,2,1,0:T(8,128)(2,1)S(1)} %bitcast.29), channel_id=1, source_target_pairs={{0,4},{4,0},{8,12},{12,8},{16,20},{20,16},{24,28},{28,24},{1,5},{5... | collective-permute-start | bytes 147464 | tf_op jit(solution)/shard_map/ppermute | solution.py:264
  8.2 13.2 %collective-permute-start.2 = (bf16[8,32,256]{2,1,0:T(8,128)(2,1)S(1)}, bf16[8,32,256]{2,1,0:T(8,128)(2,1)S(1)}, u32[]{:S(2)}, u32[]{:S(2)}) collective-permute-start(bf16[8,32,256]{2,1,0:T(8,128)(2,1)S(1)} %get-tuple-element.17.refs_0_.vt_ref), channel_id=1, source_target_pairs={{0,1},{1,0},{2,3},{3,2},{4,5},{5,4},{6,7},{7,6},{8,9},{9,8},{10,11... | collective-permute-start | bytes 393224 | tf_op jit(solution)/shard_map/ppermute | solution.py:258
  9.4 36.3 %copy-start.7 = (s32[8,8]{1,0:T(8,128)S(1)}, s32[8,8]{1,0:T(8,128)}, u32[]{:S(2)}) copy-start(s32[8,8]{1,0:T(8,128)} %lists_ref.5) | copy-start | bytes 772
  16.6 47.9 %collective-permute-start.8 = (bf16[256,784]{1,0:T(8,128)(2,1)S(1)}, bf16[256,784]{1,0:T(8,128)(2,1)S(1)}, u32[]{:S(2)}, u32[]{:S(2)}) collective-permute-start(bf16[256,784]{1,0:T(8,128)(2,1)S(1)} %get-tuple-element.29), channel_id=1, source_target_pairs={{4,0},{8,4},{12,8},{16,12},{20,16},{24,20},{28,24},{5,1},{9,5},{13... | collective-permute-start | bytes 1204232 | tf_op jit(solution)/shard_map/ppermute | solution.py:238
  18.5 35.3 %collective-permute-start.1 = (bf16[256,784]{1,0:T(8,128)(2,1)S(1)}, bf16[256,784]{1,0:T(8,128)(2,1)S(1)}, u32[]{:S(2)}, u32[]{:S(2)}) collective-permute-start(bf16[256,784]{1,0:T(8,128)(2,1)S(1)} %get-tuple-element.30), channel_id=1, source_target_pairs={{4,0},{8,4},{12,8},{16,12},{20,16},{24,20},{28,24},{5,1},{9,5},{13... | collective-permute-start | bytes 1204232 | tf_op jit(solution)/shard_map/ppermute | solution.py:237
  21.4 22.4 %collective-permute-start.3 = (bf16[8,64,256]{2,1,0:T(8,128)(2,1)S(1)}, bf16[8,64,256]{2,1,0:T(8,128)(2,1)S(1)}, u32[]{:S(2)}, u32[]{:S(2)}) collective-permute-start(bf16[8,64,256]{2,1,0:T(8,128)(2,1)S(1)} %pad_maximum_fusion.1), channel_id=1, source_target_pairs={{0,2},{1,3},{2,0},{3,1},{4,6},{5,7},{6,4},{7,5},{8,10},{9,11},{10,... | collective-permute-start | bytes 786440 | tf_op jit(solution)/shard_map/ppermute | solution.py:258
  23.2 17.3 %collective-permute-start.13 = (bf16[2,6,32,128]{3,2,1,0:T(8,128)(2,1)S(1)}, bf16[2,6,32,128]{3,2,1,0:T(8,128)(2,1)S(1)}, u32[]{:S(2)}, u32[]{:S(2)}) collective-permute-start(bf16[2,6,32,128]{3,2,1,0:T(8,128)(2,1)S(1)} %pad_maximum_fusion.4), channel_id=1, source_target_pairs={{0,8},{4,12},{8,0},{12,4},{16,24},{20,28},{24,16},{28,20},{1,9},{5... | collective-permute-start | bytes 294920 | tf_op jit(solution)/shard_map/ppermute | solution.py:264
  40.6 32.8 %collective-permute-start.14 = (bf16[4,6,32,128]{3,2,1,0:T(8,128)(2,1)S(1)}, bf16[4,6,32,128]{3,2,1,0:T(8,128)(2,1)S(1)}, u32[]{:S(2)}, u32[]{:S(2)}) collective-permute-start(bf16[4,6,32,128]{3,2,1,0:T(8,128)(2,1)S(1)} %pad_maximum_fusion.2), channel_id=1, source_target_pairs={{0,16},{4,20},{8,24},{12,28},{16,0},{20,4},{24,8},{28,12},{1,17},{... | collective-permute-start | bytes 589832 | tf_op jit(solution)/shard_map/ppermute | solution.py:264
  43.8 10.0 %collective-permute-start.4 = (bf16[2,128,256]{2,1,0:T(8,128)(2,1)S(1)}, bf16[2,128,256]{2,1,0:T(8,128)(2,1)S(1)}, u32[]{:S(2)}, u32[]{:S(2)}) collective-permute-start(bf16[2,128,256]{2,1,0:T(8,128)(2,1)S(1)} %pad_maximum_fusion.3), channel_id=1, source_target_pairs={{4,0},{8,4},{12,8},{16,12},{20,16},{24,20},{28,24},{5,1},{9,5},{13... | collective-permute-start | bytes 393224 | tf_op jit(solution)/shard_map/ppermute | solution.py:275
  45.7 2.0 %copy-start = (bf16[2048,784]{1,0:T(8,128)(2,1)S(1)}, bf16[2048,784]{1,0:T(8,128)(2,1)}, u32[]{:S(2)}) copy-start(bf16[2048,784]{1,0:T(8,128)(2,1)} %copy.14.x_ref) | copy-start | bytes 9633796
  57.3 11.8 %collective-permute-start.5 = (bf16[128,256]{1,0:T(8,128)(2,1)S(1)}, bf16[128,256]{1,0:T(8,128)(2,1)S(1)}, u32[]{:S(2)}, u32[]{:S(2)}) collective-permute-start(bf16[128,256]{1,0:T(8,128)(2,1)S(1)} %convert_element_type.14), channel_id=1, source_target_pairs={{0,4},{4,8},{8,12},{12,16},{16,20},{20,24},{24,28},{1,5},{5,9},{9,... | collective-permute-start | bytes 196616 | tf_op jit(solution)/shard_map/ppermute | solution.py:325
  66.6 10.4 %copy-start.1 = (f32[8,8,64,64]{3,2,1,0:T(8,128)S(1)}, f32[8,8,64,64]{3,2,1,0:T(8,128)}, u32[]{:S(2)}) copy-start(f32[8,8,64,64]{3,2,1,0:T(8,128)} %coupling_ref.1) | copy-start | bytes 3145732
  66.6 10.4 %copy-start.3 = (f32[8,64,64]{2,1,0:T(8,128)S(1)}, f32[8,64,64]{2,1,0:T(8,128)}, u32[]{:S(2)}) copy-start(f32[8,64,64]{2,1,0:T(8,128)} %transfer_ref.3) | copy-start | bytes 393220
  66.6 10.4 %copy-start.4 = (f32[4,8,64,64]{3,2,1,0:T(8,128)S(1)}, f32[4,8,64,64]{3,2,1,0:T(8,128)}, u32[]{:S(2)}) copy-start(f32[4,8,64,64]{3,2,1,0:T(8,128)} %up_ref.1) | copy-start | bytes 1572868
  66.7 10.4 %copy-start.5 = (s32[8,8]{1,0:T(8,128)S(1)}, s32[8,8]{1,0:T(8,128)}, u32[]{:S(2)}) copy-start(s32[8,8]{1,0:T(8,128)} %far_leaf_ref.1) | copy-start | bytes 772
  66.7 10.4 %copy-start.6 = (s32[4,8]{1,0:T(4,128)S(1)}, s32[4,8]{1,0:T(4,128)}, u32[]{:S(2)}) copy-start(s32[4,8]{1,0:T(4,128)} %far_up_ref.1) | copy-start | bytes 388
  66.7 6.3 %collective-permute-start.9 = (bf16[128,256]{1,0:T(8,128)(2,1)S(1)}, bf16[128,256]{1,0:T(8,128)(2,1)S(1)}, u32[]{:S(2)}, u32[]{:S(2)}) collective-permute-start(bf16[128,256]{1,0:T(8,128)(2,1)S(1)} %convert_element_type.16), channel_id=1, source_target_pairs={{0,4},{4,8},{8,12},{12,16},{16,20},{20,24},{24,28},{1,5},{5,9},{9,... | collective-permute-start | bytes 196616 | tf_op jit(solution)/shard_map/ppermute | solution.py:330
  69.2 4.3 %collective-permute-start.6 = (f32[4,64,256]{2,1,0:T(8,128)S(1)}, f32[4,64,256]{2,1,0:T(8,128)S(1)}, u32[]{:S(2)}, u32[]{:S(2)}) collective-permute-start(f32[4,64,256]{2,1,0:T(8,128)S(1)} %select_add_fusion.1), channel_id=1, source_target_pairs={{0,1},{1,0},{2,3},{3,2},{4,5},{5,4},{6,7},{7,6},{8,9},{9,8},{10,11... | collective-permute-start | bytes 786440 | tf_op jit(solution)/shard_map/ppermute | solution.py:310
  73.1 2.8 %collective-permute-start.10 = (f32[4,64,256]{2,1,0:T(8,128)S(1)}, f32[4,64,256]{2,1,0:T(8,128)S(1)}, u32[]{:S(2)}, u32[]{:S(2)}) collective-permute-start(f32[4,64,256]{2,1,0:T(8,128)S(1)} %select_add_fusion), channel_id=1, source_target_pairs={{0,1},{1,0},{2,3},{3,2},{4,5},{5,4},{6,7},{7,6},{8,9},{9,8},{10,11... | collective-permute-start | bytes 786440 | tf_op jit(solution)/shard_map/ppermute | solution.py:310
  73.6 8.4 %collective-permute-start.7 = (bf16[4,32,256]{2,1,0:T(8,128)(2,1)S(1)}, bf16[4,32,256]{2,1,0:T(8,128)(2,1)S(1)}, u32[]{:S(2)}, u32[]{:S(2)}) collective-permute-start(bf16[4,32,256]{2,1,0:T(8,128)(2,1)S(1)} %slice.105), channel_id=1, source_target_pairs={{0,2},{1,3},{2,0},{3,1},{4,6},{5,7},{6,4},{7,5},{8,10},{9,11},{10,... | collective-permute-start | bytes 196616 | tf_op jit(solution)/shard_map/ppermute | solution.py:310
  76.1 5.9 %collective-permute-start.11 = (bf16[4,32,256]{2,1,0:T(8,128)(2,1)S(1)}, bf16[4,32,256]{2,1,0:T(8,128)(2,1)S(1)}, u32[]{:S(2)}, u32[]{:S(2)}) collective-permute-start(bf16[4,32,256]{2,1,0:T(8,128)(2,1)S(1)} %slice.104), channel_id=1, source_target_pairs={{0,2},{1,3},{2,0},{3,1},{4,6},{5,7},{6,4},{7,5},{8,10},{9,11},{10,... | collective-permute-start | bytes 196616 | tf_op jit(solution)/shard_map/ppermute | solution.py:310

commit v2 on v0

v2 whole, which is shorter than its diff:
```python
import functools
import math

import jax
import jax.numpy as jnp
from jax import lax
from jax.experimental import pallas as pl
from jax.experimental.pallas import tpu as pltpu
from jax.sharding import PartitionSpec as P

RIDGE = 0.5
LOG2E = math.log2(math.e)
FLAG_ROWS = 16
F32 = jnp.float32
BF16 = jnp.bfloat16
NN = (((1,), (0,)), ((), ()))
NT = (((1,), (1,)), ((), ()))
VMEM = pl.BlockSpec(memory_space=pltpu.VMEM)
SMEM = pl.BlockSpec(memory_space=pltpu.SMEM)
MIB = 1 << 20


def dot(a, b, dims):
    return lax.dot_general(a, b, dims, preferred_element_type=F32)


def halves(x):
    high = x.astype(BF16)
    return high, (x - high.astype(F32)).astype(BF16)


def split_dot(a, b, dims):
    a_high, a_low = halves(a)
    b_high, b_low = halves(b)
    return dot(a_high, b_high, dims) + (dot(a_high, b_low, dims) + dot(a_low, b_high, dims))


def half_split_dot(a, b, dims):
    b_high, b_low = halves(b)
    return dot(a, b_high, dims) + dot(a, b_low, dims)


def span(index, size):
    return pl.ds(pl.multiple_of(index * size, size), size)


def listed(lists_ref, row, leaf):
    found = lists_ref[row, 0] == leaf
    for k in range(1, lists_ref.shape[1]):
        found = found | (lists_ref[row, k] == leaf)
    return found


def pack_kernel(v_ref, bases_ref, transfer_ref, msg_ref):
    leaves, _, pts = bases_ref.shape
    coeffs = []
    lifted = []
    for leaf in range(leaves):
        v = v_ref[:, leaf * pts : (leaf + 1) * pts]
        coeffs.append(half_split_dot(v, bases_ref[leaf], NT))
        lifted.append(split_dot(coeffs[-1], transfer_ref[leaf], NN))
    parents = [lifted[2 * q] + lifted[2 * q + 1] for q in range(leaves // 2)]
    entries = coeffs + parents
    for e in range(len(entries) // 2):
        msg_ref[e] = jnp.concatenate(entries[2 * e : 2 * e + 2], axis=1).astype(BF16)


def assemble_kernel(leaves, sc_ref, lists_ref, x_ref, *refs):
    piece_refs, (v_ref, down_ref, up_ref) = refs[:-3], refs[-3:]
    features, points = x_ref.shape
    pts = points // leaves
    rows = v_ref.shape[0]
    cols = piece_refs[0].shape[0]
    even = [piece_refs[0][...]] + [p[:cols] for p in piece_refs[2:]]
    odd = [piece_refs[1][...]] + [p[cols:] for p in piece_refs[2:]]
    for spot, block in enumerate(even + odd):
        v_ref[spot * cols : (spot + 1) * cols] = block
    low, upper, base = sc_ref[0], sc_ref[2], sc_ref[3]

    def flags(leaf, first):
        found = [
            jnp.full((1, pts), listed(lists_ref, leaf, first + a).astype(F32))
            for a in range(leaves)
        ]
        found.append(jnp.zeros((FLAG_ROWS - leaves, pts), F32))
        return jnp.concatenate(found, axis=0).astype(BF16)

    down_ref[:rows] = v_ref[:, span(low, pts)]
    down_ref[rows:] = flags(low, base - leaves)
    up_ref[:features] = x_ref[:, span(upper, pts)]
    up_ref[features : features + rows] = v_ref[:, span(upper, pts)]
    up_ref[features + rows :] = flags(upper, base + leaves)


def row_sums(x, features):
    return jnp.sum(jnp.square(x.astype(F32)), axis=0, keepdims=True) * (LOG2E / features)


def tiles(x_b, x, col, row, features):
    cross = dot(x_b, x, NN) * (2.0 * LOG2E / features)
    return jnp.exp2(cross - (col + row)).astype(BF16)


def column_sums(x_b, features):
    return jnp.sum(jnp.square(x_b.astype(F32)), axis=1, keepdims=True) * (LOG2E / features)


def mask_row(flags, pts):
    return jnp.concatenate([jnp.full((1, pts), f.astype(F32)) for f in flags], axis=1)


def own_kernel(leaves, sc_ref, lists_ref, x_ref, v_ref, *refs):
    out_refs, sums_ref = refs[:4], refs[4]
    features, points = x_ref.shape
    pts = points // leaves
    rows = v_ref.shape[0]
    low, high, base = sc_ref[0], sc_ref[1], sc_ref[3]
    for leaf in range(leaves):
        here = slice(leaf * pts, (leaf + 1) * pts)
        sums_ref[:, here] = jnp.broadcast_to(
            row_sums(x_ref[:, here], features), (sums_ref.shape[0], pts)
        )
    half = leaves // 2
    updates = [None, None]
    x_bs = [x_ref[:, span(b, pts)].T for b in (high, low)]
    cols = [column_sums(x_b, features) for x_b in x_bs]
    for group in (1, 0):
        here = slice(group * half * pts, (group + 1) * half * pts)
        total = None
        for which, b in enumerate((high, low)[: 2 - group]):
            tile = tiles(x_bs[which], x_ref[:, here], cols[which], sums_ref[0:1, here], features)
            leaf_ids = [group * half + i for i in range(half)]
            to_a = [(a <= b) & listed(lists_ref, a, base + b) for a in leaf_ids]
            to_b = [(a < b) & listed(lists_ref, b, base + a) for a in leaf_ids]
            term = dot(v_ref[:, span(b, pts)], tile, NN) * mask_row(to_a, pts)
            total = term if total is None else total + term
            masked = v_ref[:, here] * mask_row(to_b, pts).astype(BF16)
            back = dot(masked, tile, NT)
            updates[which] = back if updates[which] is None else updates[which] + back
        out_refs[2 * group][...] = total[: rows // 2]
        out_refs[2 * group + 1][...] = total[rows // 2 :]
    for b, back, group in ((high, updates[0], 1), (low, updates[1], 0)):
        place = span(b - group * half, pts)
        out_refs[2 * group][:, place] += back[: rows // 2]
        out_refs[2 * group + 1][:, place] += back[rows // 2 :]


def low_kernel(
    leaves, sc_ref, lists_ref, x_ref, halo_ref, near_ref, sums_ref, v_ref, *refs
):
    ins, outs, back_ref = refs[:4], refs[4:8], refs[8]
    features, points = x_ref.shape
    pts = points // leaves
    rows = v_ref.shape[0]
    half = leaves // 2
    b, base = sc_ref[0], sc_ref[3]
    x_b = halo_ref[...].T
    col = column_sums(x_b, features)
    back = None
    for group in (0, 1):
        here = slice(group * half * pts, (group + 1) * half * pts)
        leaf_ids = [group * half + i for i in range(half)]
        tile = tiles(x_b, x_ref[:, here], col, sums_ref[0:1, here], features)
        to_a = [(a >= b) & listed(lists_ref, a, base + leaves + b) for a in leaf_ids]
        term = dot(near_ref[:rows], tile, NN) * mask_row(to_a, pts)
        outs[2 * group][...] = ins[2 * group][...] + term[: rows // 2]
        outs[2 * group + 1][...] = ins[2 * group + 1][...] + term[rows // 2 :]
        to_b = jnp.concatenate([near_ref[rows + a : rows + a + 1, :] for a in leaf_ids], axis=1)
        to_b = to_b * mask_row([a >= b for a in leaf_ids], pts).astype(BF16)
        term = dot(v_ref[:, here] * to_b, tile, NT)
        back = term if back is None else back + term
    back_ref[...] = back.astype(back_ref.dtype)


def high_kernel(leaves, sc_ref, lists_ref, x_ref, halo_ref, sums_ref, v_ref, *refs):
    ins, outs = refs[:2], refs[2:]
    features, points = x_ref.shape
    pts = points // leaves
    rows = v_ref.shape[0]
    half = leaves // 2
    b, base = sc_ref[2], sc_ref[3]
    x_b = halo_ref[:features].T
    col = column_sums(x_b, features)
    here = slice(half * pts, leaves * pts)
    leaf_ids = [half + i for i in range(half)]
    tile = tiles(x_b, x_ref[:, here], col, sums_ref[0:1, here], features)
    to_a = [(a <= b) & listed(lists_ref, a, base - leaves + b) for a in leaf_ids]
    term = dot(halo_ref[features : features + rows], tile, NN) * mask_row(to_a, pts)
    first = features + rows
    to_b = jnp.concatenate([halo_ref[first + a : first + a + 1, :] for a in leaf_ids], axis=1)
    to_b = to_b * mask_row([a <= b for a in leaf_ids], pts).astype(BF16)
    back = dot(v_ref[:, here] * to_b, tile, NT)
    for i in (0, 1):
        block = slice(i * rows // 2, (i + 1) * rows // 2)
        outs[i][:, : half * pts] = ins[i][...] + term[block]
        outs[i][:, half * pts :] = back[block]


def merge_kernel(sc_ref, keep_ref, send_ref, back_ref, keep_out_ref, send_out_ref):
    rows, pts = back_ref.shape
    keep_out_ref[...] = keep_ref[...]
    send_out_ref[...] = send_ref[...]
    place = span(sc_ref[0], pts)
    keep_out_ref[:, place] += back_ref[: rows // 2].astype(F32)
    send_out_ref[:, place] += back_ref[rows // 2 :].astype(F32)


def split_kernel(backs, keep_ref, came_ref, out_ref, *refs):
    cols, wide = out_ref.shape
    blocks = keep_ref.shape[0] // cols
    pts = keep_ref.shape[1] - wide
    for m in range(blocks):
        block = slice(m * cols, (m + 1) * cols)
        total = keep_ref[block, :wide] + came_ref[block, :wide]
        if m == 0:
            out_ref[...] = total
        else:
            refs[m - 1][...] = total.astype(BF16)
        if backs:
            refs[blocks - 1 + m][:, :pts] = keep_ref[block, wide:].astype(BF16)
            refs[blocks - 1 + m][:, pts:] = came_ref[block, wide:].astype(BF16)


def far_kernel(
    sc_ref, far_leaf_ref, far_up_ref, all_ref, coupling_ref, up_ref, transfer_ref, bases_ref,
    v_ref, out_ref
):
    leaves, rank, pts = bases_ref.shape
    device = sc_ref[4]

    def entry(index, per_device, first):
        owner = lax.div(index, per_device)
        place = lax.rem(index, per_device)
        pair = all_ref[owner ^ device, first + lax.div(place, 2)].astype(F32)
        swapped = pltpu.roll(pair, rank, 1)
        return jnp.where(lax.rem(place, 2) == 1, swapped, pair)[:, :rank].astype(BF16)

    def field(list_ref, row, matrix_ref, per_device, first):
        total = None
        for k in range(list_ref.shape[1]):
            c = entry(list_ref[row, k], per_device, first)
            both = jnp.concatenate(halves(matrix_ref[row, k]), axis=0)
            term = dot(c, both, NT)
            total = term if total is None else total + term
        return total[:, :rank] + total[:, rank:]

    for parent in range(leaves // 2):
        upper = field(far_up_ref, parent, up_ref, leaves // 2, leaves // 2)
        for leaf in (2 * parent, 2 * parent + 1):
            total = field(far_leaf_ref, leaf, coupling_ref, leaves, 0)
            total = total + split_dot(upper, transfer_ref[leaf], NT)
            here = slice(leaf * pts, (leaf + 1) * pts)
            far = split_dot(total, bases_ref[leaf], NN)
            out_ref[:, here] = far + RIDGE * v_ref[:, here].astype(F32)


def finish_kernel(blocks, sc_ref, far_ref, *refs):
    out_ref = refs[-1]
    low_refs, high_refs = refs[:blocks], refs[blocks : 2 * blocks]
    back_refs = refs[2 * blocks : 3 * blocks]
    wide = low_refs[0].shape[1]
    pts = back_refs[0].shape[1] // 2
    column = sc_ref[0]
    for group, part_refs in enumerate((low_refs, high_refs)):
        here = slice(group * wide, (group + 1) * wide)
        total = part_refs[0][...]
        for ref in part_refs[1:]:
            total = total + ref[...].astype(F32)
        out_ref[:, here] = far_ref[:, here] + total
    for m in range(blocks):
        for core in (0, 1):
            place = span((column ^ (2 * m + core)) + wide // pts, pts)
            out_ref[:, place] += back_refs[m][:, core * pts : (core + 1) * pts].astype(F32)


def call(body, out_shape, in_specs, args, name, flops=0, bytes_accessed=0):
    return pl.pallas_call(
        body,
        out_shape=out_shape,
        in_specs=in_specs,
        out_specs=jax.tree.map(lambda _: VMEM, out_shape),
        compiler_params=pltpu.CompilerParams(vmem_limit_bytes=32 * MIB),
        cost_estimate=pl.CostEstimate(
            flops=flops, bytes_accessed=bytes_accessed, transcendentals=0
        ),
        name=name,
    )(*args)


def local(
    points, vectors, bases, leaf_coupling, transfer, up_coupling, far_leaf, far_up, near_lists
):
    leaves, pts, rank = bases.shape
    features = points.shape[1]
    cols = vectors.shape[1]
    half = leaves // 2
    shape = jax.ShapeDtypeStruct
    leaf_devices = lax.axis_size("leaf")
    rhs_devices = lax.axis_size("rhs")
    assert leaves == 2 * rhs_devices and leaves <= FLAG_ROWS
    rows = cols * rhs_devices
    wide = half * pts
    device = lax.axis_index("leaf")
    column = lax.axis_index("rhs")
    low, high, upper = column, leaves - 1 - column, half + column
    scalars = jnp.stack([low, high, upper, device * leaves, device]).astype(jnp.int32)

    def over_rhs(array, mask):
        return lax.ppermute(array, "rhs", [(i, i ^ mask) for i in range(rhs_devices)])

    def over_leaf(array, step, mask=0):
        pairs = [
            (i * rhs_devices + j, (i + step) * rhs_devices + (j ^ mask))
            for i in range(leaf_devices)
            if 0 <= i + step < leaf_devices
            for j in range(rhs_devices)
        ]
        return lax.ppermute(array, ("leaf", "rhs"), pairs)

    x = points.T
    v = vectors.T
    bases_t = jnp.swapaxes(bases, 1, 2)

    halo_low = over_leaf(lax.dynamic_slice_in_dim(x, low * pts, pts, 1), -1)
    v_other = over_rhs(v, 1)
    both = jnp.concatenate([v, v_other], axis=0)
    pieces = [v, v_other] + [over_rhs(both, m) for m in range(2, rhs_devices, 2)]

    message = call(
        pack_kernel,
        shape((half + half // 2, cols, 2 * rank), BF16),
        [VMEM] * 3,
        (v, bases_t, transfer),
        "pack",
        10**8,
        3 * MIB,
    )
    everything = message[None]
    bit = 1
    while bit < leaf_devices:
        arrived = lax.ppermute(everything, "leaf", [(i, i ^ bit) for i in range(leaf_devices)])
        everything = jnp.concatenate([everything, arrived], axis=0)
        bit *= 2

    all_v, down, up = call(
        functools.partial(assemble_kernel, leaves),
        (
            shape((rows, leaves * pts), BF16),
            shape((rows + FLAG_ROWS, pts), BF16),
            shape((features + rows + FLAG_ROWS, pts), BF16),
        ),
        [SMEM] * 2 + [VMEM] * (1 + len(pieces)),
        (scalars, near_lists, x, *pieces),
        "assemble",
        0,
        3 * MIB,
    )
    near_low = over_leaf(down, -1)
    halo_high = over_leaf(up, 1)

    part = shape((rows // 2, wide), F32)
    *totals, sums = call(
        functools.partial(own_kernel, leaves),
        (part,) * 4 + (shape((8, leaves * pts), F32),),
        [SMEM] * 2 + [VMEM] * 2,
        (scalars, near_lists, x, all_v),
        "own_tiles",
        3 * 10**9,
        6 * MIB,
    )
    *totals, back_low = call(
        functools.partial(low_kernel, leaves),
        (part,) * 4 + (shape((rows, pts), BF16),),
        [SMEM] * 2 + [VMEM] * 9,
        (scalars, near_lists, x, halo_low, near_low, sums, all_v, *totals),
        "low_tiles",
        2 * 10**9,
        6 * MIB,
    )
    came_low = over_leaf(back_low, 1)
    keep_low, send_low = call(
        merge_kernel,
        (part,) * 2,
        [SMEM] + [VMEM] * 3,
        (scalars, *totals[:2], came_low),
        "merge",
        0,
        MIB,
    )

    blocks = rhs_devices // 2
    kept = shape((cols, wide), F32)
    sent = shape((cols, wide), BF16)

    def split(keep, came, backs):
        outs = (kept,) + (sent,) * (blocks - 1)
        if backs:
            outs += (shape((cols, 2 * pts), BF16),) * blocks
        return call(
            functools.partial(split_kernel, backs), outs, [VMEM] * 2, (keep, came), "split",
            0, MIB
        )

    first, *others = split(keep_low, over_rhs(send_low, 1), False)
    low_parts = [first] + [over_rhs(block, 2 * m + 2) for m, block in enumerate(others)]

    longer = shape((rows // 2, wide + pts), F32)
    keep_high, send_high = call(
        functools.partial(high_kernel, leaves),
        (longer,) * 2,
        [SMEM] * 2 + [VMEM] * 6,
        (scalars, near_lists, x, halo_high, sums, all_v, *totals[2:]),
        "high_tiles",
        10**9,
        4 * MIB,
    )
    first, *others = split(keep_high, over_rhs(send_high, 1), True)
    backs = [over_leaf(block, -1, 2 * m) for m, block in enumerate(others[blocks - 1 :])]
    high_parts = [first] + [
        over_rhs(block, 2 * m + 2) for m, block in enumerate(others[: blocks - 1])
    ]

    far = call(
        far_kernel,
        shape((cols, leaves * pts), F32),
        [SMEM] * 3 + [VMEM] * 6,
        (
            scalars, far_leaf, far_up, everything, leaf_coupling, up_coupling, transfer, bases_t,
            v,
        ),
        "far_field",
        10**9,
        6 * MIB,
    )
    out = call(
        functools.partial(finish_kernel, blocks),
        shape((cols, leaves * pts), F32),
        [SMEM] + [VMEM] * (1 + 3 * blocks),
        (scalars, far, *low_parts, *high_parts, *backs),
        "finish",
        0,
        2 * MIB,
    )
    return out.T


def solution(mesh):
    return jax.shard_map(
        local,
        mesh=mesh,
        in_specs=(
            P("leaf", None),
            P("leaf", "rhs"),
            P("leaf", None, None),
            P("leaf", None, None, None),
            P("leaf", None, None),
            P("leaf", None, None, None),
            P("leaf", None),
            P("leaf", None),
            P("leaf", None),
        ),
        out_specs=P("leaf", "rhs"),
        check_vma=False,
    )
```

time: 362 us -> 71.1 us (0.20); the launches traced: 356 us -> 70.6 us
  waiting for transfers between devices: 145 us -> 15.3 us
  blocking collectives: 59.7 us -> 0 us
  local copies, waits for them, and re-layouts: 50.3 us -> 7.55 us
  matrix products: 42.6 us -> 0 us
  loops' own time: 20.1 us -> 0 us
  Pallas kernels: 0 us -> 17.4 us
  starting transfers between devices: 12.8 us -> 29 us
  between operations: 13.7 us -> 0.35 us
  other arithmetic: 12.3 us -> 1 us
    ppermute x4 -> x15, waiting for transfers between devices: 135 us -> 15.3 us  [the longest x3 8.14 us: local(): lax.ppermute(everything, 'leaf', [(i, i ^ bit) for i in range(leaf_device...]
    all_gather x2 -> x0, blocking collectives: 59.7 us -> none  [the longest x1 30.9 us: local(): lax.all_gather(parents.reshape(half_count, rank_size * columns), 'leaf',...]
    dot_general x24 -> x0, matrix products: 42.6 us -> none  [the longest x16 32.1 us: near_tiles(): jnp.dot(kernel, near_vectors, preferred_element_type=jnp.float32)]
    another operation x1 -> x0, loops' own time: 20.1 us -> none  [local(): lax.map(partial(near_tiles, all_vectors), (point_blocks, norm_blocks, par...]
    pallas_call x0 -> x10, Pallas kernels: none -> 17.4 us  [call(): pl.pallas_call(body, out_shape=out_shape, in_specs=in_specs, out_specs=ja...]
    ppermute x4 -> x15, starting transfers between devices: 12.7 us -> 29 us  [the longest x6 23.5 us: over_leaf(): return lax.ppermute(array, ('leaf', 'rhs'), pairs)]
    while x2 -> x0, local copies, waits for them, and re-layouts: 16.2 us -> none  [local(): lax.map(partial(near_tiles, all_vectors), (point_blocks, norm_blocks, par...]
    all_gather x1 -> x0, waiting for transfers between devices: 9.66 us -> none  [local(): all_vectors = lax.all_gather(window_vectors, 'rhs', axis=1, tiled=True)]
  transfers between devices with their start and end apart: 6 -> 15, of which waited for: 2 -> 4; matrix products, arithmetic and copies ran while one was open for 10% -> 2% of each run, Pallas kernels for 0% -> 23%
where the time goes in v2:
time: 71.1 us; the launch traced here: 70.6 us
  starting transfers between devices  29 us (41%)
  Pallas kernels  17.4 us (24%)
  waiting for transfers between devices  15.3 us (22%)
  local copies, waits for them, and re-layouts  7.55 us (11%)
  other arithmetic  1 us (1%)
    ppermute x6, starting transfers between devices, over_leaf(): return lax.ppermute(array, ('leaf', 'rhs'), pairs)  23.5 us
    pallas_call x10, Pallas kernels, call(): pl.pallas_call(body, out_shape=out_shape, in_specs=in_specs, out_specs=ja...  17.4 us
    ppermute x3, waiting for transfers between devices, local(): lax.ppermute(everything, 'leaf', [(i, i ^ bit) for i in range(leaf_device...  8.14 us
    unnamed x30, local copies, waits for them, and re-layouts  6.45 us
    ppermute x6, waiting for transfers between devices, over_leaf(): return lax.ppermute(array, ('leaf', 'rhs'), pairs)  5.56 us
    ppermute x6, starting transfers between devices, over_rhs(): lax.ppermute(array, 'rhs', [(i, i ^ mask) for i in range(rhs_devices)])  4.36 us
    ppermute x6, waiting for transfers between devices, over_rhs(): lax.ppermute(array, 'rhs', [(i, i ^ mask) for i in range(rhs_devices)])  1.58 us
  transfers between devices with their start and end apart: 15, of which 4 were waited for; matrix products, arithmetic and copies ran while one was open for 2% of the time, Pallas kernels for 23%

profile of v2, /device:TPU:10, one launch (start us, length us, event | category | flops | bytes accessed | tf_op | source)
XLA Modules:
  0.0 70.6 jit_solution(13430786215421635020)
XLA Ops:
  0.0 1.6 %collective-permute-done.4.refs_1_ = bf16[32,2048]{1,0:T(8,128)(2,1)S(1)} collective-permute-done((bf16[32,2048]{1,0:T(8,128)(2,1)}, bf16[32,2048]{1,0:T(8,128)(2,1)S(1)}, u32[]{:S(2)}, u32[]{:S(2)}) %collective-permute-start.4) | collective-permute-done | bytes 131104 | tf_op jit(solution)/shard_map/ppermute | solution.py:309
  1.6 0.9 %pad_maximum_fusion.1 = bf16[64,2048]{1,0:T(8,128)(2,1)S(1)} fusion(bf16[32,2048]{1,0:T(8,128)(2,1)S(1)} %collective-permute-done.4.refs_1_, bf16[32,2048]{1,0:T(8,128)(2,1)} %bitcast.19), kind=kLoop, calls=%fused_computation.2 | loop fusion | flops 524288 | bytes 524288 | tf_op jit(solution)/shard_map/concatenate | solution.py:326
  2.5 1.6 %collective-permute-start.5 = (bf16[64,2048]{1,0:T(8,128)(2,1)S(1)}, bf16[64,2048]{1,0:T(8,128)(2,1)S(1)}, u32[]{:S(2)}, u32[]{:S(2)}) collective-permute-start(bf16[64,2048]{1,0:T(8,128)(2,1)S(1)} %pad_maximum_fusion.1), channel_id=1, source_target_pairs={{0,2},{1,3},{2,0},{3,1},{4,6},{5,7},{6,4},{7,5},{8,10},{9,11},{10,... | collective-permute-start | bytes 786440 | tf_op jit(solution)/shard_map/ppermute | solution.py:309
  4.1 1.0 %copy-done.3 = f32[8,256,64]{1,2,0:T(8,128)S(1)} copy-done((f32[8,256,64]{1,2,0:T(8,128)S(1)}, f32[8,256,64]{1,2,0:T(8,128)}, u32[]{:S(2)}) %copy-start.3) | copy-done | bytes 524312
  5.1 0.9 %copy-done.5 = bf16[2048,32]{0,1:T(8,128)(2,1)S(1)} copy-done((bf16[2048,32]{0,1:T(8,128)(2,1)S(1)}, bf16[2048,32]{0,1:T(8,128)(2,1)}, u32[]{:S(2)}) %copy-start.5) | copy-done | bytes 131096
  6.0 0.9 %copy-done.9 = f32[8,64,64]{2,1,0:T(8,128)S(1)} copy-done((f32[8,64,64]{2,1,0:T(8,128)S(1)}, f32[8,64,64]{2,1,0:T(8,128)}, u32[]{:S(2)}) %copy-start.9) | copy-done | bytes 131096
  7.0 1.2 %pack.1 = bf16[6,32,128]{2,1,0:T(8,128)(2,1)S(1)} custom-call(bf16[32,2048]{1,0:T(8,128)(2,1)S(1)} %bitcast.20, f32[8,64,256]{2,1,0:T(8,128)S(1)} %bitcast.16, f32[8,64,64]{2,1,0:T(8,128)S(1)} %copy-done.9), custom_call_target="tpu_custom_call" | custom-call | flops 100000000 | bytes 3145728 | tf_op jit(solution)/shard_map/pack/pallas_call | solution.py:277
  8.8 1.0 %dynamic-slice_bitcast_fusion = bf16[784,256]{1,0:T(8,128)(2,1)S(1)} fusion(bf16[2048,784]{0,1:T(8,128)(2,1)} %param.9, s32[]{:T(128)S(6)} %select_n.3), kind=kLoop, calls=%fused_computation | loop fusion | bytes 802820 | tf_op jit(solution)/shard_map/dynamic_slice | solution.py:324
  9.8 3.4 %collective-permute-start.3 = (bf16[784,256]{1,0:T(8,128)(2,1)S(1)}, bf16[784,256]{1,0:T(8,128)(2,1)S(1)}, u32[]{:S(2)}, u32[]{:S(2)}) collective-permute-start(bf16[784,256]{1,0:T(8,128)(2,1)S(1)} %dynamic-slice_bitcast_fusion), channel_id=1, source_target_pairs={{4,0},{5,1},{6,2},{7,3},{8,4},{9,5},{10,6},{11,7},{12,8},{13,9},{1... | collective-permute-start | bytes 1204232 | tf_op jit(solution)/shard_map/ppermute | solution.py:318
  13.3 1.9 %copy-done = bf16[2048,784]{0,1:T(8,128)(2,1)S(1)} copy-done((bf16[2048,784]{0,1:T(8,128)(2,1)S(1)}, bf16[2048,784]{0,1:T(8,128)(2,1)}, u32[]{:S(2)}) %copy-start) | copy-done | bytes 3211288
  15.2 0.9 %copy-done.6 = bf16[2048,32]{0,1:T(8,128)(2,1)S(1)} copy-done((bf16[2048,32]{0,1:T(8,128)(2,1)S(1)}, bf16[2048,32]{0,1:T(8,128)(2,1)}, u32[]{:S(2)}) %copy-start.6) | copy-done | bytes 131096
  17.5 3.5 %collective-permute-start.10 = (bf16[928,256]{1,0:T(8,128)(2,1)S(1)}, bf16[928,256]{1,0:T(8,128)(2,1)S(1)}, u32[]{:S(2)}, u32[]{:S(2)}) collective-permute-start(bf16[928,256]{1,0:T(8,128)(2,1)S(1)} %get-tuple-element.42), channel_id=1, source_target_pairs={{0,4},{1,5},{2,6},{3,7},{4,8},{5,9},{6,10},{7,11},{8,12},{9,13},{1... | collective-permute-start | bytes 1425416 | tf_op jit(solution)/shard_map/ppermute | solution.py:318
  21.5 2.5 %collective-permute-start.6 = (bf16[144,256]{1,0:T(8,128)(2,1)S(1)}, bf16[144,256]{1,0:T(8,128)(2,1)S(1)}, u32[]{:S(2)}, u32[]{:S(2)}) collective-permute-start(bf16[144,256]{1,0:T(8,128)(2,1)S(1)} %get-tuple-element.28), channel_id=1, source_target_pairs={{4,0},{5,1},{6,2},{7,3},{8,4},{9,5},{10,6},{11,7},{12,8},{13,9},{1... | collective-permute-start | bytes 221192 | tf_op jit(solution)/shard_map/ppermute | solution.py:318
  24.1 3.6 %own_tiles.1 = (f32[64,1024]{1,0:T(8,128)S(1)}, f32[64,1024]{1,0:T(8,128)S(1)}, f32[64,1024]{1,0:T(8,128)S(1)}, f32[64,1024]{1,0:T(8,128)S(1)}, f32[8,2048]{1,0:T(8,128)S(1)}) custom-call(s32[5]{0:T(128)S(1)} %stack.23.sc_ref, s32[8,8]{1,0:T(8,128)S(1)} %copy-done.12, bf16[784,2048]{1,0:T(8,128)(2,1)S(1)} %bitcast.13, ...), custom_call_target="tpu_custom_call" | custom-call | flops 3000000000 | bytes 6291456 | tf_op jit(solution)/shard_map/own_tiles/pallas_call | solution.py:277
  27.7 4.8 %collective-permute-done.3.halo_ref = bf16[784,256]{1,0:T(8,128)(2,1)S(1)} collective-permute-done((bf16[784,256]{1,0:T(8,128)(2,1)S(1)}, bf16[784,256]{1,0:T(8,128)(2,1)S(1)}, u32[]{:S(2)}, u32[]{:S(2)}) %collective-permute-start.3) | collective-permute-done | bytes 401440 | tf_op jit(solution)/shard_map/ppermute | solution.py:318
  33.2 2.8 %low_tiles.1 = (f32[64,1024]{1,0:T(8,128)S(1)}, f32[64,1024]{1,0:T(8,128)S(1)}, f32[64,1024]{1,0:T(8,128)S(1)}, f32[64,1024]{1,0:T(8,128)S(1)}, bf16[128,256]{1,0:T(8,128)(2,1)S(1)}) custom-call(s32[5]{0:T(128)S(1)} %stack.23.sc_ref, s32[8,8]{1,0:T(8,128)S(1)} %copy-done.12, bf16[784,2048]{1,0:T(8,128)(2,1)S(1)} %bitcast.14, ...), custom_call_target="tpu_custom_call" | custom-call | flops 2000000000 | bytes 6291456 | tf_op jit(solution)/shard_map/low_tiles/pallas_call | solution.py:277
  36.1 5.4 %collective-permute-start.7 = (bf16[128,256]{1,0:T(8,128)(2,1)S(1)}, bf16[128,256]{1,0:T(8,128)(2,1)S(1)}, u32[]{:S(2)}, u32[]{:S(2)}) collective-permute-start(bf16[128,256]{1,0:T(8,128)(2,1)S(1)} %get-tuple-element.37), channel_id=1, source_target_pairs={{0,4},{1,5},{2,6},{3,7},{4,8},{5,9},{6,10},{7,11},{8,12},{9,13},{1... | collective-permute-start | bytes 196616 | tf_op jit(solution)/shard_map/ppermute | solution.py:318
  41.6 1.7 %high_tiles.1 = (f32[64,1280]{1,0:T(8,128)S(1)}, f32[64,1280]{1,0:T(8,128)S(1)}) custom-call(s32[5]{0:T(128)S(1)} %stack.23.sc_ref, s32[8,8]{1,0:T(8,128)S(1)} %copy-done.12, bf16[784,2048]{1,0:T(8,128)(2,1)S(1)} %bitcast.15, bf16[928,256]{1,0:T(8,128)(2,1)S(1)} %collective-permute-done.10.halo_ref, f32[8,2048]{1,0:T(8,128)S(1)} %get-tuple-element.30.sums_ref, ...), custom_call_target="tpu_custom_call" | custom-call | flops 1000000000 | bytes 4194304 | tf_op jit(solution)/shard_map/high_tiles/pallas_call | solution.py:277
  44.7 8.1 %collective-permute-done.2 = bf16[4,6,32,128]{3,2,1,0:T(8,128)(2,1)S(1)} collective-permute-done((bf16[4,6,32,128]{3,2,1,0:T(8,128)(2,1)S(1)}, bf16[4,6,32,128]{3,2,1,0:T(8,128)(2,1)S(1)}, u32[]{:S(2)}, u32[]{:S(2)}) %collective-permute-start.2) | collective-permute-done | bytes 196640 | tf_op jit(solution)/shard_map/ppermute | solution.py:341
  53.5 1.6 %collective-permute-start.12 = (bf16[32,1024]{1,0:T(8,128)(2,1)S(1)}, bf16[32,1024]{1,0:T(8,128)(2,1)S(1)}, u32[]{:S(2)}, u32[]{:S(2)}) collective-permute-start(bf16[32,1024]{1,0:T(8,128)(2,1)S(1)} %get-tuple-element.48), channel_id=1, source_target_pairs={{0,2},{1,3},{2,0},{3,1},{4,6},{5,7},{6,4},{7,5},{8,10},{9,11},{10,... | collective-permute-start | bytes 196616 | tf_op jit(solution)/shard_map/ppermute | solution.py:309
  55.1 3.1 %collective-permute-start.13 = (bf16[32,512]{1,0:T(8,128)(2,1)S(1)}, bf16[32,512]{1,0:T(8,128)(2,1)S(1)}, u32[]{:S(2)}, u32[]{:S(2)}) collective-permute-start(bf16[32,512]{1,0:T(8,128)(2,1)S(1)} %get-tuple-element.49), channel_id=1, source_target_pairs={{4,0},{5,1},{6,2},{7,3},{8,4},{9,5},{10,6},{11,7},{12,8},{13,9},{1... | collective-permute-start | bytes 98312 | tf_op jit(solution)/shard_map/ppermute | solution.py:318
  58.3 5.6 %collective-permute-start.14 = (bf16[32,512]{1,0:T(8,128)(2,1)S(1)}, bf16[32,512]{1,0:T(8,128)(2,1)S(1)}, u32[]{:S(2)}, u32[]{:S(2)}) collective-permute-start(bf16[32,512]{1,0:T(8,128)(2,1)S(1)} %get-tuple-element.50), channel_id=1, source_target_pairs={{4,2},{5,3},{6,0},{7,1},{8,6},{9,7},{10,4},{11,5},{12,10},{13,11},... | collective-permute-start | bytes 98312 | tf_op jit(solution)/shard_map/ppermute | solution.py:318
  64.0 5.3 %far_field.1.far_ref = f32[32,2048]{1,0:T(8,128)S(1)} custom-call(s32[5]{0:T(128)S(1)} %stack.23.sc_ref, s32[8,8]{1,0:T(8,128)S(1)} %copy-done.13, s32[4,8]{1,0:T(4,128)S(1)} %copy-done.14, bf16[8,6,32,128]{3,2,1,0:T(8,128)(2,1)S(1)} %pad_maximum_fusion.all_ref, f32[8,8,64,64]{3,2,1,0:T(8,128)S(1)} %copy-done.2, f32[4,8,64,64]{3,2,1,0:T(8,128)S(1)} %copy-done.8, ...), custom_call_target="tpu_custom_call" | custom-call | flops 1000000000 | bytes 6291456 | tf_op jit(solution)/shard_map/far_field/pallas_call | solution.py:277
  69.3 1.3 %finish.1 = f32[32,2048]{1,0:T(8,128)} custom-call(s32[5]{0:T(128)S(1)} %stack.23.sc_ref, f32[32,2048]{1,0:T(8,128)S(1)} %far_field.1.far_ref, f32[32,1024]{1,0:T(8,128)S(1)} %get-tuple-element.40.refs_0_, bf16[32,1024]{1,0:T(8,128)(2,1)S(1)} %collective-permute-done.9.refs_1_, f32[32,1024]{1,0:T(8,128)S(1)} %get-tuple-element.47.refs_2_, ...), custom_call_target="tpu_custom_call" | custom-call | bytes 2097152 | tf_op jit(solution)/shard_map/finish/pallas_call | solution.py:277
  (52 shorter events, 5.4 us)
Async XLA Ops:
  0.0 24.1 %copy-start.12 = (s32[8,8]{1,0:T(8,128)S(1)}, s32[8,8]{1,0:T(8,128)}, u32[]{:S(2)}) copy-start(s32[8,8]{1,0:T(8,128)} %lists_ref.7) | copy-start | bytes 772
  0.0 1.6 %collective-permute-start.4 = (bf16[32,2048]{1,0:T(8,128)(2,1)}, bf16[32,2048]{1,0:T(8,128)(2,1)S(1)}, u32[]{:S(2)}, u32[]{:S(2)}) collective-permute-start(bf16[32,2048]{1,0:T(8,128)(2,1)} %bitcast.18), channel_id=1, source_target_pairs={{0,1},{1,0},{2,3},{3,2},{4,5},{5,4},{6,7},{7,6},{8,9},{9,8},{10,11... | collective-permute-start | bytes 393224 | tf_op jit(solution)/shard_map/ppermute | solution.py:309
  2.5 10.8 %collective-permute-start.5 = (bf16[64,2048]{1,0:T(8,128)(2,1)S(1)}, bf16[64,2048]{1,0:T(8,128)(2,1)S(1)}, u32[]{:S(2)}, u32[]{:S(2)}) collective-permute-start(bf16[64,2048]{1,0:T(8,128)(2,1)S(1)} %pad_maximum_fusion.1), channel_id=1, source_target_pairs={{0,2},{1,3},{2,0},{3,1},{4,6},{5,7},{6,4},{7,5},{8,10},{9,11},{10,... | collective-permute-start | bytes 786440 | tf_op jit(solution)/shard_map/ppermute | solution.py:309
  8.2 12.8 %collective-permute-start = (bf16[1,6,32,128]{3,2,1,0:T(8,128)(2,1)S(1)}, bf16[1,6,32,128]{3,2,1,0:T(8,128)(2,1)S(1)}, u32[]{:S(2)}, u32[]{:S(2)}) collective-permute-start(bf16[1,6,32,128]{3,2,1,0:T(8,128)(2,1)S(1)} %bitcast.23), channel_id=1, source_target_pairs={{0,4},{4,0},{8,12},{12,8},{16,20},{20,16},{24,28},{28,24},{1,5},{5... | collective-permute-start | bytes 147464 | tf_op jit(solution)/shard_map/ppermute | solution.py:341
  9.8 22.7 %collective-permute-start.3 = (bf16[784,256]{1,0:T(8,128)(2,1)S(1)}, bf16[784,256]{1,0:T(8,128)(2,1)S(1)}, u32[]{:S(2)}, u32[]{:S(2)}) collective-permute-start(bf16[784,256]{1,0:T(8,128)(2,1)S(1)} %dynamic-slice_bitcast_fusion), channel_id=1, source_target_pairs={{4,0},{5,1},{6,2},{7,3},{8,4},{9,5},{10,6},{11,7},{12,8},{13,9},{1... | collective-permute-start | bytes 1204232 | tf_op jit(solution)/shard_map/ppermute | solution.py:318
  16.8 7.3 %copy-start.1 = (bf16[2048,784]{0,1:T(8,128)(2,1)S(1)}, bf16[2048,784]{0,1:T(8,128)(2,1)}, u32[]{:S(2)}) copy-start(bf16[2048,784]{0,1:T(8,128)(2,1)} %param.9) | copy-start | bytes 9633796
  17.5 24.0 %collective-permute-start.10 = (bf16[928,256]{1,0:T(8,128)(2,1)S(1)}, bf16[928,256]{1,0:T(8,128)(2,1)S(1)}, u32[]{:S(2)}, u32[]{:S(2)}) collective-permute-start(bf16[928,256]{1,0:T(8,128)(2,1)S(1)} %get-tuple-element.42), channel_id=1, source_target_pairs={{0,4},{1,5},{2,6},{3,7},{4,8},{5,9},{6,10},{7,11},{8,12},{9,13},{1... | collective-permute-start | bytes 1425416 | tf_op jit(solution)/shard_map/ppermute | solution.py:318
  21.0 22.4 %collective-permute-start.1 = (bf16[2,6,32,128]{3,2,1,0:T(8,128)(2,1)S(1)}, bf16[2,6,32,128]{3,2,1,0:T(8,128)(2,1)S(1)}, u32[]{:S(2)}, u32[]{:S(2)}) collective-permute-start(bf16[2,6,32,128]{3,2,1,0:T(8,128)(2,1)S(1)} %pad_maximum_fusion.3), channel_id=1, source_target_pairs={{0,8},{4,12},{8,0},{12,4},{16,24},{20,28},{24,16},{28,20},{1,9},{5... | collective-permute-start | bytes 294920 | tf_op jit(solution)/shard_map/ppermute | solution.py:341
  21.5 11.7 %collective-permute-start.6 = (bf16[144,256]{1,0:T(8,128)(2,1)S(1)}, bf16[144,256]{1,0:T(8,128)(2,1)S(1)}, u32[]{:S(2)}, u32[]{:S(2)}) collective-permute-start(bf16[144,256]{1,0:T(8,128)(2,1)S(1)} %get-tuple-element.28), channel_id=1, source_target_pairs={{4,0},{5,1},{6,2},{7,3},{8,4},{9,5},{10,6},{11,7},{12,8},{13,9},{1... | collective-permute-start | bytes 221192 | tf_op jit(solution)/shard_map/ppermute | solution.py:318
  36.1 7.4 %collective-permute-start.7 = (bf16[128,256]{1,0:T(8,128)(2,1)S(1)}, bf16[128,256]{1,0:T(8,128)(2,1)S(1)}, u32[]{:S(2)}, u32[]{:S(2)}) collective-permute-start(bf16[128,256]{1,0:T(8,128)(2,1)S(1)} %get-tuple-element.37), channel_id=1, source_target_pairs={{0,4},{1,5},{2,6},{3,7},{4,8},{5,9},{6,10},{7,11},{8,12},{9,13},{1... | collective-permute-start | bytes 196616 | tf_op jit(solution)/shard_map/ppermute | solution.py:318
  41.5 22.4 %copy-start.2 = (f32[8,8,64,64]{3,2,1,0:T(8,128)S(1)}, f32[8,8,64,64]{3,2,1,0:T(8,128)}, u32[]{:S(2)}) copy-start(f32[8,8,64,64]{3,2,1,0:T(8,128)} %coupling_ref.1) | copy-start | bytes 3145732
  41.5 22.4 %copy-start.4 = (f32[8,256,64]{1,2,0:T(8,128)S(1)}, f32[8,256,64]{1,2,0:T(8,128)}, u32[]{:S(2)}) copy-start(f32[8,256,64]{1,2,0:T(8,128)} %param.11) | copy-start | bytes 1572868
  41.5 22.4 %copy-start.7 = (bf16[2048,32]{0,1:T(8,128)(2,1)S(1)}, bf16[2048,32]{0,1:T(8,128)(2,1)}, u32[]{:S(2)}) copy-start(bf16[2048,32]{0,1:T(8,128)(2,1)} %param.10) | copy-start | bytes 393220
  41.5 22.4 %copy-start.8 = (f32[4,8,64,64]{3,2,1,0:T(8,128)S(1)}, f32[4,8,64,64]{3,2,1,0:T(8,128)}, u32[]{:S(2)}) copy-start(f32[4,8,64,64]{3,2,1,0:T(8,128)} %up_ref.1) | copy-start | bytes 1572868
  41.6 22.4 %copy-start.10 = (f32[8,64,64]{2,1,0:T(8,128)S(1)}, f32[8,64,64]{2,1,0:T(8,128)}, u32[]{:S(2)}) copy-start(f32[8,64,64]{2,1,0:T(8,128)} %transfer_ref.3) | copy-start | bytes 393220
  41.6 22.4 %copy-start.13 = (s32[8,8]{1,0:T(8,128)S(1)}, s32[8,8]{1,0:T(8,128)}, u32[]{:S(2)}) copy-start(s32[8,8]{1,0:T(8,128)} %far_leaf_ref.1) | copy-start | bytes 772
  41.6 22.4 %copy-start.14 = (s32[4,8]{1,0:T(4,128)S(1)}, s32[4,8]{1,0:T(4,128)}, u32[]{:S(2)}) copy-start(s32[4,8]{1,0:T(4,128)} %far_up_ref.1) | copy-start | bytes 388
  43.3 10.2 %collective-permute-start.11 = (f32[64,1280]{1,0:T(8,128)S(1)}, f32[64,1280]{1,0:T(8,128)S(1)}, u32[]{:S(2)}, u32[]{:S(2)}) collective-permute-start(f32[64,1280]{1,0:T(8,128)S(1)} %get-tuple-element.46), channel_id=1, source_target_pairs={{0,1},{1,0},{2,3},{3,2},{4,5},{5,4},{6,7},{7,6},{8,9},{9,8},{10,11... | collective-permute-start | bytes 983048 | tf_op jit(solution)/shard_map/ppermute | solution.py:309
  43.4 9.4 %collective-permute-start.2 = (bf16[4,6,32,128]{3,2,1,0:T(8,128)(2,1)S(1)}, bf16[4,6,32,128]{3,2,1,0:T(8,128)(2,1)S(1)}, u32[]{:S(2)}, u32[]{:S(2)}) collective-permute-start(bf16[4,6,32,128]{3,2,1,0:T(8,128)(2,1)S(1)} %pad_maximum_fusion.2), channel_id=1, source_target_pairs={{0,16},{4,20},{8,24},{12,28},{16,0},{20,4},{24,8},{28,12},{1,17},{... | collective-permute-start | bytes 589832 | tf_op jit(solution)/shard_map/ppermute | solution.py:341
  44.1 8.7 %collective-permute-start.8 = (f32[64,1024]{1,0:T(8,128)S(1)}, f32[64,1024]{1,0:T(8,128)S(1)}, u32[]{:S(2)}, u32[]{:S(2)}) collective-permute-start(f32[64,1024]{1,0:T(8,128)S(1)} %get-tuple-element.39), channel_id=1, source_target_pairs={{0,1},{1,0},{2,3},{3,2},{4,5},{5,4},{6,7},{7,6},{8,9},{9,8},{10,11... | collective-permute-start | bytes 786440 | tf_op jit(solution)/shard_map/ppermute | solution.py:309
  52.9 16.4 %collective-permute-start.9 = (bf16[32,1024]{1,0:T(8,128)(2,1)S(1)}, bf16[32,1024]{1,0:T(8,128)(2,1)S(1)}, u32[]{:S(2)}, u32[]{:S(2)}) collective-permute-start(bf16[32,1024]{1,0:T(8,128)(2,1)S(1)} %get-tuple-element.41), channel_id=1, source_target_pairs={{0,2},{1,3},{2,0},{3,1},{4,6},{5,7},{6,4},{7,5},{8,10},{9,11},{10,... | collective-permute-start | bytes 196616 | tf_op jit(solution)/shard_map/ppermute | solution.py:309
  53.5 15.8 %collective-permute-start.12 = (bf16[32,1024]{1,0:T(8,128)(2,1)S(1)}, bf16[32,1024]{1,0:T(8,128)(2,1)S(1)}, u32[]{:S(2)}, u32[]{:S(2)}) collective-permute-start(bf16[32,1024]{1,0:T(8,128)(2,1)S(1)} %get-tuple-element.48), channel_id=1, source_target_pairs={{0,2},{1,3},{2,0},{3,1},{4,6},{5,7},{6,4},{7,5},{8,10},{9,11},{10,... | collective-permute-start | bytes 196616 | tf_op jit(solution)/shard_map/ppermute | solution.py:309
  55.1 14.2 %collective-permute-start.13 = (bf16[32,512]{1,0:T(8,128)(2,1)S(1)}, bf16[32,512]{1,0:T(8,128)(2,1)S(1)}, u32[]{:S(2)}, u32[]{:S(2)}) collective-permute-start(bf16[32,512]{1,0:T(8,128)(2,1)S(1)} %get-tuple-element.49), channel_id=1, source_target_pairs={{4,0},{5,1},{6,2},{7,3},{8,4},{9,5},{10,6},{11,7},{12,8},{13,9},{1... | collective-permute-start | bytes 98312 | tf_op jit(solution)/shard_map/ppermute | solution.py:318
  58.3 11.1 %collective-permute-start.14 = (bf16[32,512]{1,0:T(8,128)(2,1)S(1)}, bf16[32,512]{1,0:T(8,128)(2,1)S(1)}, u32[]{:S(2)}, u32[]{:S(2)}) collective-permute-start(bf16[32,512]{1,0:T(8,128)(2,1)S(1)} %get-tuple-element.50), channel_id=1, source_target_pairs={{4,2},{5,3},{6,0},{7,1},{8,6},{9,7},{10,4},{11,5},{12,10},{13,11},... | collective-permute-start | bytes 98312 | tf_op jit(solution)/shard_map/ppermute | solution.py:318
  (6 other events, 6.4 us)

commit v3 on v2

v3 whole, which is shorter than its diff:
```python
import functools
import math

import jax
import jax.numpy as jnp
from jax import lax
from jax.experimental import pallas as pl
from jax.experimental.pallas import tpu as pltpu
from jax.sharding import PartitionSpec as P

RIDGE = 0.5
LOG2E = math.log2(math.e)
FLAG_ROWS = 16
CORE_PARTS = 3
PACK_LIMIT = 58
F32 = jnp.float32
BF16 = jnp.bfloat16
NN = (((1,), (0,)), ((), ()))
NT = (((1,), (1,)), ((), ()))
VMEM = pl.BlockSpec(memory_space=pltpu.VMEM)
SMEM = pl.BlockSpec(memory_space=pltpu.SMEM)
HBM = pl.BlockSpec(memory_space=pltpu.HBM)
ANY = pl.BlockSpec(memory_space=pl.ANY)
MIB = 1 << 20
WEIGHTS = {"own_low": 5, "high_tiles": 10, "far_field": 3, "split_back": 5, "finish": 0.1, "pack": 2, "stack": 1}


def dot(a, b, dims):
    return lax.dot_general(a, b, dims, preferred_element_type=F32)


def halves(x):
    high = x.astype(BF16)
    return high, (x - high.astype(F32)).astype(BF16)


def split_dot(a, b, dims):
    a_high, a_low = halves(a)
    b_high, b_low = halves(b)
    return dot(a_high, b_high, dims) + (dot(a_high, b_low, dims) + dot(a_low, b_high, dims))


def half_split_dot(a, b, dims):
    b_high, b_low = halves(b)
    return dot(a, b_high, dims) + dot(a, b_low, dims)


def span(index, size):
    return pl.ds(pl.multiple_of(index * size, size), size)


def listed(table_ref, row, leaf):
    found = table_ref[row + 1, 0] == leaf
    for k in range(1, table_ref.shape[1]):
        found = found | (table_ref[row + 1, k] == leaf)
    return found


def pack_kernel(
    v_in_ref, bases_in_ref, transfer_in_ref, msg_ref, v_ref, bases_ref, transfer_ref, sems
):
    copies = [
        pltpu.make_async_copy(source, target, sems.at[i])
        for i, (source, target) in enumerate(
            (
                (v_in_ref, v_ref), (bases_in_ref, bases_ref), (transfer_in_ref, transfer_ref)
            )
        )
    ]
    for copy in copies:
        copy.start()
    for copy in copies:
        copy.wait()
    leaves, _, pts = bases_ref.shape
    coeffs = []
    lifted = []
    for leaf in range(leaves):
        v = v_ref[:, leaf * pts : (leaf + 1) * pts]
        coeffs.append(half_split_dot(v, bases_ref[leaf], NT))
        lifted.append(split_dot(coeffs[-1], transfer_ref[leaf], NN))
    parents = [lifted[2 * q] + lifted[2 * q + 1] for q in range(leaves // 2)]
    entries = coeffs + parents
    for e in range(len(entries) // 2):
        msg_ref[e] = jnp.concatenate(entries[2 * e : 2 * e + 2], axis=1).astype(BF16)


def join_kernel(mine_ref, came_ref, after_ref, out_ref):
    count = mine_ref.shape[0]
    out_ref[:count] = mine_ref[...]
    out_ref[count:] = came_ref[...]


def assemble_kernel(leaves, sc_ref, x_ref, even_ref, odd_ref, v_ref, down_ref, up_ref):
    features, pts = x_ref.shape
    rows = v_ref.shape[0]
    v_ref[: rows // 2] = even_ref[...]
    v_ref[rows // 2 :] = odd_ref[...]
    low, upper, base = sc_ref[0, 0], sc_ref[0, 2], sc_ref[0, 3]

    def flags(leaf, first):
        found = [
            jnp.full((1, pts), listed(sc_ref, leaf, first + a).astype(F32))
            for a in range(leaves)
        ]
        found.append(jnp.zeros((FLAG_ROWS - leaves, pts), F32))
        return jnp.concatenate(found, axis=0).astype(BF16)

    down_ref[:rows] = v_ref[:, span(low, pts)]
    down_ref[rows:] = flags(low, base - leaves)
    up_ref[:features] = x_ref[...]
    up_ref[features : features + rows] = v_ref[:, span(upper, pts)]
    up_ref[features + rows :] = flags(upper, base + leaves)


def stack_kernel(*refs):
    out_ref = refs[-1]
    first = 0
    for ref in refs[:-1]:
        out_ref[first : first + ref.shape[0]] = ref[...]
        first += ref.shape[0]


def row_sums(x, features):
    return jnp.sum(jnp.square(x.astype(F32)), axis=0, keepdims=True) * (LOG2E / features)


def tiles(x_b, x, col, row, features):
    cross = dot(x_b, x, NN) * (2.0 * LOG2E / features)
    return jnp.exp2(cross - (col + row)).astype(BF16)


def column_sums(x_b, features):
    return jnp.sum(jnp.square(x_b.astype(F32)), axis=1, keepdims=True) * (LOG2E / features)


def mask_row(flags, pts):
    return jnp.concatenate([jnp.full((1, pts), f.astype(F32)) for f in flags], axis=1)


def own_low_kernel(
    leaves, sc_ref, x_ref, v_ref, halo_ref, near_ref, unused_ref, *refs
):
    out_refs, sums_ref, back_ref = refs[:4], refs[4], refs[5]
    features, points = x_ref.shape
    pts = points // leaves
    rows = v_ref.shape[0]
    half = leaves // 2
    low, high, base = sc_ref[0, 0], sc_ref[0, 1], sc_ref[0, 3]
    for leaf in range(leaves):
        here = slice(leaf * pts, (leaf + 1) * pts)
        sums_ref[:, here] = jnp.broadcast_to(
            row_sums(x_ref[:, here], features), (sums_ref.shape[0], pts)
        )
    updates = [None, None]
    back = None
    x_bs = [x_ref[:, span(b, pts)].T for b in (high, low)] + [halo_ref[...].T]
    cols = [column_sums(x_b, features) for x_b in x_bs]
    for group in (1, 0):
        here = slice(group * half * pts, (group + 1) * half * pts)
        leaf_ids = [group * half + i for i in range(half)]
        row = sums_ref[0:1, here]

        tile = tiles(x_bs[2], x_ref[:, here], cols[2], row, features)
        to_a = [(a >= low) & listed(sc_ref, a, base + leaves + low) for a in leaf_ids]
        total = dot(near_ref[:rows], tile, NN) * mask_row(to_a, pts)
        to_b = jnp.concatenate([near_ref[rows + a : rows + a + 1, :] for a in leaf_ids], axis=1)
        to_b = to_b * mask_row([a >= low for a in leaf_ids], pts).astype(BF16)
        term = dot(v_ref[:, here] * to_b, tile, NT)
        back = term if back is None else back + term

        for which, b in enumerate((high, low)[: 2 - group]):
            tile = tiles(x_bs[which], x_ref[:, here], cols[which], row, features)
            to_a = [(a <= b) & listed(sc_ref, a, base + b) for a in leaf_ids]
            to_b = [(a < b) & listed(sc_ref, b, base + a) for a in leaf_ids]
            total = total + dot(v_ref[:, span(b, pts)], tile, NN) * mask_row(to_a, pts)
            masked = v_ref[:, here] * mask_row(to_b, pts).astype(BF16)
            term = dot(masked, tile, NT)
            updates[which] = term if updates[which] is None else updates[which] + term
        out_refs[2 * group][...] = total[: rows // 2]
        out_refs[2 * group + 1][...] = total[rows // 2 :]
    back_ref[...] = back.astype(back_ref.dtype)
    for b, term, group in ((high, updates[0], 1), (low, updates[1], 0)):
        place = span(b - group * half, pts)
        out_refs[2 * group][:, place] += term[: rows // 2]
        out_refs[2 * group + 1][:, place] += term[rows // 2 :]


def high_kernel(leaves, sc_ref, x_ref, halo_ref, sums_ref, v_ref, came_ref, unused_ref, *refs):
    ins, keep_ref, sends = refs[:4], refs[4], refs[5:]
    features, points = x_ref.shape
    pts = points // leaves
    rows = v_ref.shape[0]
    half = leaves // 2
    b, base = sc_ref[0, 2], sc_ref[0, 3]
    x_b = halo_ref[:features].T
    col = column_sums(x_b, features)
    here = slice(half * pts, leaves * pts)
    leaf_ids = [half + i for i in range(half)]
    tile = tiles(x_b, x_ref[:, here], col, sums_ref[0:1, here], features)
    to_a = [(a <= b) & listed(sc_ref, a, base - leaves + b) for a in leaf_ids]
    term = dot(halo_ref[features : features + rows], tile, NN) * mask_row(to_a, pts)
    first = features + rows
    to_b = jnp.concatenate([halo_ref[first + a : first + a + 1, :] for a in leaf_ids], axis=1)
    to_b = to_b * mask_row([a <= b for a in leaf_ids], pts).astype(BF16)
    back = dot(v_ref[:, here] * to_b, tile, NT)
    mine = mask_row([b - half == i for i in range(half)], pts)
    came = came_ref[...].astype(F32)
    parts = []
    for i in (0, 1):
        block = slice(i * rows // 2, (i + 1) * rows // 2)
        first = ins[i][...] + jnp.concatenate([came[block]] * half, axis=1) * mine
        parts.append(
            jnp.concatenate([first, ins[2 + i][...] + term[block], back[block]], axis=1)
        )
    keep_ref[...] = parts[0]
    size = sends[0].shape[1]
    for i, ref in enumerate(sends):
        ref[...] = parts[1][:, i * size : (i + 1) * size]


def split_kernel(keep_ref, unused_ref, *refs):
    came = jnp.concatenate([ref[...] for ref in refs[:CORE_PARTS]], axis=1)
    out_ref, refs = refs[CORE_PARTS], refs[CORE_PARTS + 1 :]
    cols, wide = out_ref.shape
    blocks = keep_ref.shape[0] // cols
    pts = keep_ref.shape[1] - wide
    for m in range(blocks):
        block = slice(m * cols, (m + 1) * cols)
        total = keep_ref[block, :wide] + came[block, :wide]
        if m == 0:
            out_ref[...] = total
        else:
            refs[m - 1][...] = total.astype(BF16)
        refs[blocks - 1 + m][:, :pts] = keep_ref[block, wide:].astype(BF16)
        refs[blocks - 1 + m][:, pts:] = came[block, wide:].astype(BF16)


def far_kernel(
    sc_ref, far_leaf_ref, far_up_ref, mine_ref, came_ref, coupling_ref, up_ref, transfer_ref,
    bases_ref, v_ref, out_ref, all_ref
):
    leaves, rank, pts = bases_ref.shape
    device = sc_ref[0, 4]
    count = mine_ref.shape[0]
    all_ref[:count] = mine_ref[...]
    all_ref[count:] = came_ref[...]

    lanes = lax.broadcasted_iota(jnp.int32, mine_ref.shape[2:], 1)

    def entry(index, per_device, first, right):
        owner = lax.div(index, per_device)
        place = lax.rem(index, per_device)
        other = owner ^ device
        at = lax.div(other, 2) + lax.rem(other, 2) * count
        pair = all_ref[at, first + lax.div(place, 2)].astype(F32)
        return jnp.where(lax.rem(place, 2) == right, pair, pltpu.roll(pair, rank, 1))

    def field(list_ref, row, matrix_ref, per_device, first):
        lhs, highs, lows = [], [], []
        for k in range(0, list_ref.shape[1], 2):
            left = entry(list_ref[row, k], per_device, first, 0)
            right = entry(list_ref[row, k + 1], per_device, first, 1)
            lhs.append(jnp.where(lanes < rank, left, right).astype(BF16))
            wide = jnp.concatenate([matrix_ref[row, k], matrix_ref[row, k + 1]], axis=1)
            high, low = halves(wide)
            highs.append(high)
            lows.append(low)
        rhs = jnp.concatenate(
            [jnp.concatenate(highs, axis=1), jnp.concatenate(lows, axis=1)], axis=0
        )
        total = dot(jnp.concatenate(lhs, axis=1), rhs, NT)
        return total[:, :rank] + total[:, rank:]

    def stacked_dot(a, b, dims):
        both = jnp.concatenate(halves(a), axis=0)
        high, low = halves(b)
        total = dot(both, high, dims)
        rows = a.shape[0]
        return total[:rows] + total[rows:] + dot(both[:rows], low, dims)

    for parent in range(leaves // 2):
        upper = field(far_up_ref, parent, up_ref, leaves // 2, leaves // 2)
        for leaf in (2 * parent, 2 * parent + 1):
            total = field(far_leaf_ref, leaf, coupling_ref, leaves, 0)
            total = total + stacked_dot(upper, transfer_ref[leaf], NT)
            here = slice(leaf * pts, (leaf + 1) * pts)
            far = stacked_dot(total, bases_ref[leaf], NN)
            out_ref[:, here] = far + RIDGE * v_ref[:, here].astype(F32)


def finish_kernel(blocks, sc_ref, far_ref, *refs):
    out_ref = refs[-1]
    total = far_ref[...]
    for ref in refs[:blocks]:
        total = total + ref[...].astype(F32)
    out_ref[...] = total
    back_refs = refs[blocks : 2 * blocks]
    pts = back_refs[0].shape[1] // 2
    column = sc_ref[0, 0]
    for m in range(blocks):
        for core in (0, 1):
            place = span((column ^ (2 * m + core)) + out_ref.shape[1] // pts // 2, pts)
            out_ref[:, place] += back_refs[m][:, core * pts : (core + 1) * pts].astype(F32)


def call(body, out_shape, in_specs, args, name, flops=0, bytes_accessed=0, scratch=(), limit=32):
    flops, bytes_accessed = int(WEIGHTS.get(name, 0) * 1.15e9), 0
    return pl.pallas_call(
        body,
        out_shape=out_shape,
        in_specs=in_specs,
        out_specs=jax.tree.map(lambda _: VMEM, out_shape),
        scratch_shapes=list(scratch),
        compiler_params=pltpu.CompilerParams(vmem_limit_bytes=limit * MIB),
        cost_estimate=pl.CostEstimate(
            flops=flops, bytes_accessed=bytes_accessed, transcendentals=0
        ),
        name=name,
    )(*args)


def local(
    points, vectors, bases, leaf_coupling, transfer, up_coupling, far_leaf, far_up, near_lists
):
    leaves, pts, rank = bases.shape
    features = points.shape[1]
    cols = vectors.shape[1]
    half = leaves // 2
    shape = jax.ShapeDtypeStruct
    leaf_devices = lax.axis_size("leaf")
    rhs_devices = lax.axis_size("rhs")
    assert leaves == 2 * rhs_devices and leaves <= FLAG_ROWS
    rows = cols * rhs_devices
    wide = half * pts
    device = lax.axis_index("leaf")
    column = lax.axis_index("rhs")
    low, high, upper = column, leaves - 1 - column, half + column
    slots = near_lists.shape[1]
    scalars = jnp.stack([low, high, upper, device * leaves, device]).astype(jnp.int32)
    scalars = jnp.pad(scalars, (0, slots - scalars.shape[0]))
    scalars = jnp.concatenate([scalars[None], near_lists], axis=0)

    def over_rhs(array, mask):
        return lax.ppermute(array, "rhs", [(i, i ^ mask) for i in range(rhs_devices)])

    def over_leaf(array, step, mask=0):
        pairs = [
            (i * rhs_devices + j, (i + step) * rhs_devices + (j ^ mask))
            for i in range(leaf_devices)
            if 0 <= i + step < leaf_devices
            for j in range(rhs_devices)
        ]
        return lax.ppermute(array, ("leaf", "rhs"), pairs)

    x = points.T
    v = vectors.T
    bases_t = jnp.swapaxes(bases, 1, 2)

    chunk_low = lax.dynamic_slice_in_dim(x, low * pts, pts, 1)
    chunk_up = lax.dynamic_slice_in_dim(x, upper * pts, pts, 1)
    halo_low = over_leaf(chunk_low, -1)
    others = [over_rhs(v, m) for m in range(2, rhs_devices, 2)]

    message, v_here = call(
        pack_kernel,
        (
            shape((half + half // 2, cols, 2 * rank), BF16),
            shape(v.shape, BF16),
        ),
        [HBM] * 3,
        (v, bases_t, transfer),
        "pack",
        scratch=[
            pltpu.VMEM(bases_t.shape, F32),
            pltpu.VMEM(transfer.shape, F32),
            pltpu.SemaphoreType.DMA((3,)),
        ],
        limit=PACK_LIMIT,
    )
    even_v = call(
        stack_kernel,
        shape((rows // 2, leaves * pts), BF16),
        [VMEM] * (1 + len(others)),
        (v_here, *others),
        "stack",
    )
    odd_v = over_rhs(even_v, 1)
    all_v, down, up = call(
        functools.partial(assemble_kernel, leaves),
        (
            shape((rows, leaves * pts), BF16),
            shape((rows + FLAG_ROWS, pts), BF16),
            shape((features + rows + FLAG_ROWS, pts), BF16),
        ),
        [SMEM] + [VMEM] * 3,
        (scalars, chunk_up, even_v, odd_v),
        "assemble",
    )

    near_low = over_leaf(down, -1)
    halo_high = over_leaf(up, 1)

    everything = message[None]
    stages = [message]
    bit = 1
    while bit < leaf_devices:
        mask = 2 * bit if 2 * bit < leaf_devices else 1
        arrived = lax.ppermute(everything, "leaf", [(i, i ^ mask) for i in range(leaf_devices)])
        stages.append(arrived)
        if 2 * bit == leaf_devices:
            break
        everything = call(
            join_kernel,
            shape((2 * bit,) + message.shape, BF16),
            [VMEM] * 2 + [ANY],
            (everything, arrived, up if bit == 1 else message),
            "join",
        )
        bit *= 2


    part = shape((rows // 2, wide), F32)
    *totals, sums, back_low = call(
        functools.partial(own_low_kernel, leaves),
        (part,) * 4 + (shape((8, leaves * pts), F32), shape((rows, pts), BF16)),
        [SMEM] + [VMEM] * 4 + [ANY],
        (scalars, x, all_v, halo_low, near_low, stages[1]),
        "own_low",
        5 * 10**9,
        0,
    )
    far = call(
        far_kernel,
        shape((cols, leaves * pts), F32),
        [SMEM] * 3 + [VMEM] * 7,
        (
            scalars, far_leaf, far_up, everything, arrived, leaf_coupling, up_coupling, transfer, bases_t,
            v,
        ),
        "far_field",
        10**9,
        6 * MIB,
        scratch=[pltpu.VMEM((leaf_devices,) + message.shape, BF16)],
    )
    came_low = over_leaf(back_low, 1)
    blocks = rhs_devices // 2
    full = (leaves + 1) * pts
    keep, *sends = call(
        functools.partial(high_kernel, leaves),
        (shape((rows // 2, full), F32),)
        + (shape((rows // 2, full // CORE_PARTS), F32),) * CORE_PARTS,
        [SMEM] + [VMEM] * 5 + [ANY] + [VMEM] * 4,
        (
            scalars, x, halo_high, sums, all_v, came_low, message,
            *totals,
        ),
        "high_tiles",
    )
    came = [over_rhs(part, 1) for part in sends]
    first, *others = call(
        split_kernel,
        (shape((cols, leaves * pts), F32),)
        + (shape((cols, leaves * pts), BF16),) * (blocks - 1)
        + (shape((cols, 2 * pts), BF16),) * blocks,
        [VMEM, ANY] + [VMEM] * CORE_PARTS,
        (keep, stages[3], *came),
        "split_back",
    )
    backs = [over_leaf(block, -1, 2 * m) for m, block in enumerate(others[blocks - 1 :])]
    parts = [first] + [
        over_rhs(block, 2 * m + 2) for m, block in enumerate(others[: blocks - 1])
    ]
    out = call(
        functools.partial(finish_kernel, blocks),
        shape((cols, leaves * pts), F32),
        [SMEM] + [VMEM] * (1 + 2 * blocks),
        (scalars, far, *parts, *backs),
        "finish",
        0,
        2 * MIB,
    )
    return out.T


def solution(mesh):
    return jax.shard_map(
        local,
        mesh=mesh,
        in_specs=(
            P("leaf", None),
            P("leaf", "rhs"),
            P("leaf", None, None),
            P("leaf", None, None, None),
            P("leaf", None, None),
            P("leaf", None, None, None),
            P("leaf", None),
            P("leaf", None),
            P("leaf", None),
        ),
        out_specs=P("leaf", "rhs"),
        check_vma=False,
    )
```

time: 71.1 us -> 54.6 us (0.77)
  the two profiles are of different devices: /device:TPU:10 before, /device:TPU:24 now
where the time goes in v3:
time: 54.6 us; the launch traced here: 54.3 us
  starting transfers between devices  30.3 us (55%)
  Pallas kernels  16.4 us (30%)
  local copies, waits for them, and re-layouts  4.12 us (8%)
  waiting for transfers between devices  3.21 us (6%)
    ppermute x6, starting transfers between devices, over_leaf(): return lax.ppermute(array, ('leaf', 'rhs'), pairs)  19.7 us
    pallas_call x10, Pallas kernels, call(): pl.pallas_call(body, out_shape=out_shape, in_specs=in_specs, out_specs=ja...  16.4 us
    ppermute x3, starting transfers between devices, local(): lax.ppermute(everything, 'leaf', [(i, i ^ mask) for i in range(leaf_devic...  6.82 us
    ppermute x6, starting transfers between devices, over_rhs(): lax.ppermute(array, 'rhs', [(i, i ^ mask) for i in range(rhs_devices)])  3.82 us
    unnamed x24, local copies, waits for them, and re-layouts  2.85 us
    ppermute x6, waiting for transfers between devices, over_rhs(): lax.ppermute(array, 'rhs', [(i, i ^ mask) for i in range(rhs_devices)])  1.76 us
    ppermute x3, waiting for transfers between devices, local(): lax.ppermute(everything, 'leaf', [(i, i ^ mask) for i in range(leaf_devic...  1.42 us
    dynamic_slice x1, local copies, waits for them, and re-layouts, local(): chunk_low = lax.dynamic_slice_in_dim(x, low * pts, pts, 1)  1.18 us
  transfers between devices with their start and end apart: 15, of which 5 were waited for; matrix products, arithmetic and copies ran while one was open for 2% of the time, Pallas kernels for 27%

profile of v3, /device:TPU:24, one launch (start us, length us, event | category | flops | bytes accessed | tf_op | source)
XLA Modules:
  0.0 54.3 jit_solution(8081386134629403813)
XLA Ops:
  0.0 1.5 %collective-permute-start.1 = (bf16[32,2048]{1,0:T(8,128)(2,1)}, bf16[32,2048]{1,0:T(8,128)(2,1)S(1)}, u32[]{:S(2)}, u32[]{:S(2)}) collective-permute-start(bf16[32,2048]{1,0:T(8,128)(2,1)} %bitcast.22), channel_id=1, source_target_pairs={{0,2},{1,3},{2,0},{3,1},{4,6},{5,7},{6,4},{7,5},{8,10},{9,11},{10,... | collective-permute-start | bytes 393224 | tf_op jit(solution)/shard_map/ppermute | solution.py:344
  1.5 1.2 %dynamic-slice_bitcast_fusion = (bf16[784,256]{1,0:T(8,128)(2,1)S(1)}, bf16[784,256]{1,0:T(8,128)(2,1)S(1)}) fusion(bf16[2048,784]{0,1:T(8,128)(2,1)} %param.9, s32[]{:T(128)S(6)} %select_n.7, s32[]{:T(128)S(6)} %select_n.6), kind=kLoop, calls=%fused_computation | loop fusion | bytes 1605640 | tf_op jit(solution)/shard_map/dynamic_slice | solution.py:359
  2.7 3.3 %collective-permute-start.6 = (bf16[784,256]{1,0:T(8,128)(2,1)S(1)}, bf16[784,256]{1,0:T(8,128)(2,1)S(1)}, u32[]{:S(2)}, u32[]{:S(2)}) collective-permute-start(bf16[784,256]{1,0:T(8,128)(2,1)S(1)} %get-tuple-element.43), channel_id=1, source_target_pairs={{4,0},{5,1},{6,2},{7,3},{8,4},{9,5},{10,6},{11,7},{12,8},{13,9},{1... | collective-permute-start | bytes 1204232 | tf_op jit(solution)/shard_map/ppermute | solution.py:353
  6.0 3.1 %pack.1 = (bf16[6,32,128]{2,1,0:T(8,128)(2,1)}, bf16[32,2048]{1,0:T(8,128)(2,1)}) custom-call(bf16[32,2048]{1,0:T(8,128)(2,1)} %bitcast.23, f32[8,64,256]{2,1,0:T(8,128)} %bitcast.20, f32[8,64,64]{2,1,0:T(8,128)} %transfer_ref.1), custom_call_target="tpu_custom_call" | custom-call | flops 2300000000 | tf_op jit(solution)/shard_map/pack/pallas_call | solution.py:308
  9.1 0.9 %copy-done.10 = bf16[32,2048]{1,0:T(8,128)(2,1)S(1)} copy-done((bf16[32,2048]{1,0:T(8,128)(2,1)S(1)}, bf16[32,2048]{1,0:T(8,128)(2,1)}, u32[]{:S(2)}) %copy-start.10) | copy-done | bytes 131096
  10.2 1.4 %collective-permute-done.2.odd_ref = bf16[64,2048]{1,0:T(8,128)(2,1)S(1)} collective-permute-done((bf16[64,2048]{1,0:T(8,128)(2,1)S(1)}, bf16[64,2048]{1,0:T(8,128)(2,1)S(1)}, u32[]{:S(2)}, u32[]{:S(2)}) %collective-permute-start.2) | collective-permute-done | bytes 262176 | tf_op jit(solution)/shard_map/ppermute | solution.py:344
  11.7 0.8 %assemble.1 = (bf16[128,2048]{1,0:T(8,128)(2,1)S(1)}, bf16[144,256]{1,0:T(8,128)(2,1)S(1)}, bf16[928,256]{1,0:T(8,128)(2,1)S(1)}) custom-call(s32[9,8]{1,0:T(8,128)S(1)} %pad_add_fusion.sc_ref, bf16[784,256]{1,0:T(8,128)(2,1)S(1)} %get-tuple-element.44.x_ref, bf16[64,2048]{1,0:T(8,128)(2,1)S(1)} %stack.25.even_ref, ...), custom_call_target="tpu_custom_call" | custom-call | tf_op jit(solution)/shard_map/assemble/pallas_call | solution.py:308
  12.4 2.4 %collective-permute-start.7 = (bf16[144,256]{1,0:T(8,128)(2,1)S(1)}, bf16[144,256]{1,0:T(8,128)(2,1)S(1)}, u32[]{:S(2)}, u32[]{:S(2)}) collective-permute-start(bf16[144,256]{1,0:T(8,128)(2,1)S(1)} %get-tuple-element.28), channel_id=1, source_target_pairs={{4,0},{5,1},{6,2},{7,3},{8,4},{9,5},{10,6},{11,7},{12,8},{13,9},{1... | collective-permute-start | bytes 221192 | tf_op jit(solution)/shard_map/ppermute | solution.py:353
  14.9 0.5 collective-permute-start
  15.4 3.4 %collective-permute-start.5 = (bf16[928,256]{1,0:T(8,128)(2,1)S(1)}, bf16[928,256]{1,0:T(8,128)(2,1)S(1)}, u32[]{:S(2)}, u32[]{:S(2)}) collective-permute-start(bf16[928,256]{1,0:T(8,128)(2,1)S(1)} %get-tuple-element.26.after_ref), channel_id=1, source_target_pairs={{0,4},{1,5},{2,6},{3,7},{4,8},{5,9},{6,10},{7,11},{8,12},{9,13},{1... | collective-permute-start | bytes 1425416 | tf_op jit(solution)/shard_map/ppermute | solution.py:353
  18.8 0.2 collective-permute-done.came_ref.unused_ref
  19.1 0.4 collective-permute-start.3
  19.5 1.9 %copy-done = bf16[2048,784]{0,1:T(8,128)(2,1)S(1)} copy-done((bf16[2048,784]{0,1:T(8,128)(2,1)S(1)}, bf16[2048,784]{0,1:T(8,128)(2,1)}, u32[]{:S(2)}) %copy-start) | copy-done | bytes 3211288
  21.4 5.4 %own_low.1 = (f32[64,1024]{1,0:T(8,128)S(1)}, f32[64,1024]{1,0:T(8,128)S(1)}, f32[64,1024]{1,0:T(8,128)S(1)}, f32[64,1024]{1,0:T(8,128)S(1)}, f32[8,2048]{1,0:T(8,128)S(1)}, /*index=5*/bf16[128,256]{1,0:T(8,128)(2,1)S(1)}) custom-call(s32[9,8]{1,0:T(8,128)S(1)} %pad_add_fusion.sc_ref, bf16[784,2048]{1,0:T(8,128)(2,1)S(1)} %bitcast.16, ...), custom_call_target="tpu_custom_call" | custom-call | flops 5750000128 | tf_op jit(solution)/shard_map/own_low/pallas_call | solution.py:308
  26.8 4.3 %collective-permute-start.8 = (bf16[128,256]{1,0:T(8,128)(2,1)S(1)}, bf16[128,256]{1,0:T(8,128)(2,1)S(1)}, u32[]{:S(2)}, u32[]{:S(2)}) collective-permute-start(bf16[128,256]{1,0:T(8,128)(2,1)S(1)} %get-tuple-element.30), channel_id=1, source_target_pairs={{0,4},{1,5},{2,6},{3,7},{4,8},{5,9},{6,10},{7,11},{8,12},{9,13},{1... | collective-permute-start | bytes 196616 | tf_op jit(solution)/shard_map/ppermute | solution.py:353
  31.2 5.9 %collective-permute-start.4 = (bf16[4,6,32,128]{3,2,1,0:T(8,128)(2,1)S(1)}, bf16[4,6,32,128]{3,2,1,0:T(8,128)(2,1)S(1)}, u32[]{:S(2)}, u32[]{:S(2)}) collective-permute-start(bf16[4,6,32,128]{3,2,1,0:T(8,128)(2,1)S(1)} %join.3.mine_ref), channel_id=1, source_target_pairs={{0,4},{4,0},{8,12},{12,8},{16,20},{20,16},{24,28},{28,24},{1,5},{5... | collective-permute-start | bytes 589832 | tf_op jit(solution)/shard_map/ppermute | solution.py:408
  37.1 1.8 %high_tiles.1 = (f32[64,2304]{1,0:T(8,128)S(1)}, f32[64,768]{1,0:T(8,128)S(1)}, f32[64,768]{1,0:T(8,128)S(1)}, f32[64,768]{1,0:T(8,128)S(1)}) custom-call(s32[9,8]{1,0:T(8,128)S(1)} %pad_add_fusion.sc_ref, bf16[784,2048]{1,0:T(8,128)(2,1)S(1)} %bitcast.17, bf16[928,256]{1,0:T(8,128)(2,1)S(1)} %collective-permute-done.5.halo_ref, ...), custom_call_target="tpu_custom_call" | custom-call | flops 11500000256 | tf_op jit(solution)/shard_map/high_tiles/pallas_call | solution.py:308
  39.0 0.5 collective-permute-start.10
  39.6 1.2 %collective-permute-done.4.came_ref.unused_ref = bf16[4,6,32,128]{3,2,1,0:T(8,128)(2,1)S(1)} collective-permute-done((bf16[4,6,32,128]{3,2,1,0:T(8,128)(2,1)S(1)}, bf16[4,6,32,128]{3,2,1,0:T(8,128)(2,1)S(1)}, u32[]{:S(2)}, u32[]{:S(2)}) %collective-permute-start.4) | collective-permute-done | bytes 196640 | tf_op jit(solution)/shard_map/ppermute | solution.py:408
  41.1 2.2 %collective-permute-start.13 = (bf16[32,512]{1,0:T(8,128)(2,1)S(1)}, bf16[32,512]{1,0:T(8,128)(2,1)S(1)}, u32[]{:S(2)}, u32[]{:S(2)}) collective-permute-start(bf16[32,512]{1,0:T(8,128)(2,1)S(1)} %get-tuple-element.41), channel_id=1, source_target_pairs={{4,0},{5,1},{6,2},{7,3},{8,4},{9,5},{10,6},{11,7},{12,8},{13,9},{1... | collective-permute-start | bytes 98312 | tf_op jit(solution)/shard_map/ppermute | solution.py:353
  43.3 4.0 %collective-permute-start.14 = (bf16[32,512]{1,0:T(8,128)(2,1)S(1)}, bf16[32,512]{1,0:T(8,128)(2,1)S(1)}, u32[]{:S(2)}, u32[]{:S(2)}) collective-permute-start(bf16[32,512]{1,0:T(8,128)(2,1)S(1)} %get-tuple-element.42), channel_id=1, source_target_pairs={{4,2},{5,3},{6,0},{7,1},{8,6},{9,7},{10,4},{11,5},{12,10},{13,11},... | collective-permute-start | bytes 98312 | tf_op jit(solution)/shard_map/ppermute | solution.py:353
  47.3 1.6 %collective-permute-start.12 = (bf16[32,2048]{1,0:T(8,128)(2,1)S(1)}, bf16[32,2048]{1,0:T(8,128)(2,1)S(1)}, u32[]{:S(2)}, u32[]{:S(2)}) collective-permute-start(bf16[32,2048]{1,0:T(8,128)(2,1)S(1)} %get-tuple-element.40), channel_id=1, source_target_pairs={{0,2},{1,3},{2,0},{3,1},{4,6},{5,7},{6,4},{7,5},{8,10},{9,11},{10,... | collective-permute-start | bytes 393224 | tf_op jit(solution)/shard_map/ppermute | solution.py:344
  49.0 3.7 %far_field.1.far_ref = f32[32,2048]{1,0:T(8,128)S(1)} custom-call(s32[9,8]{1,0:T(8,128)S(1)} %pad_add_fusion.sc_ref, s32[8,8]{1,0:T(8,128)S(1)} %copy-done.8, s32[4,8]{1,0:T(4,128)S(1)} %copy-done.9, bf16[4,6,32,128]{3,2,1,0:T(8,128)(2,1)S(1)} %join.3.mine_ref, bf16[4,6,32,128]{3,2,1,0:T(8,128)(2,1)S(1)} %collective-permute-done.4.came_ref.unused_ref, ...), custom_call_target="tpu_custom_call" | custom-call | flops 3449999872 | tf_op jit(solution)/shard_map/far_field/pallas_call | solution.py:308
  52.8 1.4 %finish.1 = f32[32,2048]{1,0:T(8,128)} custom-call(s32[9,8]{1,0:T(8,128)S(1)} %pad_add_fusion.sc_ref, f32[32,2048]{1,0:T(8,128)S(1)} %far_field.1.far_ref, f32[32,2048]{1,0:T(8,128)S(1)} %get-tuple-element.39.refs_0_, bf16[32,2048]{1,0:T(8,128)(2,1)S(1)} %collective-permute-done.12.refs_1_, bf16[32,512]{1,0:T(8,128)(2,1)S(1)} %collective-permute-done.13.refs_2_, ...), custom_call_target="tpu_custom_call" | custom-call | flops 115000000 | tf_op jit(solution)/shard_map/finish/pallas_call | solution.py:308
  (44 shorter events, 0.9 us)
Async XLA Ops:
  0.0 9.1 %collective-permute-start.1 = (bf16[32,2048]{1,0:T(8,128)(2,1)}, bf16[32,2048]{1,0:T(8,128)(2,1)S(1)}, u32[]{:S(2)}, u32[]{:S(2)}) collective-permute-start(bf16[32,2048]{1,0:T(8,128)(2,1)} %bitcast.22), channel_id=1, source_target_pairs={{0,2},{1,3},{2,0},{3,1},{4,6},{5,7},{6,4},{7,5},{8,10},{9,11},{10,... | collective-permute-start | bytes 393224 | tf_op jit(solution)/shard_map/ppermute | solution.py:344
  2.7 16.8 %collective-permute-start.6 = (bf16[784,256]{1,0:T(8,128)(2,1)S(1)}, bf16[784,256]{1,0:T(8,128)(2,1)S(1)}, u32[]{:S(2)}, u32[]{:S(2)}) collective-permute-start(bf16[784,256]{1,0:T(8,128)(2,1)S(1)} %get-tuple-element.43), channel_id=1, source_target_pairs={{4,0},{5,1},{6,2},{7,3},{8,4},{9,5},{10,6},{11,7},{12,8},{13,9},{1... | collective-permute-start | bytes 1204232 | tf_op jit(solution)/shard_map/ppermute | solution.py:353
  9.1 5.8 %copy-start.2 = (bf16[6,32,128]{2,1,0:T(8,128)(2,1)S(1)}, bf16[6,32,128]{2,1,0:T(8,128)(2,1)}, u32[]{:S(2)}) copy-start(bf16[6,32,128]{2,1,0:T(8,128)(2,1)} %get-tuple-element.24.after_ref.unused_ref) | copy-start | bytes 147460
  10.1 1.6 %collective-permute-start.2 = (bf16[64,2048]{1,0:T(8,128)(2,1)S(1)}, bf16[64,2048]{1,0:T(8,128)(2,1)S(1)}, u32[]{:S(2)}, u32[]{:S(2)}) collective-permute-start(bf16[64,2048]{1,0:T(8,128)(2,1)S(1)} %stack.25.even_ref), channel_id=1, source_target_pairs={{0,1},{1,0},{2,3},{3,2},{4,5},{5,4},{6,7},{7,6},{8,9},{9,8},{10,11... | collective-permute-start | bytes 786440 | tf_op jit(solution)/shard_map/ppermute | solution.py:344
  12.4 7.0 %collective-permute-start.7 = (bf16[144,256]{1,0:T(8,128)(2,1)S(1)}, bf16[144,256]{1,0:T(8,128)(2,1)S(1)}, u32[]{:S(2)}, u32[]{:S(2)}) collective-permute-start(bf16[144,256]{1,0:T(8,128)(2,1)S(1)} %get-tuple-element.28), channel_id=1, source_target_pairs={{4,0},{5,1},{6,2},{7,3},{8,4},{9,5},{10,6},{11,7},{12,8},{13,9},{1... | collective-permute-start | bytes 221192 | tf_op jit(solution)/shard_map/ppermute | solution.py:353
  14.9 4.2 %collective-permute-start = (bf16[1,6,32,128]{3,2,1,0:T(8,128)(2,1)S(1)}, bf16[1,6,32,128]{3,2,1,0:T(8,128)(2,1)S(1)}, u32[]{:S(2)}, u32[]{:S(2)}) collective-permute-start(bf16[1,6,32,128]{3,2,1,0:T(8,128)(2,1)S(1)} %bitcast.18), channel_id=1, source_target_pairs={{0,8},{4,12},{8,0},{12,4},{16,24},{20,28},{24,16},{28,20},{1,9},{5... | collective-permute-start | bytes 147464 | tf_op jit(solution)/shard_map/ppermute | solution.py:408
  15.4 21.7 %collective-permute-start.5 = (bf16[928,256]{1,0:T(8,128)(2,1)S(1)}, bf16[928,256]{1,0:T(8,128)(2,1)S(1)}, u32[]{:S(2)}, u32[]{:S(2)}) collective-permute-start(bf16[928,256]{1,0:T(8,128)(2,1)S(1)} %get-tuple-element.26.after_ref), channel_id=1, source_target_pairs={{0,4},{1,5},{2,6},{3,7},{4,8},{5,9},{6,10},{7,11},{8,12},{9,13},{1... | collective-permute-start | bytes 1425416 | tf_op jit(solution)/shard_map/ppermute | solution.py:353
  19.1 12.1 %collective-permute-start.3 = (bf16[2,6,32,128]{3,2,1,0:T(8,128)(2,1)S(1)}, bf16[2,6,32,128]{3,2,1,0:T(8,128)(2,1)S(1)}, u32[]{:S(2)}, u32[]{:S(2)}) collective-permute-start(bf16[2,6,32,128]{3,2,1,0:T(8,128)(2,1)S(1)} %join.2.mine_ref), channel_id=1, source_target_pairs={{0,16},{4,20},{8,24},{12,28},{16,0},{20,4},{24,8},{28,12},{1,17},{... | collective-permute-start | bytes 294920 | tf_op jit(solution)/shard_map/ppermute | solution.py:408
  21.4 15.7 %copy-start.1 = (bf16[2048,784]{0,1:T(8,128)(2,1)S(1)}, bf16[2048,784]{0,1:T(8,128)(2,1)}, u32[]{:S(2)}) copy-start(bf16[2048,784]{0,1:T(8,128)(2,1)} %param.9) | copy-start | bytes 9633796
  26.8 10.3 %collective-permute-start.8 = (bf16[128,256]{1,0:T(8,128)(2,1)S(1)}, bf16[128,256]{1,0:T(8,128)(2,1)S(1)}, u32[]{:S(2)}, u32[]{:S(2)}) collective-permute-start(bf16[128,256]{1,0:T(8,128)(2,1)S(1)} %get-tuple-element.30), channel_id=1, source_target_pairs={{0,4},{1,5},{2,6},{3,7},{4,8},{5,9},{6,10},{7,11},{8,12},{9,13},{1... | collective-permute-start | bytes 196616 | tf_op jit(solution)/shard_map/ppermute | solution.py:353
  31.2 9.6 %collective-permute-start.4 = (bf16[4,6,32,128]{3,2,1,0:T(8,128)(2,1)S(1)}, bf16[4,6,32,128]{3,2,1,0:T(8,128)(2,1)S(1)}, u32[]{:S(2)}, u32[]{:S(2)}) collective-permute-start(bf16[4,6,32,128]{3,2,1,0:T(8,128)(2,1)S(1)} %join.3.mine_ref), channel_id=1, source_target_pairs={{0,4},{4,0},{8,12},{12,8},{16,20},{20,16},{24,28},{28,24},{1,5},{5... | collective-permute-start | bytes 589832 | tf_op jit(solution)/shard_map/ppermute | solution.py:408
  38.9 1.8 %collective-permute-start.9 = (f32[64,768]{1,0:T(8,128)S(1)}, f32[64,768]{1,0:T(8,128)S(1)}, u32[]{:S(2)}, u32[]{:S(2)}) collective-permute-start(f32[64,768]{1,0:T(8,128)S(1)} %get-tuple-element.36), channel_id=1, source_target_pairs={{0,1},{1,0},{2,3},{3,2},{4,5},{5,4},{6,7},{7,6},{8,9},{9,8},{10,11... | collective-permute-start | bytes 589832 | tf_op jit(solution)/shard_map/ppermute | solution.py:344
  39.0 1.8 %collective-permute-start.10 = (f32[64,768]{1,0:T(8,128)S(1)}, f32[64,768]{1,0:T(8,128)S(1)}, u32[]{:S(2)}, u32[]{:S(2)}) collective-permute-start(f32[64,768]{1,0:T(8,128)S(1)} %get-tuple-element.37), channel_id=1, source_target_pairs={{0,1},{1,0},{2,3},{3,2},{4,5},{5,4},{6,7},{7,6},{8,9},{9,8},{10,11... | collective-permute-start | bytes 589832 | tf_op jit(solution)/shard_map/ppermute | solution.py:344
  39.5 1.5 %collective-permute-start.11 = (f32[64,768]{1,0:T(8,128)S(1)}, f32[64,768]{1,0:T(8,128)S(1)}, u32[]{:S(2)}, u32[]{:S(2)}) collective-permute-start(f32[64,768]{1,0:T(8,128)S(1)} %get-tuple-element.38), channel_id=1, source_target_pairs={{0,1},{1,0},{2,3},{3,2},{4,5},{5,4},{6,7},{7,6},{8,9},{9,8},{10,11... | collective-permute-start | bytes 589832 | tf_op jit(solution)/shard_map/ppermute | solution.py:344
  41.0 7.9 %copy-start.3 = (f32[8,8,64,64]{3,2,1,0:T(8,128)S(1)}, f32[8,8,64,64]{3,2,1,0:T(8,128)}, u32[]{:S(2)}) copy-start(f32[8,8,64,64]{3,2,1,0:T(8,128)} %coupling_ref.1) | copy-start | bytes 3145732
  41.0 7.9 %copy-start.4 = (f32[4,8,64,64]{3,2,1,0:T(8,128)S(1)}, f32[4,8,64,64]{3,2,1,0:T(8,128)}, u32[]{:S(2)}) copy-start(f32[4,8,64,64]{3,2,1,0:T(8,128)} %up_ref.1) | copy-start | bytes 1572868
  41.0 7.9 %copy-start.5 = (f32[8,256,64]{1,2,0:T(8,128)S(1)}, f32[8,256,64]{1,2,0:T(8,128)}, u32[]{:S(2)}) copy-start(f32[8,256,64]{1,2,0:T(8,128)} %param.11) | copy-start | bytes 1572868
  41.0 7.9 %copy-start.6 = (f32[8,64,64]{2,1,0:T(8,128)S(1)}, f32[8,64,64]{2,1,0:T(8,128)}, u32[]{:S(2)}) copy-start(f32[8,64,64]{2,1,0:T(8,128)} %transfer_ref.1) | copy-start | bytes 393220
  41.0 7.9 %copy-start.7 = (bf16[2048,32]{0,1:T(8,128)(2,1)S(1)}, bf16[2048,32]{0,1:T(8,128)(2,1)}, u32[]{:S(2)}) copy-start(bf16[2048,32]{0,1:T(8,128)(2,1)} %param.10) | copy-start | bytes 393220
  41.0 7.9 %copy-start.8 = (s32[8,8]{1,0:T(8,128)S(1)}, s32[8,8]{1,0:T(8,128)}, u32[]{:S(2)}) copy-start(s32[8,8]{1,0:T(8,128)} %far_leaf_ref.1) | copy-start | bytes 772
  41.0 7.9 %copy-start.9 = (s32[4,8]{1,0:T(4,128)S(1)}, s32[4,8]{1,0:T(4,128)}, u32[]{:S(2)}) copy-start(s32[4,8]{1,0:T(4,128)} %far_up_ref.1) | copy-start | bytes 388
  41.1 11.6 %collective-permute-start.13 = (bf16[32,512]{1,0:T(8,128)(2,1)S(1)}, bf16[32,512]{1,0:T(8,128)(2,1)S(1)}, u32[]{:S(2)}, u32[]{:S(2)}) collective-permute-start(bf16[32,512]{1,0:T(8,128)(2,1)S(1)} %get-tuple-element.41), channel_id=1, source_target_pairs={{4,0},{5,1},{6,2},{7,3},{8,4},{9,5},{10,6},{11,7},{12,8},{13,9},{1... | collective-permute-start | bytes 98312 | tf_op jit(solution)/shard_map/ppermute | solution.py:353
  43.3 9.4 %collective-permute-start.14 = (bf16[32,512]{1,0:T(8,128)(2,1)S(1)}, bf16[32,512]{1,0:T(8,128)(2,1)S(1)}, u32[]{:S(2)}, u32[]{:S(2)}) collective-permute-start(bf16[32,512]{1,0:T(8,128)(2,1)S(1)} %get-tuple-element.42), channel_id=1, source_target_pairs={{4,2},{5,3},{6,0},{7,1},{8,6},{9,7},{10,4},{11,5},{12,10},{13,11},... | collective-permute-start | bytes 98312 | tf_op jit(solution)/shard_map/ppermute | solution.py:353
  47.3 5.5 %collective-permute-start.12 = (bf16[32,2048]{1,0:T(8,128)(2,1)S(1)}, bf16[32,2048]{1,0:T(8,128)(2,1)S(1)}, u32[]{:S(2)}, u32[]{:S(2)}) collective-permute-start(bf16[32,2048]{1,0:T(8,128)(2,1)S(1)} %get-tuple-element.40), channel_id=1, source_target_pairs={{0,2},{1,3},{2,0},{3,1},{4,6},{5,7},{6,4},{7,5},{8,10},{9,11},{10,... | collective-permute-start | bytes 393224 | tf_op jit(solution)/shard_map/ppermute | solution.py:344
  (3 other events, 7.1 us)

commit v4 on v3

--- a/solution.py
+++ b/solution.py
@@ -22,7 +22,7 @@
 HBM = pl.BlockSpec(memory_space=pltpu.HBM)
 ANY = pl.BlockSpec(memory_space=pl.ANY)
 MIB = 1 << 20
-WEIGHTS = {"own_low": 5, "high_tiles": 10, "far_field": 3, "split_back": 5, "finish": 0.1, "pack": 2, "stack": 1}
+WEIGHTS = {"own_low": 4, "high_tiles": 10, "far_field": 3, "split_back": 5, "finish": 0.1, "pack": 2, "stack": 1}
 
 
 def dot(a, b, dims):
@@ -90,7 +90,9 @@
     out_ref[count:] = came_ref[...]
 
 
-def assemble_kernel(leaves, sc_ref, x_ref, even_ref, odd_ref, v_ref, down_ref, up_ref):
+def assemble_kernel(
+    leaves, sc_ref, x_ref, even_ref, odd_ref, v_ref, down_ref, up_ref, masks_ref
+):
     features, pts = x_ref.shape
     rows = v_ref.shape[0]
     v_ref[: rows // 2] = even_ref[...]
@@ -110,6 +112,15 @@
     up_ref[:features] = x_ref[...]
     up_ref[features : features + rows] = v_ref[:, span(upper, pts)]
     up_ref[features + rows :] = flags(upper, base + leaves)
+    half = leaves // 2
+    ids = [half + i for i in range(half)]
+    masks = [
+        [(a <= upper) & listed(sc_ref, a, base - leaves + upper) for a in ids],
+        [a <= upper for a in ids],
+    ]
+    masks += [[(low ^ m) == i for i in range(half)] for m in range(half)]
+    for i, flags_of in enumerate(masks):
+        masks_ref[i : i + 1] = mask_row(flags_of, pts)
 
 
 def stack_kernel(*refs):
@@ -185,25 +196,23 @@
         out_refs[2 * group + 1][:, place] += term[rows // 2 :]
 
 
-def high_kernel(leaves, sc_ref, x_ref, halo_ref, sums_ref, v_ref, came_ref, unused_ref, *refs):
+def high_kernel(leaves, masks_ref, x_ref, halo_ref, sums_ref, v_ref, came_ref, unused_ref, *refs):
     ins, keep_ref, sends = refs[:4], refs[4], refs[5:]
     features, points = x_ref.shape
     pts = points // leaves
     rows = v_ref.shape[0]
     half = leaves // 2
-    b, base = sc_ref[0, 2], sc_ref[0, 3]
     x_b = halo_ref[:features].T
     col = column_sums(x_b, features)
     here = slice(half * pts, leaves * pts)
     leaf_ids = [half + i for i in range(half)]
     tile = tiles(x_b, x_ref[:, here], col, sums_ref[0:1, here], features)
-    to_a = [(a <= b) & listed(sc_ref, a, base - leaves + b) for a in leaf_ids]
-    term = dot(halo_ref[features : features + rows], tile, NN) * mask_row(to_a, pts)
+    term = dot(halo_ref[features : features + rows], tile, NN) * masks_ref[0:1]
     first = features + rows
     to_b = jnp.concatenate([halo_ref[first + a : first + a + 1, :] for a in leaf_ids], axis=1)
-    to_b = to_b * mask_row([a <= b for a in leaf_ids], pts).astype(BF16)
+    to_b = to_b * masks_ref[1:2].astype(BF16)
     back = dot(v_ref[:, here] * to_b, tile, NT)
-    mine = mask_row([b - half == i for i in range(half)], pts)
+    mine = masks_ref[2:3]
     came = came_ref[...].astype(F32)
     parts = []
     for i in (0, 1):
@@ -256,20 +265,14 @@
         return jnp.where(lax.rem(place, 2) == right, pair, pltpu.roll(pair, rank, 1))
 
     def field(list_ref, row, matrix_ref, per_device, first):
-        lhs, highs, lows = [], [], []
+        lhs, rhs = [], []
         for k in range(0, list_ref.shape[1], 2):
             left = entry(list_ref[row, k], per_device, first, 0)
             right = entry(list_ref[row, k + 1], per_device, first, 1)
             lhs.append(jnp.where(lanes < rank, left, right).astype(BF16))
             wide = jnp.concatenate([matrix_ref[row, k], matrix_ref[row, k + 1]], axis=1)
-            high, low = halves(wide)
-            highs.append(high)
-            lows.append(low)
-        rhs = jnp.concatenate(
-            [jnp.concatenate(highs, axis=1), jnp.concatenate(lows, axis=1)], axis=0
-        )
-        total = dot(jnp.concatenate(lhs, axis=1), rhs, NT)
-        return total[:, :rank] + total[:, rank:]
+            rhs.append(wide.astype(BF16))
+        return dot(jnp.concatenate(lhs, axis=1), jnp.concatenate(rhs, axis=1), NT)
 
     def stacked_dot(a, b, dims):
         both = jnp.concatenate(halves(a), axis=0)
@@ -288,19 +291,20 @@
             out_ref[:, here] = far + RIDGE * v_ref[:, here].astype(F32)
 
 
-def finish_kernel(blocks, sc_ref, far_ref, *refs):
+def finish_kernel(blocks, masks_ref, far_ref, *refs):
     out_ref = refs[-1]
     total = far_ref[...]
     for ref in refs[:blocks]:
         total = total + ref[...].astype(F32)
-    out_ref[...] = total
     back_refs = refs[blocks : 2 * blocks]
     pts = back_refs[0].shape[1] // 2
-    column = sc_ref[0, 0]
-    for m in range(blocks):
-        for core in (0, 1):
-            place = span((column ^ (2 * m + core)) + out_ref.shape[1] // pts // 2, pts)
-            out_ref[:, place] += back_refs[m][:, core * pts : (core + 1) * pts].astype(F32)
+    half = out_ref.shape[1] // pts // 2
+    out_ref[:, : half * pts] = total[:, : half * pts]
+    rows = total[:, half * pts :]
+    for m in range(2 * blocks):
+        part = back_refs[m // 2][:, m % 2 * pts : (m % 2 + 1) * pts].astype(F32)
+        rows = rows + jnp.concatenate([part] * half, axis=1) * masks_ref[2 + m : 3 + m]
+    out_ref[:, half * pts :] = rows
 
 
 def call(body, out_shape, in_specs, args, name, flops=0, bytes_accessed=0, scratch=(), limit=32):
@@ -385,12 +389,13 @@
         "stack",
     )
     odd_v = over_rhs(even_v, 1)
-    all_v, down, up = call(
+    all_v, down, up, masks = call(
         functools.partial(assemble_kernel, leaves),
         (
             shape((rows, leaves * pts), BF16),
             shape((rows + FLAG_ROWS, pts), BF16),
             shape((features + rows + FLAG_ROWS, pts), BF16),
+            shape((2 + half, wide), F32),
         ),
         [SMEM] + [VMEM] * 3,
         (scalars, chunk_up, even_v, odd_v),
@@ -449,9 +454,9 @@
         functools.partial(high_kernel, leaves),
         (shape((rows // 2, full), F32),)
         + (shape((rows // 2, full // CORE_PARTS), F32),) * CORE_PARTS,
-        [SMEM] + [VMEM] * 5 + [ANY] + [VMEM] * 4,
+        [VMEM] * 6 + [ANY] + [VMEM] * 4,
         (
-            scalars, x, halo_high, sums, all_v, came_low, message,
+            masks, x, halo_high, sums, all_v, came_low, stages[2],
             *totals,
         ),
         "high_tiles",
@@ -463,7 +468,7 @@
         + (shape((cols, leaves * pts), BF16),) * (blocks - 1)
         + (shape((cols, 2 * pts), BF16),) * blocks,
         [VMEM, ANY] + [VMEM] * CORE_PARTS,
-        (keep, stages[3], *came),
+        (keep, stages[-1], *came),
         "split_back",
     )
     backs = [over_leaf(block, -1, 2 * m) for m, block in enumerate(others[blocks - 1 :])]
@@ -473,8 +478,8 @@
     out = call(
         functools.partial(finish_kernel, blocks),
         shape((cols, leaves * pts), F32),
-        [SMEM] + [VMEM] * (1 + 2 * blocks),
-        (scalars, far, *parts, *backs),
+        [VMEM] * (2 + 2 * blocks),
+        (masks, far, *parts, *backs),
         "finish",
         0,
         2 * MIB,

time: 54.6 us -> 52.7 us (0.965)
  the two profiles are of different devices: /device:TPU:24 before, /device:TPU:10 now
where the time goes in v4:
time: 52.7 us; the launch traced here: 51.8 us
  starting transfers between devices  22.8 us (43%)
  Pallas kernels  14 us (27%)
  waiting for transfers between devices  10.6 us (20%)
  local copies, waits for them, and re-layouts  4.13 us (8%)
    ppermute x6, starting transfers between devices, over_leaf(): return lax.ppermute(array, ('leaf', 'rhs'), pairs)  18.1 us
    pallas_call x10, Pallas kernels, call(): pl.pallas_call(body, out_shape=out_shape, in_specs=in_specs, out_specs=ja...  14 us
    ppermute x3, waiting for transfers between devices, local(): lax.ppermute(everything, 'leaf', [(i, i ^ mask) for i in range(leaf_devic...  6.79 us
    unnamed x24, local copies, waits for them, and re-layouts  2.87 us
    ppermute x6, starting transfers between devices, over_rhs(): lax.ppermute(array, 'rhs', [(i, i ^ mask) for i in range(rhs_devices)])  2.81 us
    ppermute x6, waiting for transfers between devices, over_leaf(): return lax.ppermute(array, ('leaf', 'rhs'), pairs)  2.39 us
    ppermute x3, starting transfers between devices, local(): lax.ppermute(everything, 'leaf', [(i, i ^ mask) for i in range(leaf_devic...  1.84 us
    ppermute x6, waiting for transfers between devices, over_rhs(): lax.ppermute(array, 'rhs', [(i, i ^ mask) for i in range(rhs_devices)])  1.42 us
  transfers between devices with their start and end apart: 15, of which 5 were waited for; matrix products, arithmetic and copies ran while one was open for 2% of the time, Pallas kernels for 25%

profile of v4, /device:TPU:10, one launch (start us, length us, event | category | flops | bytes accessed | tf_op | source)
XLA Modules:
  0.0 51.8 jit_solution(372575994163331039)
XLA Ops:
  0.0 1.5 %collective-permute-start = (bf16[32,2048]{1,0:T(8,128)(2,1)}, bf16[32,2048]{1,0:T(8,128)(2,1)S(1)}, u32[]{:S(2)}, u32[]{:S(2)}) collective-permute-start(bf16[32,2048]{1,0:T(8,128)(2,1)} %bitcast.22), channel_id=1, source_target_pairs={{0,2},{1,3},{2,0},{3,1},{4,6},{5,7},{6,4},{7,5},{8,10},{9,11},{10,... | collective-permute-start | bytes 393224 | tf_op jit(solution)/shard_map/ppermute | solution.py:348
  1.5 1.2 %dynamic-slice_bitcast_fusion = (bf16[784,256]{1,0:T(8,128)(2,1)S(1)}, bf16[784,256]{1,0:T(8,128)(2,1)S(1)}) fusion(bf16[2048,784]{0,1:T(8,128)(2,1)} %param.9, s32[]{:T(128)S(6)} %select_n.7, s32[]{:T(128)S(6)} %select_n.6), kind=kLoop, calls=%fused_computation | loop fusion | bytes 1605640 | tf_op jit(solution)/shard_map/dynamic_slice | solution.py:363
  2.7 2.4 %collective-permute-start.6 = (bf16[784,256]{1,0:T(8,128)(2,1)S(1)}, bf16[784,256]{1,0:T(8,128)(2,1)S(1)}, u32[]{:S(2)}, u32[]{:S(2)}) collective-permute-start(bf16[784,256]{1,0:T(8,128)(2,1)S(1)} %get-tuple-element.45), channel_id=1, source_target_pairs={{4,0},{5,1},{6,2},{7,3},{8,4},{9,5},{10,6},{11,7},{12,8},{13,9},{1... | collective-permute-start | bytes 1204232 | tf_op jit(solution)/shard_map/ppermute | solution.py:357
  5.2 3.1 %pack.1 = (bf16[6,32,128]{2,1,0:T(8,128)(2,1)}, bf16[32,2048]{1,0:T(8,128)(2,1)}) custom-call(bf16[32,2048]{1,0:T(8,128)(2,1)} %bitcast.23, f32[8,64,256]{2,1,0:T(8,128)} %bitcast.20, f32[8,64,64]{2,1,0:T(8,128)} %transfer_ref.1), custom_call_target="tpu_custom_call" | custom-call | flops 2300000000 | tf_op jit(solution)/shard_map/pack/pallas_call | solution.py:312
  8.3 0.9 %copy-done.10 = bf16[32,2048]{1,0:T(8,128)(2,1)S(1)} copy-done((bf16[32,2048]{1,0:T(8,128)(2,1)S(1)}, bf16[32,2048]{1,0:T(8,128)(2,1)}, u32[]{:S(2)}) %copy-start.10) | copy-done | bytes 131096
  9.4 1.4 %collective-permute-done.1.odd_ref = bf16[64,2048]{1,0:T(8,128)(2,1)S(1)} collective-permute-done((bf16[64,2048]{1,0:T(8,128)(2,1)S(1)}, bf16[64,2048]{1,0:T(8,128)(2,1)S(1)}, u32[]{:S(2)}, u32[]{:S(2)}) %collective-permute-start.1) | collective-permute-done | bytes 262176 | tf_op jit(solution)/shard_map/ppermute | solution.py:348
  10.8 0.8 %assemble.1 = (bf16[128,2048]{1,0:T(8,128)(2,1)S(1)}, bf16[144,256]{1,0:T(8,128)(2,1)S(1)}, bf16[928,256]{1,0:T(8,128)(2,1)S(1)}, f32[6,1024]{1,0:T(8,128)S(1)}) custom-call(s32[9,8]{1,0:T(8,128)S(1)} %pad_add_fusion.sc_ref, bf16[784,256]{1,0:T(8,128)(2,1)S(1)} %get-tuple-element.46.x_ref, bf16[64,2048]{1,0:T(8,128)(2,1)S(1)} %stack.25.even_ref, ...), custom_call_target="tpu_custom_call" | custom-call | tf_op jit(solution)/shard_map/assemble/pallas_call | solution.py:312
  11.6 3.3 %collective-permute-start.7 = (bf16[144,256]{1,0:T(8,128)(2,1)S(1)}, bf16[144,256]{1,0:T(8,128)(2,1)S(1)}, u32[]{:S(2)}, u32[]{:S(2)}) collective-permute-start(bf16[144,256]{1,0:T(8,128)(2,1)S(1)} %get-tuple-element.30), channel_id=1, source_target_pairs={{4,0},{5,1},{6,2},{7,3},{8,4},{9,5},{10,6},{11,7},{12,8},{13,9},{1... | collective-permute-start | bytes 221192 | tf_op jit(solution)/shard_map/ppermute | solution.py:357
  15.0 5.0 %collective-permute-start.5 = (bf16[928,256]{1,0:T(8,128)(2,1)S(1)}, bf16[928,256]{1,0:T(8,128)(2,1)S(1)}, u32[]{:S(2)}, u32[]{:S(2)}) collective-permute-start(bf16[928,256]{1,0:T(8,128)(2,1)S(1)} %get-tuple-element.28.after_ref), channel_id=1, source_target_pairs={{0,4},{1,5},{2,6},{3,7},{4,8},{5,9},{6,10},{7,11},{8,12},{9,13},{1... | collective-permute-start | bytes 1425416 | tf_op jit(solution)/shard_map/ppermute | solution.py:357
  20.1 1.7 %collective-permute-start.3 = (bf16[2,6,32,128]{3,2,1,0:T(8,128)(2,1)S(1)}, bf16[2,6,32,128]{3,2,1,0:T(8,128)(2,1)S(1)}, u32[]{:S(2)}, u32[]{:S(2)}) collective-permute-start(bf16[2,6,32,128]{3,2,1,0:T(8,128)(2,1)S(1)} %join.2.mine_ref), channel_id=1, source_target_pairs={{0,16},{4,20},{8,24},{12,28},{16,0},{20,4},{24,8},{28,12},{1,17},{... | collective-permute-start | bytes 294920 | tf_op jit(solution)/shard_map/ppermute | solution.py:413
  21.8 1.9 %copy-done = bf16[2048,784]{0,1:T(8,128)(2,1)S(1)} copy-done((bf16[2048,784]{0,1:T(8,128)(2,1)S(1)}, bf16[2048,784]{0,1:T(8,128)(2,1)}, u32[]{:S(2)}) %copy-start) | copy-done | bytes 3211288
  23.7 5.4 %own_low.1 = (f32[64,1024]{1,0:T(8,128)S(1)}, f32[64,1024]{1,0:T(8,128)S(1)}, f32[64,1024]{1,0:T(8,128)S(1)}, f32[64,1024]{1,0:T(8,128)S(1)}, f32[8,2048]{1,0:T(8,128)S(1)}, /*index=5*/bf16[128,256]{1,0:T(8,128)(2,1)S(1)}) custom-call(s32[9,8]{1,0:T(8,128)S(1)} %pad_add_fusion.sc_ref, bf16[784,2048]{1,0:T(8,128)(2,1)S(1)} %bitcast.16, ...), custom_call_target="tpu_custom_call" | custom-call | flops 4600000000 | tf_op jit(solution)/shard_map/own_low/pallas_call | solution.py:312
  29.1 2.1 %collective-permute-start.8 = (bf16[128,256]{1,0:T(8,128)(2,1)S(1)}, bf16[128,256]{1,0:T(8,128)(2,1)S(1)}, u32[]{:S(2)}, u32[]{:S(2)}) collective-permute-start(bf16[128,256]{1,0:T(8,128)(2,1)S(1)} %get-tuple-element.32), channel_id=1, source_target_pairs={{0,4},{1,5},{2,6},{3,7},{4,8},{5,9},{6,10},{7,11},{8,12},{9,13},{1... | collective-permute-start | bytes 196616 | tf_op jit(solution)/shard_map/ppermute | solution.py:357
  31.3 3.6 %collective-permute-done.3.came_ref.unused_ref = bf16[2,6,32,128]{3,2,1,0:T(8,128)(2,1)S(1)} collective-permute-done((bf16[2,6,32,128]{3,2,1,0:T(8,128)(2,1)S(1)}, bf16[2,6,32,128]{3,2,1,0:T(8,128)(2,1)S(1)}, u32[]{:S(2)}, u32[]{:S(2)}) %collective-permute-start.3) | collective-permute-done | bytes 98336 | tf_op jit(solution)/shard_map/ppermute | solution.py:413
  34.9 0.6 %collective-permute-done.8.came_ref = bf16[128,256]{1,0:T(8,128)(2,1)S(1)} collective-permute-done((bf16[128,256]{1,0:T(8,128)(2,1)S(1)}, bf16[128,256]{1,0:T(8,128)(2,1)S(1)}, u32[]{:S(2)}, u32[]{:S(2)}) %collective-permute-start.8) | collective-permute-done | bytes 65568 | tf_op jit(solution)/shard_map/ppermute | solution.py:357
  35.5 1.2 %high_tiles.1 = (f32[64,2304]{1,0:T(8,128)S(1)}, f32[64,768]{1,0:T(8,128)S(1)}, f32[64,768]{1,0:T(8,128)S(1)}, f32[64,768]{1,0:T(8,128)S(1)}) custom-call(f32[6,1024]{1,0:T(8,128)S(1)} %get-tuple-element.26.masks_ref, bf16[784,2048]{1,0:T(8,128)(2,1)S(1)} %bitcast.17, bf16[928,256]{1,0:T(8,128)(2,1)S(1)} %collective-permute-done.5.halo_ref, ...), custom_call_target="tpu_custom_call" | custom-call | flops 11500000256 | tf_op jit(solution)/shard_map/high_tiles/pallas_call | solution.py:312
  36.8 0.5 collective-permute-start.11
  37.3 3.2 %collective-permute-done.4.came_ref.unused_ref = bf16[4,6,32,128]{3,2,1,0:T(8,128)(2,1)S(1)} collective-permute-done((bf16[4,6,32,128]{3,2,1,0:T(8,128)(2,1)S(1)}, bf16[4,6,32,128]{3,2,1,0:T(8,128)(2,1)S(1)}, u32[]{:S(2)}, u32[]{:S(2)}) %collective-permute-start.4) | collective-permute-done | bytes 196640 | tf_op jit(solution)/shard_map/ppermute | solution.py:413
  40.7 0.6 %collective-permute-start.12 = (bf16[32,2048]{1,0:T(8,128)(2,1)S(1)}, bf16[32,2048]{1,0:T(8,128)(2,1)S(1)}, u32[]{:S(2)}, u32[]{:S(2)}) collective-permute-start(bf16[32,2048]{1,0:T(8,128)(2,1)S(1)} %get-tuple-element.42), channel_id=1, source_target_pairs={{0,2},{1,3},{2,0},{3,1},{4,6},{5,7},{6,4},{7,5},{8,10},{9,11},{10,... | collective-permute-start | bytes 393224 | tf_op jit(solution)/shard_map/ppermute | solution.py:348
  41.3 2.1 %collective-permute-start.13 = (bf16[32,512]{1,0:T(8,128)(2,1)S(1)}, bf16[32,512]{1,0:T(8,128)(2,1)S(1)}, u32[]{:S(2)}, u32[]{:S(2)}) collective-permute-start(bf16[32,512]{1,0:T(8,128)(2,1)S(1)} %get-tuple-element.43), channel_id=1, source_target_pairs={{4,0},{5,1},{6,2},{7,3},{8,4},{9,5},{10,6},{11,7},{12,8},{13,9},{1... | collective-permute-start | bytes 98312 | tf_op jit(solution)/shard_map/ppermute | solution.py:357
  43.4 3.1 %collective-permute-start.14 = (bf16[32,512]{1,0:T(8,128)(2,1)S(1)}, bf16[32,512]{1,0:T(8,128)(2,1)S(1)}, u32[]{:S(2)}, u32[]{:S(2)}) collective-permute-start(bf16[32,512]{1,0:T(8,128)(2,1)S(1)} %get-tuple-element.44), channel_id=1, source_target_pairs={{4,2},{5,3},{6,0},{7,1},{8,6},{9,7},{10,4},{11,5},{12,10},{13,11},... | collective-permute-start | bytes 98312 | tf_op jit(solution)/shard_map/ppermute | solution.py:357
  46.6 2.6 %far_field.1.far_ref = f32[32,2048]{1,0:T(8,128)S(1)} custom-call(s32[9,8]{1,0:T(8,128)S(1)} %pad_add_fusion.sc_ref, s32[8,8]{1,0:T(8,128)S(1)} %copy-done.8, s32[4,8]{1,0:T(4,128)S(1)} %copy-done.9, bf16[4,6,32,128]{3,2,1,0:T(8,128)(2,1)S(1)} %join.3.mine_ref, bf16[4,6,32,128]{3,2,1,0:T(8,128)(2,1)S(1)} %collective-permute-done.4.came_ref.unused_ref, ...), custom_call_target="tpu_custom_call" | custom-call | flops 3449999872 | tf_op jit(solution)/shard_map/far_field/pallas_call | solution.py:312
  49.3 1.8 %collective-permute-done.14.refs_3_ = bf16[32,512]{1,0:T(8,128)(2,1)S(1)} collective-permute-done((bf16[32,512]{1,0:T(8,128)(2,1)S(1)}, bf16[32,512]{1,0:T(8,128)(2,1)S(1)}, u32[]{:S(2)}, u32[]{:S(2)}) %collective-permute-start.14) | collective-permute-done | bytes 32800 | tf_op jit(solution)/shard_map/ppermute | solution.py:357
  51.0 0.8 %finish.1 = f32[32,2048]{1,0:T(8,128)} custom-call(f32[6,1024]{1,0:T(8,128)S(1)} %get-tuple-element.26.masks_ref, f32[32,2048]{1,0:T(8,128)S(1)} %far_field.1.far_ref, f32[32,2048]{1,0:T(8,128)S(1)} %get-tuple-element.41.refs_0_, bf16[32,2048]{1,0:T(8,128)(2,1)S(1)} %collective-permute-done.12.refs_1_, bf16[32,512]{1,0:T(8,128)(2,1)S(1)} %collective-permute-done.13.refs_2_, ...), custom_call_target="tpu_custom_call" | custom-call | flops 115000000 | tf_op jit(solution)/shard_map/finish/pallas_call | solution.py:312
  (44 shorter events, 0.7 us)
Async XLA Ops:
  0.0 8.3 %collective-permute-start = (bf16[32,2048]{1,0:T(8,128)(2,1)}, bf16[32,2048]{1,0:T(8,128)(2,1)S(1)}, u32[]{:S(2)}, u32[]{:S(2)}) collective-permute-start(bf16[32,2048]{1,0:T(8,128)(2,1)} %bitcast.22), channel_id=1, source_target_pairs={{0,2},{1,3},{2,0},{3,1},{4,6},{5,7},{6,4},{7,5},{8,10},{9,11},{10,... | collective-permute-start | bytes 393224 | tf_op jit(solution)/shard_map/ppermute | solution.py:348
  2.7 19.1 %collective-permute-start.6 = (bf16[784,256]{1,0:T(8,128)(2,1)S(1)}, bf16[784,256]{1,0:T(8,128)(2,1)S(1)}, u32[]{:S(2)}, u32[]{:S(2)}) collective-permute-start(bf16[784,256]{1,0:T(8,128)(2,1)S(1)} %get-tuple-element.45), channel_id=1, source_target_pairs={{4,0},{5,1},{6,2},{7,3},{8,4},{9,5},{10,6},{11,7},{12,8},{13,9},{1... | collective-permute-start | bytes 1204232 | tf_op jit(solution)/shard_map/ppermute | solution.py:357
  8.3 6.7 %copy-start.2 = (bf16[6,32,128]{2,1,0:T(8,128)(2,1)S(1)}, bf16[6,32,128]{2,1,0:T(8,128)(2,1)}, u32[]{:S(2)}) copy-start(bf16[6,32,128]{2,1,0:T(8,128)(2,1)} %get-tuple-element.27.after_ref) | copy-start | bytes 147460
  9.2 1.6 %collective-permute-start.1 = (bf16[64,2048]{1,0:T(8,128)(2,1)S(1)}, bf16[64,2048]{1,0:T(8,128)(2,1)S(1)}, u32[]{:S(2)}, u32[]{:S(2)}) collective-permute-start(bf16[64,2048]{1,0:T(8,128)(2,1)S(1)} %stack.25.even_ref), channel_id=1, source_target_pairs={{0,1},{1,0},{2,3},{3,2},{4,5},{5,4},{6,7},{7,6},{8,9},{9,8},{10,11... | collective-permute-start | bytes 786440 | tf_op jit(solution)/shard_map/ppermute | solution.py:348
  11.6 10.1 %collective-permute-start.7 = (bf16[144,256]{1,0:T(8,128)(2,1)S(1)}, bf16[144,256]{1,0:T(8,128)(2,1)S(1)}, u32[]{:S(2)}, u32[]{:S(2)}) collective-permute-start(bf16[144,256]{1,0:T(8,128)(2,1)S(1)} %get-tuple-element.30), channel_id=1, source_target_pairs={{4,0},{5,1},{6,2},{7,3},{8,4},{9,5},{10,6},{11,7},{12,8},{13,9},{1... | collective-permute-start | bytes 221192 | tf_op jit(solution)/shard_map/ppermute | solution.py:357
  15.0 5.1 %collective-permute-start.2 = (bf16[1,6,32,128]{3,2,1,0:T(8,128)(2,1)S(1)}, bf16[1,6,32,128]{3,2,1,0:T(8,128)(2,1)S(1)}, u32[]{:S(2)}, u32[]{:S(2)}) collective-permute-start(bf16[1,6,32,128]{3,2,1,0:T(8,128)(2,1)S(1)} %bitcast.18), channel_id=1, source_target_pairs={{0,8},{4,12},{8,0},{12,4},{16,24},{20,28},{24,16},{28,20},{1,9},{5... | collective-permute-start | bytes 147464 | tf_op jit(solution)/shard_map/ppermute | solution.py:413
  15.0 20.5 %collective-permute-start.5 = (bf16[928,256]{1,0:T(8,128)(2,1)S(1)}, bf16[928,256]{1,0:T(8,128)(2,1)S(1)}, u32[]{:S(2)}, u32[]{:S(2)}) collective-permute-start(bf16[928,256]{1,0:T(8,128)(2,1)S(1)} %get-tuple-element.28.after_ref), channel_id=1, source_target_pairs={{0,4},{1,5},{2,6},{3,7},{4,8},{5,9},{6,10},{7,11},{8,12},{9,13},{1... | collective-permute-start | bytes 1425416 | tf_op jit(solution)/shard_map/ppermute | solution.py:357
  20.1 14.7 %collective-permute-start.3 = (bf16[2,6,32,128]{3,2,1,0:T(8,128)(2,1)S(1)}, bf16[2,6,32,128]{3,2,1,0:T(8,128)(2,1)S(1)}, u32[]{:S(2)}, u32[]{:S(2)}) collective-permute-start(bf16[2,6,32,128]{3,2,1,0:T(8,128)(2,1)S(1)} %join.2.mine_ref), channel_id=1, source_target_pairs={{0,16},{4,20},{8,24},{12,28},{16,0},{20,4},{24,8},{28,12},{1,17},{... | collective-permute-start | bytes 294920 | tf_op jit(solution)/shard_map/ppermute | solution.py:413
  23.7 11.8 %copy-start.1 = (bf16[2048,784]{0,1:T(8,128)(2,1)S(1)}, bf16[2048,784]{0,1:T(8,128)(2,1)}, u32[]{:S(2)}) copy-start(bf16[2048,784]{0,1:T(8,128)(2,1)} %param.9) | copy-start | bytes 9633796
  29.1 6.4 %collective-permute-start.8 = (bf16[128,256]{1,0:T(8,128)(2,1)S(1)}, bf16[128,256]{1,0:T(8,128)(2,1)S(1)}, u32[]{:S(2)}, u32[]{:S(2)}) collective-permute-start(bf16[128,256]{1,0:T(8,128)(2,1)S(1)} %get-tuple-element.32), channel_id=1, source_target_pairs={{0,4},{1,5},{2,6},{3,7},{4,8},{5,9},{6,10},{7,11},{8,12},{9,13},{1... | collective-permute-start | bytes 196616 | tf_op jit(solution)/shard_map/ppermute | solution.py:357
  34.8 5.7 %collective-permute-start.4 = (bf16[4,6,32,128]{3,2,1,0:T(8,128)(2,1)S(1)}, bf16[4,6,32,128]{3,2,1,0:T(8,128)(2,1)S(1)}, u32[]{:S(2)}, u32[]{:S(2)}) collective-permute-start(bf16[4,6,32,128]{3,2,1,0:T(8,128)(2,1)S(1)} %join.3.mine_ref), channel_id=1, source_target_pairs={{0,4},{4,0},{8,12},{12,8},{16,20},{20,16},{24,28},{28,24},{1,5},{5... | collective-permute-start | bytes 589832 | tf_op jit(solution)/shard_map/ppermute | solution.py:413
  36.7 3.9 %collective-permute-start.10 = (f32[64,768]{1,0:T(8,128)S(1)}, f32[64,768]{1,0:T(8,128)S(1)}, u32[]{:S(2)}, u32[]{:S(2)}) collective-permute-start(f32[64,768]{1,0:T(8,128)S(1)} %get-tuple-element.39), channel_id=1, source_target_pairs={{0,1},{1,0},{2,3},{3,2},{4,5},{5,4},{6,7},{7,6},{8,9},{9,8},{10,11... | collective-permute-start | bytes 589832 | tf_op jit(solution)/shard_map/ppermute | solution.py:348
  36.8 3.8 %collective-permute-start.11 = (f32[64,768]{1,0:T(8,128)S(1)}, f32[64,768]{1,0:T(8,128)S(1)}, u32[]{:S(2)}, u32[]{:S(2)}) collective-permute-start(f32[64,768]{1,0:T(8,128)S(1)} %get-tuple-element.40), channel_id=1, source_target_pairs={{0,1},{1,0},{2,3},{3,2},{4,5},{5,4},{6,7},{7,6},{8,9},{9,8},{10,11... | collective-permute-start | bytes 589832 | tf_op jit(solution)/shard_map/ppermute | solution.py:348
  37.3 3.3 %collective-permute-start.9 = (f32[64,768]{1,0:T(8,128)S(1)}, f32[64,768]{1,0:T(8,128)S(1)}, u32[]{:S(2)}, u32[]{:S(2)}) collective-permute-start(f32[64,768]{1,0:T(8,128)S(1)} %get-tuple-element.38), channel_id=1, source_target_pairs={{0,1},{1,0},{2,3},{3,2},{4,5},{5,4},{6,7},{7,6},{8,9},{9,8},{10,11... | collective-permute-start | bytes 589832 | tf_op jit(solution)/shard_map/ppermute | solution.py:348
  40.6 6.0 %copy-start.3 = (f32[8,8,64,64]{3,2,1,0:T(8,128)S(1)}, f32[8,8,64,64]{3,2,1,0:T(8,128)}, u32[]{:S(2)}) copy-start(f32[8,8,64,64]{3,2,1,0:T(8,128)} %coupling_ref.1) | copy-start | bytes 3145732
  40.6 6.0 %copy-start.4 = (f32[4,8,64,64]{3,2,1,0:T(8,128)S(1)}, f32[4,8,64,64]{3,2,1,0:T(8,128)}, u32[]{:S(2)}) copy-start(f32[4,8,64,64]{3,2,1,0:T(8,128)} %up_ref.1) | copy-start | bytes 1572868
  40.6 6.0 %copy-start.5 = (f32[8,256,64]{1,2,0:T(8,128)S(1)}, f32[8,256,64]{1,2,0:T(8,128)}, u32[]{:S(2)}) copy-start(f32[8,256,64]{1,2,0:T(8,128)} %param.11) | copy-start | bytes 1572868
  40.6 6.0 %copy-start.6 = (f32[8,64,64]{2,1,0:T(8,128)S(1)}, f32[8,64,64]{2,1,0:T(8,128)}, u32[]{:S(2)}) copy-start(f32[8,64,64]{2,1,0:T(8,128)} %transfer_ref.1) | copy-start | bytes 393220
  40.6 6.0 %copy-start.7 = (bf16[2048,32]{0,1:T(8,128)(2,1)S(1)}, bf16[2048,32]{0,1:T(8,128)(2,1)}, u32[]{:S(2)}) copy-start(bf16[2048,32]{0,1:T(8,128)(2,1)} %param.10) | copy-start | bytes 393220
  40.6 6.0 %copy-start.8 = (s32[8,8]{1,0:T(8,128)S(1)}, s32[8,8]{1,0:T(8,128)}, u32[]{:S(2)}) copy-start(s32[8,8]{1,0:T(8,128)} %far_leaf_ref.1) | copy-start | bytes 772
  40.6 6.0 %copy-start.9 = (s32[4,8]{1,0:T(4,128)S(1)}, s32[4,8]{1,0:T(4,128)}, u32[]{:S(2)}) copy-start(s32[4,8]{1,0:T(4,128)} %far_up_ref.1) | copy-start | bytes 388
  40.7 10.3 %collective-permute-start.12 = (bf16[32,2048]{1,0:T(8,128)(2,1)S(1)}, bf16[32,2048]{1,0:T(8,128)(2,1)S(1)}, u32[]{:S(2)}, u32[]{:S(2)}) collective-permute-start(bf16[32,2048]{1,0:T(8,128)(2,1)S(1)} %get-tuple-element.42), channel_id=1, source_target_pairs={{0,2},{1,3},{2,0},{3,1},{4,6},{5,7},{6,4},{7,5},{8,10},{9,11},{10,... | collective-permute-start | bytes 393224 | tf_op jit(solution)/shard_map/ppermute | solution.py:348
  41.3 8.0 %collective-permute-start.13 = (bf16[32,512]{1,0:T(8,128)(2,1)S(1)}, bf16[32,512]{1,0:T(8,128)(2,1)S(1)}, u32[]{:S(2)}, u32[]{:S(2)}) collective-permute-start(bf16[32,512]{1,0:T(8,128)(2,1)S(1)} %get-tuple-element.43), channel_id=1, source_target_pairs={{4,0},{5,1},{6,2},{7,3},{8,4},{9,5},{10,6},{11,7},{12,8},{13,9},{1... | collective-permute-start | bytes 98312 | tf_op jit(solution)/shard_map/ppermute | solution.py:357
  43.4 7.6 %collective-permute-start.14 = (bf16[32,512]{1,0:T(8,128)(2,1)S(1)}, bf16[32,512]{1,0:T(8,128)(2,1)S(1)}, u32[]{:S(2)}, u32[]{:S(2)}) collective-permute-start(bf16[32,512]{1,0:T(8,128)(2,1)S(1)} %get-tuple-element.44), channel_id=1, source_target_pairs={{4,2},{5,3},{6,0},{7,1},{8,6},{9,7},{10,4},{11,5},{12,10},{13,11},... | collective-permute-start | bytes 98312 | tf_op jit(solution)/shard_map/ppermute | solution.py:357
  (3 other events, 7.1 us)

commit v5 on v4

--- a/solution.py
+++ b/solution.py
@@ -22,7 +22,7 @@
 HBM = pl.BlockSpec(memory_space=pltpu.HBM)
 ANY = pl.BlockSpec(memory_space=pl.ANY)
 MIB = 1 << 20
-WEIGHTS = {"own_low": 4, "high_tiles": 10, "far_field": 3, "split_back": 5, "finish": 0.1, "pack": 2, "stack": 1}
+WEIGHTS = {"high_tiles": 10, "far_field": 3, "split_back": 5, "finish": 0.1, "own_low": 5, "pack": 2, "stack": 1}
 
 
 def dot(a, b, dims):
@@ -119,11 +119,20 @@
         [a <= upper for a in ids],
     ]
     masks += [[(low ^ m) == i for i in range(half)] for m in range(half)]
+    high = sc_ref[0, 1]
+    for b, group in ((high, 1), (high, 0), (low, 0)):
+        ids = [group * half + i for i in range(half)]
+        masks.append([(a <= b) & listed(sc_ref, a, base + b) for a in ids])
+        masks.append([(a < b) & listed(sc_ref, b, base + a) for a in ids])
+    for group in (1, 0):
+        ids = [group * half + i for i in range(half)]
+        masks.append([(a >= low) & listed(sc_ref, a, base + leaves + low) for a in ids])
+        masks.append([a >= low for a in ids])
     for i, flags_of in enumerate(masks):
         masks_ref[i : i + 1] = mask_row(flags_of, pts)
 
 
-def stack_kernel(*refs):
+def stack_kernel(unused_ref, *refs):
     out_ref = refs[-1]
     first = 0
     for ref in refs[:-1]:
@@ -149,14 +158,19 @@
 
 
 def own_low_kernel(
-    leaves, sc_ref, x_ref, v_ref, halo_ref, near_ref, unused_ref, *refs
+    leaves, masks_ref, x_ref, v_ref, halo_ref, near_ref, unused_ref, *refs
 ):
     out_refs, sums_ref, back_ref = refs[:4], refs[4], refs[5]
     features, points = x_ref.shape
     pts = points // leaves
     rows = v_ref.shape[0]
     half = leaves // 2
-    low, high, base = sc_ref[0, 0], sc_ref[0, 1], sc_ref[0, 3]
+    low = lax.axis_index("rhs")
+    high = leaves - 1 - low
+
+    def mask(i):
+        return masks_ref[2 + half + i : 3 + half + i]
+
     for leaf in range(leaves):
         here = slice(leaf * pts, (leaf + 1) * pts)
         sums_ref[:, here] = jnp.broadcast_to(
@@ -172,19 +186,17 @@
         row = sums_ref[0:1, here]
 
         tile = tiles(x_bs[2], x_ref[:, here], cols[2], row, features)
-        to_a = [(a >= low) & listed(sc_ref, a, base + leaves + low) for a in leaf_ids]
-        total = dot(near_ref[:rows], tile, NN) * mask_row(to_a, pts)
+        total = dot(near_ref[:rows], tile, NN) * mask(8 - 2 * group)
         to_b = jnp.concatenate([near_ref[rows + a : rows + a + 1, :] for a in leaf_ids], axis=1)
-        to_b = to_b * mask_row([a >= low for a in leaf_ids], pts).astype(BF16)
+        to_b = to_b * mask(9 - 2 * group).astype(BF16)
         term = dot(v_ref[:, here] * to_b, tile, NT)
         back = term if back is None else back + term
 
         for which, b in enumerate((high, low)[: 2 - group]):
             tile = tiles(x_bs[which], x_ref[:, here], cols[which], row, features)
-            to_a = [(a <= b) & listed(sc_ref, a, base + b) for a in leaf_ids]
-            to_b = [(a < b) & listed(sc_ref, b, base + a) for a in leaf_ids]
-            total = total + dot(v_ref[:, span(b, pts)], tile, NN) * mask_row(to_a, pts)
-            masked = v_ref[:, here] * mask_row(to_b, pts).astype(BF16)
+            first = 2 * (1 - group + which)
+            total = total + dot(v_ref[:, span(b, pts)], tile, NN) * mask(first)
+            masked = v_ref[:, here] * mask(first + 1).astype(BF16)
             term = dot(masked, tile, NT)
             updates[which] = term if updates[which] is None else updates[which] + term
         out_refs[2 * group][...] = total[: rows // 2]
@@ -360,11 +372,6 @@
     v = vectors.T
     bases_t = jnp.swapaxes(bases, 1, 2)
 
-    chunk_low = lax.dynamic_slice_in_dim(x, low * pts, pts, 1)
-    chunk_up = lax.dynamic_slice_in_dim(x, upper * pts, pts, 1)
-    halo_low = over_leaf(chunk_low, -1)
-    others = [over_rhs(v, m) for m in range(2, rhs_devices, 2)]
-
     message, v_here = call(
         pack_kernel,
         (
@@ -381,29 +388,11 @@
         ],
         limit=PACK_LIMIT,
     )
-    even_v = call(
-        stack_kernel,
-        shape((rows // 2, leaves * pts), BF16),
-        [VMEM] * (1 + len(others)),
-        (v_here, *others),
-        "stack",
-    )
-    odd_v = over_rhs(even_v, 1)
-    all_v, down, up, masks = call(
-        functools.partial(assemble_kernel, leaves),
-        (
-            shape((rows, leaves * pts), BF16),
-            shape((rows + FLAG_ROWS, pts), BF16),
-            shape((features + rows + FLAG_ROWS, pts), BF16),
-            shape((2 + half, wide), F32),
-        ),
-        [SMEM] + [VMEM] * 3,
-        (scalars, chunk_up, even_v, odd_v),
-        "assemble",
-    )
-
-    near_low = over_leaf(down, -1)
-    halo_high = over_leaf(up, 1)
+    x_late, message = lax.optimization_barrier((x, message))
+    chunk_low = lax.dynamic_slice_in_dim(x_late, low * pts, pts, 1)
+    chunk_up = lax.dynamic_slice_in_dim(x_late, upper * pts, pts, 1)
+    halo_low = over_leaf(chunk_low, -1)
+    others = [over_rhs(v, m) for m in range(2, rhs_devices, 2)]
 
     everything = message[None]
     stages = [message]
@@ -418,18 +407,42 @@
             join_kernel,
             shape((2 * bit,) + message.shape, BF16),
             [VMEM] * 2 + [ANY],
-            (everything, arrived, up if bit == 1 else message),
+            (everything, arrived, message),
             "join",
         )
         bit *= 2
 
+
+    even_v = call(
+        stack_kernel,
+        shape((rows // 2, leaves * pts), BF16),
+        [ANY] + [VMEM] * (1 + len(others)),
+        (stages[1], v_here, *others),
+        "stack",
+    )
+    odd_v = over_rhs(even_v, 1)
+    all_v, down, up, masks = call(
+        functools.partial(assemble_kernel, leaves),
+        (
+            shape((rows, leaves * pts), BF16),
+            shape((rows + FLAG_ROWS, pts), BF16),
+            shape((features + rows + FLAG_ROWS, pts), BF16),
+            shape((12 + half, wide), F32),
+        ),
+        [SMEM] + [VMEM] * 3,
+        (scalars, chunk_up, even_v, odd_v),
+        "assemble",
+    )
+
+    near_low = over_leaf(down, -1)
+    halo_high = over_leaf(up, 1)
 
     part = shape((rows // 2, wide), F32)
     *totals, sums, back_low = call(
         functools.partial(own_low_kernel, leaves),
         (part,) * 4 + (shape((8, leaves * pts), F32), shape((rows, pts), BF16)),
-        [SMEM] + [VMEM] * 4 + [ANY],
-        (scalars, x, all_v, halo_low, near_low, stages[1]),
+        [VMEM] * 5 + [ANY],
+        (masks, x, all_v, halo_low, near_low, message),
         "own_low",
         5 * 10**9,
         0,
@@ -456,7 +469,7 @@
         + (shape((rows // 2, full // CORE_PARTS), F32),) * CORE_PARTS,
         [VMEM] * 6 + [ANY] + [VMEM] * 4,
         (
-            masks, x, halo_high, sums, all_v, came_low, stages[2],
+            masks, x, halo_high, sums, all_v, came_low, message,
             *totals,
         ),
         "high_tiles",

time: 52.7 us -> 52.3 us (level); the launches traced: 51.8 us -> 52 us
  starting transfers between devices: 22.8 us -> 25.5 us
  waiting for transfers between devices: 10.6 us -> 8.43 us
    ppermute x3, waiting for transfers between devices: 6.79 us -> 1.16 us  [local(): lax.ppermute(everything, 'leaf', [(i, i ^ mask) for i in range(leaf_devic...]
    ppermute x3, starting transfers between devices: 1.84 us -> 5.1 us  [local(): lax.ppermute(everything, 'leaf', [(i, i ^ mask) for i in range(leaf_devic...]
    ppermute x6, waiting for transfers between devices: 2.39 us -> 5.39 us  [over_leaf(): return lax.ppermute(array, ('leaf', 'rhs'), pairs)]
  transfers between devices with their start and end apart: 15 -> 15, of which waited for: 5 -> 8; matrix products, arithmetic and copies ran while one was open for 2% -> 2% of each run, Pallas kernels for 25% -> 25%
where the time goes in v5:
time: 52.3 us; the launch traced here: 52 us
  starting transfers between devices  25.5 us (49%)
  Pallas kernels  13.6 us (26%)
  waiting for transfers between devices  8.43 us (16%)
  local copies, waits for them, and re-layouts  4.14 us (8%)
    ppermute x6, starting transfers between devices, over_leaf(): return lax.ppermute(array, ('leaf', 'rhs'), pairs)  17.6 us
    pallas_call x10, Pallas kernels, call(): pl.pallas_call(body, out_shape=out_shape, in_specs=in_specs, out_specs=ja...  13.6 us
    ppermute x6, waiting for transfers between devices, over_leaf(): return lax.ppermute(array, ('leaf', 'rhs'), pairs)  5.39 us
    ppermute x3, starting transfers between devices, local(): lax.ppermute(everything, 'leaf', [(i, i ^ mask) for i in range(leaf_devic...  5.1 us
    unnamed x24, local copies, waits for them, and re-layouts  2.86 us
    ppermute x6, starting transfers between devices, over_rhs(): lax.ppermute(array, 'rhs', [(i, i ^ mask) for i in range(rhs_devices)])  2.81 us
    ppermute x6, waiting for transfers between devices, over_rhs(): lax.ppermute(array, 'rhs', [(i, i ^ mask) for i in range(rhs_devices)])  1.88 us
    dynamic_slice x1, local copies, waits for them, and re-layouts, local(): chunk_low = lax.dynamic_slice_in_dim(x_late, low * pts, pts, 1)  1.19 us
  transfers between devices with their start and end apart: 15, of which 8 were waited for; matrix products, arithmetic and copies ran while one was open for 2% of the time, Pallas kernels for 25%

profile of v5, /device:TPU:10, one launch (start us, length us, event | category | flops | bytes accessed | tf_op | source)
XLA Modules:
  0.0 52.0 jit_solution(13359103823510226259)
XLA Ops:
  0.0 1.5 %collective-permute-start.1 = (bf16[32,2048]{1,0:T(8,128)(2,1)}, bf16[32,2048]{1,0:T(8,128)(2,1)S(1)}, u32[]{:S(2)}, u32[]{:S(2)}) collective-permute-start(bf16[32,2048]{1,0:T(8,128)(2,1)} %bitcast.19), channel_id=1, source_target_pairs={{0,2},{1,3},{2,0},{3,1},{4,6},{5,7},{6,4},{7,5},{8,10},{9,11},{10,... | collective-permute-start | bytes 393224 | tf_op jit(solution)/shard_map/ppermute | solution.py:360
  1.5 3.1 %pack.1 = (bf16[6,32,128]{2,1,0:T(8,128)(2,1)}, bf16[32,2048]{1,0:T(8,128)(2,1)}) custom-call(bf16[32,2048]{1,0:T(8,128)(2,1)} %bitcast.20, f32[8,64,256]{2,1,0:T(8,128)} %bitcast.17, f32[8,64,64]{2,1,0:T(8,128)} %transfer_ref.1), custom_call_target="tpu_custom_call" | custom-call | flops 2300000000 | tf_op jit(solution)/shard_map/pack/pallas_call | solution.py:324
  5.1 1.2 %constant_dynamic-slice_fusion = (bf16[784,256]{1,0:T(8,128)(2,1)S(1)}, bf16[784,256]{1,0:T(8,128)(2,1)S(1)}) fusion(bf16[784,2048]{1,0:T(8,128)(2,1)} %bitcast.14, s32[]{:T(128)S(6)} %select_n.7, s32[]{:T(128)S(6)} %select_n.6), kind=kLoop, calls=%fused_computation.2 | loop fusion | bytes 1605640 | tf_op jit(solution)/shard_map/dynamic_slice | solution.py:392
  6.3 2.4 %collective-permute-start.6 = (bf16[784,256]{1,0:T(8,128)(2,1)S(1)}, bf16[784,256]{1,0:T(8,128)(2,1)S(1)}, u32[]{:S(2)}, u32[]{:S(2)}) collective-permute-start(bf16[784,256]{1,0:T(8,128)(2,1)S(1)} %get-tuple-element.49), channel_id=1, source_target_pairs={{4,0},{5,1},{6,2},{7,3},{8,4},{9,5},{10,6},{11,7},{12,8},{13,9},{1... | collective-permute-start | bytes 1204232 | tf_op jit(solution)/shard_map/ppermute | solution.py:369
  9.0 0.9 %copy-done.10 = bf16[32,2048]{1,0:T(8,128)(2,1)S(1)} copy-done((bf16[32,2048]{1,0:T(8,128)(2,1)S(1)}, bf16[32,2048]{1,0:T(8,128)(2,1)}, u32[]{:S(2)}) %copy-start.10) | copy-done | bytes 131096
  10.1 1.4 %collective-permute-done.2.odd_ref = bf16[64,2048]{1,0:T(8,128)(2,1)S(1)} collective-permute-done((bf16[64,2048]{1,0:T(8,128)(2,1)S(1)}, bf16[64,2048]{1,0:T(8,128)(2,1)S(1)}, u32[]{:S(2)}, u32[]{:S(2)}) %collective-permute-start.2) | collective-permute-done | bytes 262176 | tf_op jit(solution)/shard_map/ppermute | solution.py:360
  11.5 1.1 %assemble.1 = (bf16[128,2048]{1,0:T(8,128)(2,1)S(1)}, bf16[144,256]{1,0:T(8,128)(2,1)S(1)}, bf16[928,256]{1,0:T(8,128)(2,1)S(1)}, f32[16,1024]{1,0:T(8,128)S(1)}) custom-call(s32[9,8]{1,0:T(8,128)S(1)} %pad_add_fusion.sc_ref, bf16[784,256]{1,0:T(8,128)(2,1)S(1)} %get-tuple-element.50.x_ref, bf16[64,2048]{1,0:T(8,128)(2,1)S(1)} %stack.25.even_ref, ...), custom_call_target="tpu_custom_call" | custom-call | tf_op jit(solution)/shard_map/assemble/pallas_call | solution.py:324
  12.6 4.2 %collective-permute-start.7 = (bf16[144,256]{1,0:T(8,128)(2,1)S(1)}, bf16[144,256]{1,0:T(8,128)(2,1)S(1)}, u32[]{:S(2)}, u32[]{:S(2)}) collective-permute-start(bf16[144,256]{1,0:T(8,128)(2,1)S(1)} %get-tuple-element.34), channel_id=1, source_target_pairs={{4,0},{5,1},{6,2},{7,3},{8,4},{9,5},{10,6},{11,7},{12,8},{13,9},{1... | collective-permute-start | bytes 221192 | tf_op jit(solution)/shard_map/ppermute | solution.py:369
  16.9 2.7 %collective-permute-start.3 = (bf16[2,6,32,128]{3,2,1,0:T(8,128)(2,1)S(1)}, bf16[2,6,32,128]{3,2,1,0:T(8,128)(2,1)S(1)}, u32[]{:S(2)}, u32[]{:S(2)}) collective-permute-start(bf16[2,6,32,128]{3,2,1,0:T(8,128)(2,1)S(1)} %join.2.mine_ref), channel_id=1, source_target_pairs={{0,16},{4,20},{8,24},{12,28},{16,0},{20,4},{24,8},{28,12},{1,17},{... | collective-permute-start | bytes 294920 | tf_op jit(solution)/shard_map/ppermute | solution.py:402
  19.5 1.9 %collective-permute-start.5 = (bf16[928,256]{1,0:T(8,128)(2,1)S(1)}, bf16[928,256]{1,0:T(8,128)(2,1)S(1)}, u32[]{:S(2)}, u32[]{:S(2)}) collective-permute-start(bf16[928,256]{1,0:T(8,128)(2,1)S(1)} %get-tuple-element.32), channel_id=1, source_target_pairs={{0,4},{1,5},{2,6},{3,7},{4,8},{5,9},{6,10},{7,11},{8,12},{9,13},{1... | collective-permute-start | bytes 1425416 | tf_op jit(solution)/shard_map/ppermute | solution.py:369
  21.5 1.3 %collective-permute-done.7.near_ref = bf16[144,256]{1,0:T(8,128)(2,1)S(1)} collective-permute-done((bf16[144,256]{1,0:T(8,128)(2,1)S(1)}, bf16[144,256]{1,0:T(8,128)(2,1)S(1)}, u32[]{:S(2)}, u32[]{:S(2)}) %collective-permute-start.7) | collective-permute-done | bytes 73760 | tf_op jit(solution)/shard_map/ppermute | solution.py:369
  22.8 1.9 %copy-done.1 = bf16[2048,784]{0,1:T(8,128)(2,1)S(1)} copy-done((bf16[2048,784]{0,1:T(8,128)(2,1)S(1)}, bf16[2048,784]{0,1:T(8,128)(2,1)}, u32[]{:S(2)}) %copy-start.1) | copy-done | bytes 3211288
  24.7 4.8 %own_low.1 = (f32[64,1024]{1,0:T(8,128)S(1)}, f32[64,1024]{1,0:T(8,128)S(1)}, f32[64,1024]{1,0:T(8,128)S(1)}, f32[64,1024]{1,0:T(8,128)S(1)}, f32[8,2048]{1,0:T(8,128)S(1)}, /*index=5*/bf16[128,256]{1,0:T(8,128)(2,1)S(1)}) custom-call(f32[16,1024]{1,0:T(8,128)S(1)} %get-tuple-element.31.masks_ref, bf16[784,2048]{1,0:T(8,128)(2,1)S(1)} %bitcast.15, ...), custom_call_target="tpu_custom_call" | custom-call | flops 5750000128 | tf_op jit(solution)/shard_map/own_low/pallas_call | solution.py:324
  29.5 2.1 %collective-permute-start.8 = (bf16[128,256]{1,0:T(8,128)(2,1)S(1)}, bf16[128,256]{1,0:T(8,128)(2,1)S(1)}, u32[]{:S(2)}, u32[]{:S(2)}) collective-permute-start(bf16[128,256]{1,0:T(8,128)(2,1)S(1)} %get-tuple-element.36), channel_id=1, source_target_pairs={{0,4},{1,5},{2,6},{3,7},{4,8},{5,9},{6,10},{7,11},{8,12},{9,13},{1... | collective-permute-start | bytes 196616 | tf_op jit(solution)/shard_map/ppermute | solution.py:369
  31.6 1.9 %collective-permute-start.4 = (bf16[4,6,32,128]{3,2,1,0:T(8,128)(2,1)S(1)}, bf16[4,6,32,128]{3,2,1,0:T(8,128)(2,1)S(1)}, u32[]{:S(2)}, u32[]{:S(2)}) collective-permute-start(bf16[4,6,32,128]{3,2,1,0:T(8,128)(2,1)S(1)} %join.3.mine_ref), channel_id=1, source_target_pairs={{0,4},{4,0},{8,12},{12,8},{16,20},{20,16},{24,28},{28,24},{1,5},{5... | collective-permute-start | bytes 589832 | tf_op jit(solution)/shard_map/ppermute | solution.py:402
  33.5 3.1 %collective-permute-done.8.came_ref = bf16[128,256]{1,0:T(8,128)(2,1)S(1)} collective-permute-done((bf16[128,256]{1,0:T(8,128)(2,1)S(1)}, bf16[128,256]{1,0:T(8,128)(2,1)S(1)}, u32[]{:S(2)}, u32[]{:S(2)}) %collective-permute-start.8) | collective-permute-done | bytes 65568 | tf_op jit(solution)/shard_map/ppermute | solution.py:369
  36.6 1.1 %high_tiles.1 = (f32[64,2304]{1,0:T(8,128)S(1)}, f32[64,768]{1,0:T(8,128)S(1)}, f32[64,768]{1,0:T(8,128)S(1)}, f32[64,768]{1,0:T(8,128)S(1)}) custom-call(f32[16,1024]{1,0:T(8,128)S(1)} %get-tuple-element.31.masks_ref, bf16[784,2048]{1,0:T(8,128)(2,1)S(1)} %bitcast.16, bf16[928,256]{1,0:T(8,128)(2,1)S(1)} %collective-permute-done.5.halo_ref, ...), custom_call_target="tpu_custom_call" | custom-call | flops 11500000256 | tf_op jit(solution)/shard_map/high_tiles/pallas_call | solution.py:324
  38.4 0.9 %collective-permute-done.4.came_ref.unused_ref = bf16[4,6,32,128]{3,2,1,0:T(8,128)(2,1)S(1)} collective-permute-done((bf16[4,6,32,128]{3,2,1,0:T(8,128)(2,1)S(1)}, bf16[4,6,32,128]{3,2,1,0:T(8,128)(2,1)S(1)}, u32[]{:S(2)}, u32[]{:S(2)}) %collective-permute-start.4) | collective-permute-done | bytes 196640 | tf_op jit(solution)/shard_map/ppermute | solution.py:402
  40.0 0.6 %collective-permute-start.12 = (bf16[32,2048]{1,0:T(8,128)(2,1)S(1)}, bf16[32,2048]{1,0:T(8,128)(2,1)S(1)}, u32[]{:S(2)}, u32[]{:S(2)}) collective-permute-start(bf16[32,2048]{1,0:T(8,128)(2,1)S(1)} %get-tuple-element.46), channel_id=1, source_target_pairs={{0,2},{1,3},{2,0},{3,1},{4,6},{5,7},{6,4},{7,5},{8,10},{9,11},{10,... | collective-permute-start | bytes 393224 | tf_op jit(solution)/shard_map/ppermute | solution.py:360
  40.5 3.0 %collective-permute-start.13 = (bf16[32,512]{1,0:T(8,128)(2,1)S(1)}, bf16[32,512]{1,0:T(8,128)(2,1)S(1)}, u32[]{:S(2)}, u32[]{:S(2)}) collective-permute-start(bf16[32,512]{1,0:T(8,128)(2,1)S(1)} %get-tuple-element.47), channel_id=1, source_target_pairs={{4,0},{5,1},{6,2},{7,3},{8,4},{9,5},{10,6},{11,7},{12,8},{13,9},{1... | collective-permute-start | bytes 98312 | tf_op jit(solution)/shard_map/ppermute | solution.py:369
  43.6 3.9 %collective-permute-start.14 = (bf16[32,512]{1,0:T(8,128)(2,1)S(1)}, bf16[32,512]{1,0:T(8,128)(2,1)S(1)}, u32[]{:S(2)}, u32[]{:S(2)}) collective-permute-start(bf16[32,512]{1,0:T(8,128)(2,1)S(1)} %get-tuple-element.48), channel_id=1, source_target_pairs={{4,2},{5,3},{6,0},{7,1},{8,6},{9,7},{10,4},{11,5},{12,10},{13,11},... | collective-permute-start | bytes 98312 | tf_op jit(solution)/shard_map/ppermute | solution.py:369
  47.6 2.6 %far_field.1.far_ref = f32[32,2048]{1,0:T(8,128)S(1)} custom-call(s32[9,8]{1,0:T(8,128)S(1)} %pad_add_fusion.sc_ref, s32[8,8]{1,0:T(8,128)S(1)} %copy-done.8, s32[4,8]{1,0:T(4,128)S(1)} %copy-done.9, bf16[4,6,32,128]{3,2,1,0:T(8,128)(2,1)S(1)} %join.3.mine_ref, bf16[4,6,32,128]{3,2,1,0:T(8,128)(2,1)S(1)} %collective-permute-done.4.came_ref.unused_ref, ...), custom_call_target="tpu_custom_call" | custom-call | flops 3449999872 | tf_op jit(solution)/shard_map/far_field/pallas_call | solution.py:324
  50.3 0.9 %collective-permute-done.14.refs_3_ = bf16[32,512]{1,0:T(8,128)(2,1)S(1)} collective-permute-done((bf16[32,512]{1,0:T(8,128)(2,1)S(1)}, bf16[32,512]{1,0:T(8,128)(2,1)S(1)}, u32[]{:S(2)}, u32[]{:S(2)}) %collective-permute-start.14) | collective-permute-done | bytes 32800 | tf_op jit(solution)/shard_map/ppermute | solution.py:369
  51.2 0.8 %finish.1 = f32[32,2048]{1,0:T(8,128)} custom-call(f32[16,1024]{1,0:T(8,128)S(1)} %get-tuple-element.31.masks_ref, f32[32,2048]{1,0:T(8,128)S(1)} %far_field.1.far_ref, f32[32,2048]{1,0:T(8,128)S(1)} %get-tuple-element.45.refs_0_, bf16[32,2048]{1,0:T(8,128)(2,1)S(1)} %collective-permute-done.12.refs_1_, bf16[32,512]{1,0:T(8,128)(2,1)S(1)} %collective-permute-done.13.refs_2_, ...), custom_call_target="tpu_custom_call" | custom-call | flops 115000000 | tf_op jit(solution)/shard_map/finish/pallas_call | solution.py:324
  (44 shorter events, 2.2 us)
Async XLA Ops:
  0.0 9.0 %collective-permute-start.1 = (bf16[32,2048]{1,0:T(8,128)(2,1)}, bf16[32,2048]{1,0:T(8,128)(2,1)S(1)}, u32[]{:S(2)}, u32[]{:S(2)}) collective-permute-start(bf16[32,2048]{1,0:T(8,128)(2,1)} %bitcast.19), channel_id=1, source_target_pairs={{0,2},{1,3},{2,0},{3,1},{4,6},{5,7},{6,4},{7,5},{8,10},{9,11},{10,... | collective-permute-start | bytes 393224 | tf_op jit(solution)/shard_map/ppermute | solution.py:360
  4.6 4.4 %collective-permute-start = (bf16[1,6,32,128]{3,2,1,0:T(8,128)(2,1)}, bf16[1,6,32,128]{3,2,1,0:T(8,128)(2,1)S(1)}, u32[]{:S(2)}, u32[]{:S(2)}) collective-permute-start(bf16[1,6,32,128]{3,2,1,0:T(8,128)(2,1)} %bitcast.12), channel_id=1, source_target_pairs={{0,8},{4,12},{8,0},{12,4},{16,24},{20,28},{24,16},{28,20},{1,9},{5... | collective-permute-start | bytes 147464 | tf_op jit(solution)/shard_map/ppermute | solution.py:402
  5.1 11.7 %copy-start = (bf16[6,32,128]{2,1,0:T(8,128)(2,1)S(1)}, bf16[6,32,128]{2,1,0:T(8,128)(2,1)}, u32[]{:S(2)}) copy-start(bf16[6,32,128]{2,1,0:T(8,128)(2,1)} %get-tuple-element.29.after_ref.unused_ref) | copy-start | bytes 147460
  6.3 15.1 %collective-permute-start.6 = (bf16[784,256]{1,0:T(8,128)(2,1)S(1)}, bf16[784,256]{1,0:T(8,128)(2,1)S(1)}, u32[]{:S(2)}, u32[]{:S(2)}) collective-permute-start(bf16[784,256]{1,0:T(8,128)(2,1)S(1)} %get-tuple-element.49), channel_id=1, source_target_pairs={{4,0},{5,1},{6,2},{7,3},{8,4},{9,5},{10,6},{11,7},{12,8},{13,9},{1... | collective-permute-start | bytes 1204232 | tf_op jit(solution)/shard_map/ppermute | solution.py:369
  9.9 1.6 %collective-permute-start.2 = (bf16[64,2048]{1,0:T(8,128)(2,1)S(1)}, bf16[64,2048]{1,0:T(8,128)(2,1)S(1)}, u32[]{:S(2)}, u32[]{:S(2)}) collective-permute-start(bf16[64,2048]{1,0:T(8,128)(2,1)S(1)} %stack.25.even_ref), channel_id=1, source_target_pairs={{0,1},{1,0},{2,3},{3,2},{4,5},{5,4},{6,7},{7,6},{8,9},{9,8},{10,11... | collective-permute-start | bytes 786440 | tf_op jit(solution)/shard_map/ppermute | solution.py:360
  12.6 10.2 %collective-permute-start.7 = (bf16[144,256]{1,0:T(8,128)(2,1)S(1)}, bf16[144,256]{1,0:T(8,128)(2,1)S(1)}, u32[]{:S(2)}, u32[]{:S(2)}) collective-permute-start(bf16[144,256]{1,0:T(8,128)(2,1)S(1)} %get-tuple-element.34), channel_id=1, source_target_pairs={{4,0},{5,1},{6,2},{7,3},{8,4},{9,5},{10,6},{11,7},{12,8},{13,9},{1... | collective-permute-start | bytes 221192 | tf_op jit(solution)/shard_map/ppermute | solution.py:369
  16.9 14.7 %collective-permute-start.3 = (bf16[2,6,32,128]{3,2,1,0:T(8,128)(2,1)S(1)}, bf16[2,6,32,128]{3,2,1,0:T(8,128)(2,1)S(1)}, u32[]{:S(2)}, u32[]{:S(2)}) collective-permute-start(bf16[2,6,32,128]{3,2,1,0:T(8,128)(2,1)S(1)} %join.2.mine_ref), channel_id=1, source_target_pairs={{0,16},{4,20},{8,24},{12,28},{16,0},{20,4},{24,8},{28,12},{1,17},{... | collective-permute-start | bytes 294920 | tf_op jit(solution)/shard_map/ppermute | solution.py:402
  19.5 17.1 %collective-permute-start.5 = (bf16[928,256]{1,0:T(8,128)(2,1)S(1)}, bf16[928,256]{1,0:T(8,128)(2,1)S(1)}, u32[]{:S(2)}, u32[]{:S(2)}) collective-permute-start(bf16[928,256]{1,0:T(8,128)(2,1)S(1)} %get-tuple-element.32), channel_id=1, source_target_pairs={{0,4},{1,5},{2,6},{3,7},{4,8},{5,9},{6,10},{7,11},{8,12},{9,13},{1... | collective-permute-start | bytes 1425416 | tf_op jit(solution)/shard_map/ppermute | solution.py:369
  24.7 11.9 %copy-start.2 = (bf16[2048,784]{0,1:T(8,128)(2,1)S(1)}, bf16[2048,784]{0,1:T(8,128)(2,1)}, u32[]{:S(2)}) copy-start(bf16[2048,784]{0,1:T(8,128)(2,1)} %param.9) | copy-start | bytes 9633796
  29.5 7.1 %collective-permute-start.8 = (bf16[128,256]{1,0:T(8,128)(2,1)S(1)}, bf16[128,256]{1,0:T(8,128)(2,1)S(1)}, u32[]{:S(2)}, u32[]{:S(2)}) collective-permute-start(bf16[128,256]{1,0:T(8,128)(2,1)S(1)} %get-tuple-element.36), channel_id=1, source_target_pairs={{0,4},{1,5},{2,6},{3,7},{4,8},{5,9},{6,10},{7,11},{8,12},{9,13},{1... | collective-permute-start | bytes 196616 | tf_op jit(solution)/shard_map/ppermute | solution.py:369
  31.6 7.8 %collective-permute-start.4 = (bf16[4,6,32,128]{3,2,1,0:T(8,128)(2,1)S(1)}, bf16[4,6,32,128]{3,2,1,0:T(8,128)(2,1)S(1)}, u32[]{:S(2)}, u32[]{:S(2)}) collective-permute-start(bf16[4,6,32,128]{3,2,1,0:T(8,128)(2,1)S(1)} %join.3.mine_ref), channel_id=1, source_target_pairs={{0,4},{4,0},{8,12},{12,8},{16,20},{20,16},{24,28},{28,24},{1,5},{5... | collective-permute-start | bytes 589832 | tf_op jit(solution)/shard_map/ppermute | solution.py:402
  37.8 1.6 %collective-permute-start.10 = (f32[64,768]{1,0:T(8,128)S(1)}, f32[64,768]{1,0:T(8,128)S(1)}, u32[]{:S(2)}, u32[]{:S(2)}) collective-permute-start(f32[64,768]{1,0:T(8,128)S(1)} %get-tuple-element.43), channel_id=1, source_target_pairs={{0,1},{1,0},{2,3},{3,2},{4,5},{5,4},{6,7},{7,6},{8,9},{9,8},{10,11... | collective-permute-start | bytes 589832 | tf_op jit(solution)/shard_map/ppermute | solution.py:360
  37.9 1.7 %collective-permute-start.11 = (f32[64,768]{1,0:T(8,128)S(1)}, f32[64,768]{1,0:T(8,128)S(1)}, u32[]{:S(2)}, u32[]{:S(2)}) collective-permute-start(f32[64,768]{1,0:T(8,128)S(1)} %get-tuple-element.44), channel_id=1, source_target_pairs={{0,1},{1,0},{2,3},{3,2},{4,5},{5,4},{6,7},{7,6},{8,9},{9,8},{10,11... | collective-permute-start | bytes 589832 | tf_op jit(solution)/shard_map/ppermute | solution.py:360
  38.4 1.5 %collective-permute-start.9 = (f32[64,768]{1,0:T(8,128)S(1)}, f32[64,768]{1,0:T(8,128)S(1)}, u32[]{:S(2)}, u32[]{:S(2)}) collective-permute-start(f32[64,768]{1,0:T(8,128)S(1)} %get-tuple-element.42), channel_id=1, source_target_pairs={{0,1},{1,0},{2,3},{3,2},{4,5},{5,4},{6,7},{7,6},{8,9},{9,8},{10,11... | collective-permute-start | bytes 589832 | tf_op jit(solution)/shard_map/ppermute | solution.py:360
  39.9 7.7 %copy-start.3 = (f32[8,8,64,64]{3,2,1,0:T(8,128)S(1)}, f32[8,8,64,64]{3,2,1,0:T(8,128)}, u32[]{:S(2)}) copy-start(f32[8,8,64,64]{3,2,1,0:T(8,128)} %coupling_ref.1) | copy-start | bytes 3145732
  39.9 7.7 %copy-start.4 = (f32[4,8,64,64]{3,2,1,0:T(8,128)S(1)}, f32[4,8,64,64]{3,2,1,0:T(8,128)}, u32[]{:S(2)}) copy-start(f32[4,8,64,64]{3,2,1,0:T(8,128)} %up_ref.1) | copy-start | bytes 1572868
  39.9 7.7 %copy-start.5 = (f32[8,256,64]{1,2,0:T(8,128)S(1)}, f32[8,256,64]{1,2,0:T(8,128)}, u32[]{:S(2)}) copy-start(f32[8,256,64]{1,2,0:T(8,128)} %param.11) | copy-start | bytes 1572868
  39.9 7.7 %copy-start.6 = (f32[8,64,64]{2,1,0:T(8,128)S(1)}, f32[8,64,64]{2,1,0:T(8,128)}, u32[]{:S(2)}) copy-start(f32[8,64,64]{2,1,0:T(8,128)} %transfer_ref.1) | copy-start | bytes 393220
  39.9 7.7 %copy-start.7 = (bf16[2048,32]{0,1:T(8,128)(2,1)S(1)}, bf16[2048,32]{0,1:T(8,128)(2,1)}, u32[]{:S(2)}) copy-start(bf16[2048,32]{0,1:T(8,128)(2,1)} %param.10) | copy-start | bytes 393220
  39.9 7.7 %copy-start.8 = (s32[8,8]{1,0:T(8,128)S(1)}, s32[8,8]{1,0:T(8,128)}, u32[]{:S(2)}) copy-start(s32[8,8]{1,0:T(8,128)} %far_leaf_ref.1) | copy-start | bytes 772
  39.9 7.7 %copy-start.9 = (s32[4,8]{1,0:T(4,128)S(1)}, s32[4,8]{1,0:T(4,128)}, u32[]{:S(2)}) copy-start(s32[4,8]{1,0:T(4,128)} %far_up_ref.1) | copy-start | bytes 388
  40.0 11.2 %collective-permute-start.12 = (bf16[32,2048]{1,0:T(8,128)(2,1)S(1)}, bf16[32,2048]{1,0:T(8,128)(2,1)S(1)}, u32[]{:S(2)}, u32[]{:S(2)}) collective-permute-start(bf16[32,2048]{1,0:T(8,128)(2,1)S(1)} %get-tuple-element.46), channel_id=1, source_target_pairs={{0,2},{1,3},{2,0},{3,1},{4,6},{5,7},{6,4},{7,5},{8,10},{9,11},{10,... | collective-permute-start | bytes 393224 | tf_op jit(solution)/shard_map/ppermute | solution.py:360
  40.5 9.7 %collective-permute-start.13 = (bf16[32,512]{1,0:T(8,128)(2,1)S(1)}, bf16[32,512]{1,0:T(8,128)(2,1)S(1)}, u32[]{:S(2)}, u32[]{:S(2)}) collective-permute-start(bf16[32,512]{1,0:T(8,128)(2,1)S(1)} %get-tuple-element.47), channel_id=1, source_target_pairs={{4,0},{5,1},{6,2},{7,3},{8,4},{9,5},{10,6},{11,7},{12,8},{13,9},{1... | collective-permute-start | bytes 98312 | tf_op jit(solution)/shard_map/ppermute | solution.py:369
  43.6 7.6 %collective-permute-start.14 = (bf16[32,512]{1,0:T(8,128)(2,1)S(1)}, bf16[32,512]{1,0:T(8,128)(2,1)S(1)}, u32[]{:S(2)}, u32[]{:S(2)}) collective-permute-start(bf16[32,512]{1,0:T(8,128)(2,1)S(1)} %get-tuple-element.48), channel_id=1, source_target_pairs={{4,2},{5,3},{6,0},{7,1},{8,6},{9,7},{10,4},{11,5},{12,10},{13,11},... | collective-permute-start | bytes 98312 | tf_op jit(solution)/shard_map/ppermute | solution.py:369
  (3 other events, 8.3 us)

commit v6 on v5

--- a/solution.py
+++ b/solution.py
@@ -12,6 +12,7 @@
 LOG2E = math.log2(math.e)
 FLAG_ROWS = 16
 CORE_PARTS = 3
+V_PARTS = 2
 PACK_LIMIT = 58
 F32 = jnp.float32
 BF16 = jnp.bfloat16
@@ -91,12 +92,16 @@
 
 
 def assemble_kernel(
-    leaves, sc_ref, x_ref, even_ref, odd_ref, v_ref, down_ref, up_ref, masks_ref
+    leaves, sc_ref, x_ref, *refs
 ):
+    piece_refs, (v_ref, down_ref, up_ref, masks_ref) = refs[:-4], refs[-4:]
     features, pts = x_ref.shape
     rows = v_ref.shape[0]
-    v_ref[: rows // 2] = even_ref[...]
-    v_ref[rows // 2 :] = odd_ref[...]
+    size = v_ref.shape[1] // V_PARTS
+    for part in range(V_PARTS):
+        here = slice(part * size, (part + 1) * size)
+        v_ref[: rows // 2, here] = piece_refs[part][...]
+        v_ref[rows // 2 :, here] = piece_refs[V_PARTS + part][...]
     low, upper, base = sc_ref[0, 0], sc_ref[0, 2], sc_ref[0, 3]
 
     def flags(leaf, first):
@@ -133,11 +138,14 @@
 
 
 def stack_kernel(unused_ref, *refs):
-    out_ref = refs[-1]
-    first = 0
-    for ref in refs[:-1]:
-        out_ref[first : first + ref.shape[0]] = ref[...]
-        first += ref.shape[0]
+    ins, outs = refs[:-V_PARTS], refs[-V_PARTS:]
+    size = outs[0].shape[1]
+    for part, out_ref in enumerate(outs):
+        first = 0
+        for ref in ins:
+            rows = slice(first, first + ref.shape[0])
+            out_ref[rows] = ref[:, part * size : (part + 1) * size]
+            first += ref.shape[0]
 
 
 def row_sums(x, features):
@@ -415,12 +423,12 @@
 
     even_v = call(
         stack_kernel,
-        shape((rows // 2, leaves * pts), BF16),
+        (shape((rows // 2, leaves * pts // V_PARTS), BF16),) * V_PARTS,
         [ANY] + [VMEM] * (1 + len(others)),
         (stages[1], v_here, *others),
         "stack",
     )
-    odd_v = over_rhs(even_v, 1)
+    odd_v = [over_rhs(part, 1) for part in even_v]
     all_v, down, up, masks = call(
         functools.partial(assemble_kernel, leaves),
         (
@@ -429,8 +437,8 @@
             shape((features + rows + FLAG_ROWS, pts), BF16),
             shape((12 + half, wide), F32),
         ),
-        [SMEM] + [VMEM] * 3,
-        (scalars, chunk_up, even_v, odd_v),
+        [SMEM] + [VMEM] * (1 + 2 * V_PARTS),
+        (scalars, chunk_up, *even_v, *odd_v),
         "assemble",
     )
 

time: 52.3 us -> 52.7 us (level)
  waiting for transfers between devices: 8.43 us -> 11 us
  local copies, waits for them, and re-layouts: 4.14 us -> 2.38 us
    ppermute x6, waiting for transfers between devices: 5.39 us -> 8.45 us  [over_leaf(): return lax.ppermute(array, ('leaf', 'rhs'), pairs)]
    unnamed x24 -> x22, local copies, waits for them, and re-layouts: 2.86 us -> 1.1 us
    ppermute x6 -> x7, waiting for transfers between devices: 1.88 us -> 1.26 us  [over_rhs(): lax.ppermute(array, 'rhs', [(i, i ^ mask) for i in range(rhs_devices)])]
    ppermute x6 -> x7, starting transfers between devices: 2.81 us -> 3.3 us  [over_rhs(): lax.ppermute(array, 'rhs', [(i, i ^ mask) for i in range(rhs_devices)])]
  transfers between devices with their start and end apart: 15 -> 16, of which waited for: 8 -> 8; matrix products, arithmetic and copies ran while one was open for 2% -> 2% of each run, Pallas kernels for 25% -> 24%
where the time goes in v6:
time: 52.7 us; the launch traced here: 52.4 us
  starting transfers between devices  25.1 us (48%)
  Pallas kernels  13.6 us (26%)
  waiting for transfers between devices  11 us (21%)
  local copies, waits for them, and re-layouts  2.38 us (5%)
    ppermute x6, starting transfers between devices, over_leaf(): return lax.ppermute(array, ('leaf', 'rhs'), pairs)  17.1 us
    pallas_call x10, Pallas kernels, call(): pl.pallas_call(body, out_shape=out_shape, in_specs=in_specs, out_specs=ja...  13.6 us
    ppermute x6, waiting for transfers between devices, over_leaf(): return lax.ppermute(array, ('leaf', 'rhs'), pairs)  8.45 us
    ppermute x3, starting transfers between devices, local(): lax.ppermute(everything, 'leaf', [(i, i ^ mask) for i in range(leaf_devic...  4.69 us
    ppermute x7, starting transfers between devices, over_rhs(): lax.ppermute(array, 'rhs', [(i, i ^ mask) for i in range(rhs_devices)])  3.3 us
    ppermute x3, waiting for transfers between devices, local(): lax.ppermute(everything, 'leaf', [(i, i ^ mask) for i in range(leaf_devic...  1.28 us
    ppermute x7, waiting for transfers between devices, over_rhs(): lax.ppermute(array, 'rhs', [(i, i ^ mask) for i in range(rhs_devices)])  1.26 us
    dynamic_slice x1, local copies, waits for them, and re-layouts, local(): chunk_low = lax.dynamic_slice_in_dim(x_late, low * pts, pts, 1)  1.19 us
  transfers between devices with their start and end apart: 16, of which 8 were waited for; matrix products, arithmetic and copies ran while one was open for 2% of the time, Pallas kernels for 24%

profile of v6, /device:TPU:10, one launch (start us, length us, event | category | flops | bytes accessed | tf_op | source)
XLA Modules:
  0.0 52.4 jit_solution(13460992445364360600)
XLA Ops:
  0.0 1.5 %collective-permute-start.1 = (bf16[32,2048]{1,0:T(8,128)(2,1)}, bf16[32,2048]{1,0:T(8,128)(2,1)S(1)}, u32[]{:S(2)}, u32[]{:S(2)}) collective-permute-start(bf16[32,2048]{1,0:T(8,128)(2,1)} %bitcast.19), channel_id=1, source_target_pairs={{0,2},{1,3},{2,0},{3,1},{4,6},{5,7},{6,4},{7,5},{8,10},{9,11},{10,... | collective-permute-start | bytes 393224 | tf_op jit(solution)/shard_map/ppermute | solution.py:368
  1.5 3.1 %pack.1 = (bf16[6,32,128]{2,1,0:T(8,128)(2,1)}, bf16[32,2048]{1,0:T(8,128)(2,1)}) custom-call(bf16[32,2048]{1,0:T(8,128)(2,1)} %bitcast.20, f32[8,64,256]{2,1,0:T(8,128)} %bitcast.17, f32[8,64,64]{2,1,0:T(8,128)} %transfer_ref.1), custom_call_target="tpu_custom_call" | custom-call | flops 2300000000 | tf_op jit(solution)/shard_map/pack/pallas_call | solution.py:332
  4.6 0.5 collective-permute-start
  5.1 1.2 %constant_dynamic-slice_fusion = (bf16[784,256]{1,0:T(8,128)(2,1)S(1)}, bf16[784,256]{1,0:T(8,128)(2,1)S(1)}) fusion(bf16[784,2048]{1,0:T(8,128)(2,1)} %bitcast.14, s32[]{:T(128)S(6)} %select_n.7, s32[]{:T(128)S(6)} %select_n.6), kind=kLoop, calls=%fused_computation.2 | loop fusion | bytes 1605640 | tf_op jit(solution)/shard_map/dynamic_slice | solution.py:400
  6.3 2.4 %collective-permute-start.7 = (bf16[784,256]{1,0:T(8,128)(2,1)S(1)}, bf16[784,256]{1,0:T(8,128)(2,1)S(1)}, u32[]{:S(2)}, u32[]{:S(2)}) collective-permute-start(bf16[784,256]{1,0:T(8,128)(2,1)S(1)} %get-tuple-element.53), channel_id=1, source_target_pairs={{4,0},{5,1},{6,2},{7,3},{8,4},{9,5},{10,6},{11,7},{12,8},{13,9},{1... | collective-permute-start | bytes 1204232 | tf_op jit(solution)/shard_map/ppermute | solution.py:377
  9.0 1.1 %copy-done.9 = bf16[32,2048]{1,0:T(8,128)(2,1)S(1)} copy-done((bf16[32,2048]{1,0:T(8,128)(2,1)S(1)}, bf16[32,2048]{1,0:T(8,128)(2,1)}, u32[]{:S(2)}) %copy-start.9) | copy-done | bytes 131096
  10.7 0.8 %collective-permute-done.2.refs_2_ = bf16[64,1024]{1,0:T(8,128)(2,1)S(1)} collective-permute-done((bf16[64,1024]{1,0:T(8,128)(2,1)S(1)}, bf16[64,1024]{1,0:T(8,128)(2,1)S(1)}, u32[]{:S(2)}, u32[]{:S(2)}) %collective-permute-start.2) | collective-permute-done | bytes 131104 | tf_op jit(solution)/shard_map/ppermute | solution.py:368
  11.7 1.1 %assemble.1 = (bf16[128,2048]{1,0:T(8,128)(2,1)S(1)}, bf16[144,256]{1,0:T(8,128)(2,1)S(1)}, bf16[928,256]{1,0:T(8,128)(2,1)S(1)}, f32[16,1024]{1,0:T(8,128)S(1)}) custom-call(s32[9,8]{1,0:T(8,128)S(1)} %pad_add_fusion.sc_ref, bf16[784,256]{1,0:T(8,128)(2,1)S(1)} %get-tuple-element.54.x_ref, bf16[64,1024]{1,0:T(8,128)(2,1)S(1)} %get-tuple-element.33.refs_0_, ...), custom_call_target="tpu_custom_call" | custom-call | tf_op jit(solution)/shard_map/assemble/pallas_call | solution.py:332
  12.8 4.3 %collective-permute-start.8 = (bf16[144,256]{1,0:T(8,128)(2,1)S(1)}, bf16[144,256]{1,0:T(8,128)(2,1)S(1)}, u32[]{:S(2)}, u32[]{:S(2)}) collective-permute-start(bf16[144,256]{1,0:T(8,128)(2,1)S(1)} %get-tuple-element.38), channel_id=1, source_target_pairs={{4,0},{5,1},{6,2},{7,3},{8,4},{9,5},{10,6},{11,7},{12,8},{13,9},{1... | collective-permute-start | bytes 221192 | tf_op jit(solution)/shard_map/ppermute | solution.py:377
  17.1 2.7 %collective-permute-start.4 = (bf16[2,6,32,128]{3,2,1,0:T(8,128)(2,1)S(1)}, bf16[2,6,32,128]{3,2,1,0:T(8,128)(2,1)S(1)}, u32[]{:S(2)}, u32[]{:S(2)}) collective-permute-start(bf16[2,6,32,128]{3,2,1,0:T(8,128)(2,1)S(1)} %join.2.mine_ref), channel_id=1, source_target_pairs={{0,16},{4,20},{8,24},{12,28},{16,0},{20,4},{24,8},{28,12},{1,17},{... | collective-permute-start | bytes 294920 | tf_op jit(solution)/shard_map/ppermute | solution.py:410
  19.8 1.9 %collective-permute-start.6 = (bf16[928,256]{1,0:T(8,128)(2,1)S(1)}, bf16[928,256]{1,0:T(8,128)(2,1)S(1)}, u32[]{:S(2)}, u32[]{:S(2)}) collective-permute-start(bf16[928,256]{1,0:T(8,128)(2,1)S(1)} %get-tuple-element.36), channel_id=1, source_target_pairs={{0,4},{1,5},{2,6},{3,7},{4,8},{5,9},{6,10},{7,11},{8,12},{9,13},{1... | collective-permute-start | bytes 1425416 | tf_op jit(solution)/shard_map/ppermute | solution.py:377
  21.7 0.7 %collective-permute-done.8.near_ref = bf16[144,256]{1,0:T(8,128)(2,1)S(1)} collective-permute-done((bf16[144,256]{1,0:T(8,128)(2,1)S(1)}, bf16[144,256]{1,0:T(8,128)(2,1)S(1)}, u32[]{:S(2)}, u32[]{:S(2)}) %collective-permute-start.8) | collective-permute-done | bytes 73760 | tf_op jit(solution)/shard_map/ppermute | solution.py:377
  22.4 4.8 %own_low.1 = (f32[64,1024]{1,0:T(8,128)S(1)}, f32[64,1024]{1,0:T(8,128)S(1)}, f32[64,1024]{1,0:T(8,128)S(1)}, f32[64,1024]{1,0:T(8,128)S(1)}, f32[8,2048]{1,0:T(8,128)S(1)}, /*index=5*/bf16[128,256]{1,0:T(8,128)(2,1)S(1)}) custom-call(f32[16,1024]{1,0:T(8,128)S(1)} %get-tuple-element.35.masks_ref, bf16[784,2048]{1,0:T(8,128)(2,1)S(1)} %bitcast.15, ...), custom_call_target="tpu_custom_call" | custom-call | flops 5750000128 | tf_op jit(solution)/shard_map/own_low/pallas_call | solution.py:332
  27.2 2.5 %collective-permute-start.9 = (bf16[128,256]{1,0:T(8,128)(2,1)S(1)}, bf16[128,256]{1,0:T(8,128)(2,1)S(1)}, u32[]{:S(2)}, u32[]{:S(2)}) collective-permute-start(bf16[128,256]{1,0:T(8,128)(2,1)S(1)} %get-tuple-element.40), channel_id=1, source_target_pairs={{0,4},{1,5},{2,6},{3,7},{4,8},{5,9},{6,10},{7,11},{8,12},{9,13},{1... | collective-permute-start | bytes 196616 | tf_op jit(solution)/shard_map/ppermute | solution.py:377
  29.7 1.5 %collective-permute-start.5 = (bf16[4,6,32,128]{3,2,1,0:T(8,128)(2,1)S(1)}, bf16[4,6,32,128]{3,2,1,0:T(8,128)(2,1)S(1)}, u32[]{:S(2)}, u32[]{:S(2)}) collective-permute-start(bf16[4,6,32,128]{3,2,1,0:T(8,128)(2,1)S(1)} %join.3.mine_ref), channel_id=1, source_target_pairs={{0,4},{4,0},{8,12},{12,8},{16,20},{20,16},{24,28},{28,24},{1,5},{5... | collective-permute-start | bytes 589832 | tf_op jit(solution)/shard_map/ppermute | solution.py:410
  31.2 5.6 %collective-permute-done.9.came_ref = bf16[128,256]{1,0:T(8,128)(2,1)S(1)} collective-permute-done((bf16[128,256]{1,0:T(8,128)(2,1)S(1)}, bf16[128,256]{1,0:T(8,128)(2,1)S(1)}, u32[]{:S(2)}, u32[]{:S(2)}) %collective-permute-start.9) | collective-permute-done | bytes 65568 | tf_op jit(solution)/shard_map/ppermute | solution.py:377
  36.8 1.2 %high_tiles.1 = (f32[64,2304]{1,0:T(8,128)S(1)}, f32[64,768]{1,0:T(8,128)S(1)}, f32[64,768]{1,0:T(8,128)S(1)}, f32[64,768]{1,0:T(8,128)S(1)}) custom-call(f32[16,1024]{1,0:T(8,128)S(1)} %get-tuple-element.35.masks_ref, bf16[784,2048]{1,0:T(8,128)(2,1)S(1)} %bitcast.16, bf16[928,256]{1,0:T(8,128)(2,1)S(1)} %collective-permute-done.6.halo_ref, ...), custom_call_target="tpu_custom_call" | custom-call | flops 11500000256 | tf_op jit(solution)/shard_map/high_tiles/pallas_call | solution.py:332
  38.6 1.2 %collective-permute-done.5.came_ref.unused_ref = bf16[4,6,32,128]{3,2,1,0:T(8,128)(2,1)S(1)} collective-permute-done((bf16[4,6,32,128]{3,2,1,0:T(8,128)(2,1)S(1)}, bf16[4,6,32,128]{3,2,1,0:T(8,128)(2,1)S(1)}, u32[]{:S(2)}, u32[]{:S(2)}) %collective-permute-start.5) | collective-permute-done | bytes 196640 | tf_op jit(solution)/shard_map/ppermute | solution.py:410
  40.2 0.6 %collective-permute-start.13 = (bf16[32,2048]{1,0:T(8,128)(2,1)S(1)}, bf16[32,2048]{1,0:T(8,128)(2,1)S(1)}, u32[]{:S(2)}, u32[]{:S(2)}) collective-permute-start(bf16[32,2048]{1,0:T(8,128)(2,1)S(1)} %get-tuple-element.50), channel_id=1, source_target_pairs={{0,2},{1,3},{2,0},{3,1},{4,6},{5,7},{6,4},{7,5},{8,10},{9,11},{10,... | collective-permute-start | bytes 393224 | tf_op jit(solution)/shard_map/ppermute | solution.py:368
  40.7 3.3 %collective-permute-start.14 = (bf16[32,512]{1,0:T(8,128)(2,1)S(1)}, bf16[32,512]{1,0:T(8,128)(2,1)S(1)}, u32[]{:S(2)}, u32[]{:S(2)}) collective-permute-start(bf16[32,512]{1,0:T(8,128)(2,1)S(1)} %get-tuple-element.51), channel_id=1, source_target_pairs={{4,0},{5,1},{6,2},{7,3},{8,4},{9,5},{10,6},{11,7},{12,8},{13,9},{1... | collective-permute-start | bytes 98312 | tf_op jit(solution)/shard_map/ppermute | solution.py:377
  44.0 2.7 %collective-permute-start.15 = (bf16[32,512]{1,0:T(8,128)(2,1)S(1)}, bf16[32,512]{1,0:T(8,128)(2,1)S(1)}, u32[]{:S(2)}, u32[]{:S(2)}) collective-permute-start(bf16[32,512]{1,0:T(8,128)(2,1)S(1)} %get-tuple-element.52), channel_id=1, source_target_pairs={{4,2},{5,3},{6,0},{7,1},{8,6},{9,7},{10,4},{11,5},{12,10},{13,11},... | collective-permute-start | bytes 98312 | tf_op jit(solution)/shard_map/ppermute | solution.py:377
  46.8 2.6 %far_field.1.far_ref = f32[32,2048]{1,0:T(8,128)S(1)} custom-call(s32[9,8]{1,0:T(8,128)S(1)} %pad_add_fusion.sc_ref, s32[8,8]{1,0:T(8,128)S(1)} %copy-done.7, s32[4,8]{1,0:T(4,128)S(1)} %copy-done.8, bf16[4,6,32,128]{3,2,1,0:T(8,128)(2,1)S(1)} %join.3.mine_ref, bf16[4,6,32,128]{3,2,1,0:T(8,128)(2,1)S(1)} %collective-permute-done.5.came_ref.unused_ref, ...), custom_call_target="tpu_custom_call" | custom-call | flops 3449999872 | tf_op jit(solution)/shard_map/far_field/pallas_call | solution.py:332
  49.5 2.1 %collective-permute-done.15.refs_3_ = bf16[32,512]{1,0:T(8,128)(2,1)S(1)} collective-permute-done((bf16[32,512]{1,0:T(8,128)(2,1)S(1)}, bf16[32,512]{1,0:T(8,128)(2,1)S(1)}, u32[]{:S(2)}, u32[]{:S(2)}) %collective-permute-start.15) | collective-permute-done | bytes 32800 | tf_op jit(solution)/shard_map/ppermute | solution.py:377
  51.6 0.8 %finish.1 = f32[32,2048]{1,0:T(8,128)} custom-call(f32[16,1024]{1,0:T(8,128)S(1)} %get-tuple-element.35.masks_ref, f32[32,2048]{1,0:T(8,128)S(1)} %far_field.1.far_ref, f32[32,2048]{1,0:T(8,128)S(1)} %get-tuple-element.49.refs_0_, bf16[32,2048]{1,0:T(8,128)(2,1)S(1)} %collective-permute-done.13.refs_1_, bf16[32,512]{1,0:T(8,128)(2,1)S(1)} %collective-permute-done.14.refs_2_, ...), custom_call_target="tpu_custom_call" | custom-call | flops 115000000 | tf_op jit(solution)/shard_map/finish/pallas_call | solution.py:332
  (44 shorter events, 2.0 us)
Async XLA Ops:
  0.0 9.0 %collective-permute-start.1 = (bf16[32,2048]{1,0:T(8,128)(2,1)}, bf16[32,2048]{1,0:T(8,128)(2,1)S(1)}, u32[]{:S(2)}, u32[]{:S(2)}) collective-permute-start(bf16[32,2048]{1,0:T(8,128)(2,1)} %bitcast.19), channel_id=1, source_target_pairs={{0,2},{1,3},{2,0},{3,1},{4,6},{5,7},{6,4},{7,5},{8,10},{9,11},{10,... | collective-permute-start | bytes 393224 | tf_op jit(solution)/shard_map/ppermute | solution.py:368
  4.6 4.4 %collective-permute-start = (bf16[1,6,32,128]{3,2,1,0:T(8,128)(2,1)}, bf16[1,6,32,128]{3,2,1,0:T(8,128)(2,1)S(1)}, u32[]{:S(2)}, u32[]{:S(2)}) collective-permute-start(bf16[1,6,32,128]{3,2,1,0:T(8,128)(2,1)} %bitcast.12), channel_id=1, source_target_pairs={{0,8},{4,12},{8,0},{12,4},{16,24},{20,28},{24,16},{28,20},{1,9},{5... | collective-permute-start | bytes 147464 | tf_op jit(solution)/shard_map/ppermute | solution.py:410
  5.1 12.0 %copy-start = (bf16[6,32,128]{2,1,0:T(8,128)(2,1)S(1)}, bf16[6,32,128]{2,1,0:T(8,128)(2,1)}, u32[]{:S(2)}) copy-start(bf16[6,32,128]{2,1,0:T(8,128)(2,1)} %get-tuple-element.31.after_ref.unused_ref) | copy-start | bytes 147460
  6.3 16.1 %collective-permute-start.7 = (bf16[784,256]{1,0:T(8,128)(2,1)S(1)}, bf16[784,256]{1,0:T(8,128)(2,1)S(1)}, u32[]{:S(2)}, u32[]{:S(2)}) collective-permute-start(bf16[784,256]{1,0:T(8,128)(2,1)S(1)} %get-tuple-element.53), channel_id=1, source_target_pairs={{4,0},{5,1},{6,2},{7,3},{8,4},{9,5},{10,6},{11,7},{12,8},{13,9},{1... | collective-permute-start | bytes 1204232 | tf_op jit(solution)/shard_map/ppermute | solution.py:377
  8.9 13.5 %copy-start.1 = (bf16[2048,784]{0,1:T(8,128)(2,1)S(1)}, bf16[2048,784]{0,1:T(8,128)(2,1)}, u32[]{:S(2)}) copy-start(bf16[2048,784]{0,1:T(8,128)(2,1)} %param.9) | copy-start | bytes 9633796
  10.1 1.4 %collective-permute-start.2 = (bf16[64,1024]{1,0:T(8,128)(2,1)S(1)}, bf16[64,1024]{1,0:T(8,128)(2,1)S(1)}, u32[]{:S(2)}, u32[]{:S(2)}) collective-permute-start(bf16[64,1024]{1,0:T(8,128)(2,1)S(1)} %get-tuple-element.33.refs_0_), channel_id=1, source_target_pairs={{0,1},{1,0},{2,3},{3,2},{4,5},{5,4},{6,7},{7,6},{8,9},{9,8},{10,11... | collective-permute-start | bytes 393224 | tf_op jit(solution)/shard_map/ppermute | solution.py:368
  10.1 1.5 %collective-permute-start.3 = (bf16[64,1024]{1,0:T(8,128)(2,1)S(1)}, bf16[64,1024]{1,0:T(8,128)(2,1)S(1)}, u32[]{:S(2)}, u32[]{:S(2)}) collective-permute-start(bf16[64,1024]{1,0:T(8,128)(2,1)S(1)} %get-tuple-element.34.refs_1_), channel_id=1, source_target_pairs={{0,1},{1,0},{2,3},{3,2},{4,5},{5,4},{6,7},{7,6},{8,9},{9,8},{10,11... | collective-permute-start | bytes 393224 | tf_op jit(solution)/shard_map/ppermute | solution.py:368
  12.8 9.6 %collective-permute-start.8 = (bf16[144,256]{1,0:T(8,128)(2,1)S(1)}, bf16[144,256]{1,0:T(8,128)(2,1)S(1)}, u32[]{:S(2)}, u32[]{:S(2)}) collective-permute-start(bf16[144,256]{1,0:T(8,128)(2,1)S(1)} %get-tuple-element.38), channel_id=1, source_target_pairs={{4,0},{5,1},{6,2},{7,3},{8,4},{9,5},{10,6},{11,7},{12,8},{13,9},{1... | collective-permute-start | bytes 221192 | tf_op jit(solution)/shard_map/ppermute | solution.py:377
  17.1 12.5 %collective-permute-start.4 = (bf16[2,6,32,128]{3,2,1,0:T(8,128)(2,1)S(1)}, bf16[2,6,32,128]{3,2,1,0:T(8,128)(2,1)S(1)}, u32[]{:S(2)}, u32[]{:S(2)}) collective-permute-start(bf16[2,6,32,128]{3,2,1,0:T(8,128)(2,1)S(1)} %join.2.mine_ref), channel_id=1, source_target_pairs={{0,16},{4,20},{8,24},{12,28},{16,0},{20,4},{24,8},{28,12},{1,17},{... | collective-permute-start | bytes 294920 | tf_op jit(solution)/shard_map/ppermute | solution.py:410
  19.8 17.1 %collective-permute-start.6 = (bf16[928,256]{1,0:T(8,128)(2,1)S(1)}, bf16[928,256]{1,0:T(8,128)(2,1)S(1)}, u32[]{:S(2)}, u32[]{:S(2)}) collective-permute-start(bf16[928,256]{1,0:T(8,128)(2,1)S(1)} %get-tuple-element.36), channel_id=1, source_target_pairs={{0,4},{1,5},{2,6},{3,7},{4,8},{5,9},{6,10},{7,11},{8,12},{9,13},{1... | collective-permute-start | bytes 1425416 | tf_op jit(solution)/shard_map/ppermute | solution.py:377
  27.2 9.6 %collective-permute-start.9 = (bf16[128,256]{1,0:T(8,128)(2,1)S(1)}, bf16[128,256]{1,0:T(8,128)(2,1)S(1)}, u32[]{:S(2)}, u32[]{:S(2)}) collective-permute-start(bf16[128,256]{1,0:T(8,128)(2,1)S(1)} %get-tuple-element.40), channel_id=1, source_target_pairs={{0,4},{1,5},{2,6},{3,7},{4,8},{5,9},{6,10},{7,11},{8,12},{9,13},{1... | collective-permute-start | bytes 196616 | tf_op jit(solution)/shard_map/ppermute | solution.py:377
  29.7 10.1 %collective-permute-start.5 = (bf16[4,6,32,128]{3,2,1,0:T(8,128)(2,1)S(1)}, bf16[4,6,32,128]{3,2,1,0:T(8,128)(2,1)S(1)}, u32[]{:S(2)}, u32[]{:S(2)}) collective-permute-start(bf16[4,6,32,128]{3,2,1,0:T(8,128)(2,1)S(1)} %join.3.mine_ref), channel_id=1, source_target_pairs={{0,4},{4,0},{8,12},{12,8},{16,20},{20,16},{24,28},{28,24},{1,5},{5... | collective-permute-start | bytes 589832 | tf_op jit(solution)/shard_map/ppermute | solution.py:410
  38.0 1.8 %collective-permute-start.10 = (f32[64,768]{1,0:T(8,128)S(1)}, f32[64,768]{1,0:T(8,128)S(1)}, u32[]{:S(2)}, u32[]{:S(2)}) collective-permute-start(f32[64,768]{1,0:T(8,128)S(1)} %get-tuple-element.46), channel_id=1, source_target_pairs={{0,1},{1,0},{2,3},{3,2},{4,5},{5,4},{6,7},{7,6},{8,9},{9,8},{10,11... | collective-permute-start | bytes 589832 | tf_op jit(solution)/shard_map/ppermute | solution.py:368
  38.1 1.7 %collective-permute-start.11 = (f32[64,768]{1,0:T(8,128)S(1)}, f32[64,768]{1,0:T(8,128)S(1)}, u32[]{:S(2)}, u32[]{:S(2)}) collective-permute-start(f32[64,768]{1,0:T(8,128)S(1)} %get-tuple-element.47), channel_id=1, source_target_pairs={{0,1},{1,0},{2,3},{3,2},{4,5},{5,4},{6,7},{7,6},{8,9},{9,8},{10,11... | collective-permute-start | bytes 589832 | tf_op jit(solution)/shard_map/ppermute | solution.py:368
  38.6 1.5 %collective-permute-start.12 = (f32[64,768]{1,0:T(8,128)S(1)}, f32[64,768]{1,0:T(8,128)S(1)}, u32[]{:S(2)}, u32[]{:S(2)}) collective-permute-start(f32[64,768]{1,0:T(8,128)S(1)} %get-tuple-element.48), channel_id=1, source_target_pairs={{0,1},{1,0},{2,3},{3,2},{4,5},{5,4},{6,7},{7,6},{8,9},{9,8},{10,11... | collective-permute-start | bytes 589832 | tf_op jit(solution)/shard_map/ppermute | solution.py:368
  40.1 6.7 %copy-start.3 = (f32[4,8,64,64]{3,2,1,0:T(8,128)S(1)}, f32[4,8,64,64]{3,2,1,0:T(8,128)}, u32[]{:S(2)}) copy-start(f32[4,8,64,64]{3,2,1,0:T(8,128)} %up_ref.1) | copy-start | bytes 1572868
  40.1 6.7 %copy-start.4 = (f32[8,256,64]{1,2,0:T(8,128)S(1)}, f32[8,256,64]{1,2,0:T(8,128)}, u32[]{:S(2)}) copy-start(f32[8,256,64]{1,2,0:T(8,128)} %param.11) | copy-start | bytes 1572868
  40.1 6.7 %copy-start.5 = (f32[8,64,64]{2,1,0:T(8,128)S(1)}, f32[8,64,64]{2,1,0:T(8,128)}, u32[]{:S(2)}) copy-start(f32[8,64,64]{2,1,0:T(8,128)} %transfer_ref.1) | copy-start | bytes 393220
  40.1 6.7 %copy-start.6 = (bf16[2048,32]{0,1:T(8,128)(2,1)S(1)}, bf16[2048,32]{0,1:T(8,128)(2,1)}, u32[]{:S(2)}) copy-start(bf16[2048,32]{0,1:T(8,128)(2,1)} %param.10) | copy-start | bytes 393220
  40.1 6.7 %copy-start.7 = (s32[8,8]{1,0:T(8,128)S(1)}, s32[8,8]{1,0:T(8,128)}, u32[]{:S(2)}) copy-start(s32[8,8]{1,0:T(8,128)} %far_leaf_ref.1) | copy-start | bytes 772
  40.1 6.7 %copy-start.8 = (s32[4,8]{1,0:T(4,128)S(1)}, s32[4,8]{1,0:T(4,128)}, u32[]{:S(2)}) copy-start(s32[4,8]{1,0:T(4,128)} %far_up_ref.1) | copy-start | bytes 388
  40.2 11.5 %collective-permute-start.13 = (bf16[32,2048]{1,0:T(8,128)(2,1)S(1)}, bf16[32,2048]{1,0:T(8,128)(2,1)S(1)}, u32[]{:S(2)}, u32[]{:S(2)}) collective-permute-start(bf16[32,2048]{1,0:T(8,128)(2,1)S(1)} %get-tuple-element.50), channel_id=1, source_target_pairs={{0,2},{1,3},{2,0},{3,1},{4,6},{5,7},{6,4},{7,5},{8,10},{9,11},{10,... | collective-permute-start | bytes 393224 | tf_op jit(solution)/shard_map/ppermute | solution.py:368
  40.7 8.7 %collective-permute-start.14 = (bf16[32,512]{1,0:T(8,128)(2,1)S(1)}, bf16[32,512]{1,0:T(8,128)(2,1)S(1)}, u32[]{:S(2)}, u32[]{:S(2)}) collective-permute-start(bf16[32,512]{1,0:T(8,128)(2,1)S(1)} %get-tuple-element.51), channel_id=1, source_target_pairs={{4,0},{5,1},{6,2},{7,3},{8,4},{9,5},{10,6},{11,7},{12,8},{13,9},{1... | collective-permute-start | bytes 98312 | tf_op jit(solution)/shard_map/ppermute | solution.py:377
  44.0 7.6 %collective-permute-start.15 = (bf16[32,512]{1,0:T(8,128)(2,1)S(1)}, bf16[32,512]{1,0:T(8,128)(2,1)S(1)}, u32[]{:S(2)}, u32[]{:S(2)}) collective-permute-start(bf16[32,512]{1,0:T(8,128)(2,1)S(1)} %get-tuple-element.52), channel_id=1, source_target_pairs={{4,2},{5,3},{6,0},{7,1},{8,6},{9,7},{10,4},{11,5},{12,10},{13,11},... | collective-permute-start | bytes 98312 | tf_op jit(solution)/shard_map/ppermute | solution.py:377
  (3 other events, 13.8 us)
